TPU v7x, 32 devices: a whole 2x2x4 slice. The times are simulated.
32 devices in a mesh: rep: 8 (over y, x, core), tp: 4 (over z).
Axes of the slice: x: 2, y: 2, z: 4, core: 2. Of those that a mesh axis runs over, the one named last changes fastest.
Arguments:
- inputs: bfloat16 [4, 512, 5120], P(None, 'rep'), may hold values from -6 to 6
- qkv_weight: bfloat16 [2, 5120, 6144], P(None, ('rep', 'tp')), may hold values from -0.078125 to 0.078125
- out_weight: bfloat16 [2, 5120, 4096], P(None, ('rep', 'tp')), may hold values from -0.25 to 0.25
- norm_gain: float32 [2, 5120], replicated, may hold values from 0.1 to 1.9
- query_gain: float32 [2, 128], replicated, may hold values from 0.5 to 2
- key_gain: float32 [2, 128], replicated, may hold values from 0.5 to 2
- stored_rotated_keys: bfloat16 [2, 512, 8, 256, 128], P(None, 'rep', 'tp'), may hold values from -540 to 540
- stored_cache_values: bfloat16 [2, 512, 8, 256, 128], P(None, 'rep', 'tp'), may hold values from -6 to 6
- lengths: int32 [512], P('rep'), may hold values from 1 to 256, as said below
Outputs:
- final_hidden: bfloat16 [4, 512, 5120], P(None, 'rep')
Inputs may be any that keep to these rules, and one draw needn't show every extreme that they name: `lengths`: in every replica some row has exactly 256 cached positions.
All inputs are finite; a program needn't handle non-finite values.
Results may differ from a plain program's by a relative error of at most 0.039.
The roundings to bfloat16 on the way count: a program that leaves them out, or rounds other values in their place, can miss the bound.
Values may be sent and summed in bfloat16 or wider, within the bound.
No kernel may reach another device: no remote copies, remote signals or barrier semaphores. Data moves between devices by JAX's collectives and lax.ppermute only.
A program may use at most 192 MiB of HBM per device.

v0:
```python
import jax
import jax.numpy as jnp
from jax import lax
from jax.sharding import PartitionSpec as P

epsilon = 1e-06
rope_base = 1000000.0


def rms_scale(value_rows, gain):
    wide = value_rows.astype(jnp.float32)
    return wide * lax.rsqrt(jnp.mean(wide * wide, axis=-1, keepdims=True) + epsilon) * gain


def rotate(value_rows, positions):
    half_dim = value_rows.shape[-1] // 2
    frequency = rope_base ** (-jnp.arange(half_dim, dtype=jnp.float32) / half_dim)
    angles = positions.astype(jnp.float32)[..., None] * frequency
    cosine = jnp.cos(angles)
    sine = jnp.sin(angles)
    leading_shape = value_rows[..., :half_dim]
    trailing_shape = value_rows[..., half_dim:]
    return jnp.concatenate(
        [
            leading_shape * cosine - trailing_shape * sine,
            trailing_shape * cosine + leading_shape * sine,
        ],
        axis=-1,
    )


def attend(queries, new_keys, new_values, old_keys, old_values, lengths):
    step_count = queries.shape[0]
    head_dim = queries.shape[-1]
    slots = old_keys.shape[2]
    score_old = jnp.einsum(
        "srkgd,rkcd->srkgc", queries, old_keys, preferred_element_type=jnp.float32
    ) * head_dim ** (-0.5)
    score_new = jnp.einsum(
        "srkgd,trkd->srkgt", queries, new_keys, preferred_element_type=jnp.float32
    ) * head_dim ** (-0.5)
    live = jnp.arange(slots, dtype=jnp.int32)[None, :] < lengths[:, None]
    score_old = jnp.where(live[None, :, None, None, :], score_old, -jnp.inf)
    order = jnp.arange(step_count, dtype=jnp.int32)
    causal = order[None, :] <= order[:, None]
    score_new = jnp.where(causal[:, None, None, None, :], score_new, -jnp.inf)
    highest = jnp.maximum(jnp.max(score_old, axis=-1), jnp.max(score_new, axis=-1))[..., None]
    weight_old = jnp.exp(score_old - highest)
    weight_new = jnp.exp(score_new - highest)
    denominator = jnp.sum(weight_old, axis=-1, keepdims=True) + jnp.sum(
        weight_new, axis=-1, keepdims=True
    )
    share_old = (weight_old / denominator).astype(jnp.bfloat16)
    share_new = (weight_new / denominator).astype(jnp.bfloat16)
    mixed = jnp.einsum(
        "srkgc,rkcd->srkgd", share_old, old_values, preferred_element_type=jnp.float32
    )
    mixed = mixed + jnp.einsum(
        "srkgt,trkd->srkgd", share_new, new_values, preferred_element_type=jnp.float32
    )
    return mixed.astype(jnp.bfloat16)


def on_device(
    inputs,
    qkv_weight,
    out_weight,
    norm_gain,
    query_gain,
    key_gain,
    stored_rotated_keys,
    stored_cache_values,
    lengths,
):
    step_count = inputs.shape[0]
    row_count = inputs.shape[1]
    model_width = inputs.shape[2]
    flat_rows = step_count * row_count
    groups_here = stored_rotated_keys.shape[2]
    head_dim = stored_rotated_keys.shape[4]
    per_group = qkv_weight.shape[2] // (lax.axis_size("tp") * groups_here * head_dim)
    block_qkv, block_out = (
        lax.all_to_all(qkv_weight, "tp", split_axis=2, concat_axis=1, tiled=True),
        lax.all_to_all(out_weight, "tp", split_axis=2, concat_axis=1, tiled=True),
    )
    rows_qkv, rows_out = (
        lax.all_gather(block_qkv, "rep", axis=1, tiled=True),
        lax.all_gather(block_out, "rep", axis=1, tiled=True),
    )
    positions = lengths[None, :] + jnp.arange(step_count, dtype=jnp.int32)[:, None]
    hidden = inputs
    for layer_index in range(qkv_weight.shape[0]):
        normed = (
            rms_scale(hidden, norm_gain[layer_index])
            .astype(jnp.bfloat16)
            .reshape(flat_rows, model_width)
        )
        mixed = jnp.dot(normed, rows_qkv[layer_index], preferred_element_type=jnp.float32)
        mixed = mixed.reshape(step_count, row_count, groups_here, per_group, head_dim)
        queries = rotate(
            rms_scale(mixed[:, :, :, : per_group - 2], query_gain[layer_index]),
            positions[:, :, None, None],
        ).astype(jnp.bfloat16)
        new_keys = rotate(
            rms_scale(mixed[:, :, :, per_group - 2], key_gain[layer_index]), positions[:, :, None]
        ).astype(jnp.bfloat16)
        new_values = mixed[:, :, :, per_group - 1].astype(jnp.bfloat16)
        attended = attend(
            queries,
            new_keys,
            new_values,
            stored_rotated_keys[layer_index],
            stored_cache_values[layer_index],
            lengths,
        )
        attended = attended.reshape(flat_rows, -1)
        projected = lax.dot_general(
            attended,
            rows_out[layer_index],
            (((1,), (1,)), ((), ())),
            preferred_element_type=jnp.float32,
        )
        summed = lax.psum(projected, "tp")
        hidden = (
            hidden.astype(jnp.float32) + summed.reshape(step_count, row_count, model_width)
        ).astype(jnp.bfloat16)
    return hidden


def solution(mesh):
    return jax.shard_map(
        on_device,
        mesh=mesh,
        in_specs=(
            P(None, "rep", None),
            P(None, ("rep", "tp"), None),
            P(None, ("rep", "tp"), None),
            P(),
            P(),
            P(),
            P(None, "rep", "tp", None, None),
            P(None, "rep", "tp", None, None),
            P("rep"),
        ),
        out_specs=P(None, "rep", None),
        check_vma=False,
    )
```

profile of v0, /device:TPU:0, one launch (start us, length us, event | category | flops | bytes accessed | tf_op | source)
XLA Modules:
  0.0 903.1 jit_solution(1629452170836878275)
XLA Ops:
  6.5 15.7 %copy.129 = bf16[2,160,6144]{1,0,2:T(2,128)(2,1)} copy(bf16[2,160,6144]{2,1,0:T(8,128)(2,1)} %param.10) | data formatting | bytes 7864320 | tf_op args[1]
  22.2 146.5 %all_to_all.36 = bf16[2,160,6144]{1,0,2:T(2,128)(2,1)} all-to-all(bf16[2,160,6144]{1,0,2:T(2,128)(2,1)} %copy.129), channel_id=1, replica_groups=mesh['rep'=8,'tp'=4] {'tp'}, dimensions={2} | all-to-all | bytes 7864320 | tf_op jit(solution)/shard_map/all_to_all | solution.py:83
  168.7 16.8 %copy.170 = bf16[2,160,4,1536]{3,2,1,0:T(4,128)(2,1)} copy(bf16[2,160,4,1536]{1,0,3,2:T(2,128)(2,1)} %bitcast.164) | data formatting | bytes 7864320 | tf_op jit(solution)/shard_map/all_to_all | solution.py:83
  185.5 4.7 copy.131
  192.0 7.4 copy.144
  199.3 98.6 %all_to_all.37 = bf16[2,160,4096]{1,0,2:T(2,128)(2,1)} all-to-all(bf16[2,160,4096]{1,0,2:T(2,128)(2,1)} %copy.144), channel_id=1, replica_groups=mesh['rep'=8,'tp'=4] {'tp'}, dimensions={2} | all-to-all | bytes 5242880 | tf_op jit(solution)/shard_map/all_to_all | solution.py:84
  298.0 10.9 %copy.175 = bf16[2,160,4,1024]{3,2,1,0:T(4,128)(2,1)S(1)} copy(bf16[2,160,4,1024]{1,0,3,2:T(2,128)(2,1)} %bitcast.165) | data formatting | bytes 5242880 | tf_op jit(solution)/shard_map/all_to_all | solution.py:84
  308.8 2.3 copy.146
  314.2 27.3 %all-gather.3.cloned.1.call-done = bf16[2,5120,1536]{2,1,0:T(8,128)(2,1)} async-done(((bf16[2,640,1536]{2,1,0:T(8,128)(2,1)}), bf16[2,5120,1536]{2,1,0:T(8,128)(2,1)}) %all-gather.3.cloned.1.call-update) | async-done | bytes 31457296 | tf_op jit(solution)/shard_map/all_gather | solution.py:87
  341.5 22.3 %slice_bitcast_fusion.1 = (bf16[1536,5120]{0,1:T(8,128)(2,1)}, bf16[1536,5120]{0,1:T(8,128)(2,1)}) fusion(bf16[2,5120,1536]{2,1,0:T(8,128)(2,1)} %all-gather.3.cloned.1.call-done), kind=kLoop, calls=%fused_computation.1 | loop fusion | bytes 62914560 | tf_op jit(solution)/shard_map/dot_general | solution.py:98
  363.8 20.7 %copy.132 = bf16[1536,5120]{1,0:T(8,128)(2,1)} copy(bf16[1536,5120]{0,1:T(8,128)(2,1)} %get-tuple-element.7) | data formatting | bytes 31457280 | tf_op jit(solution)/shard_map/dot_general | solution.py:98
  384.5 9.2 %fusion.26 = f32[4,64,2,6,128]{4,1,3,2,0:T(8,128)S(1)} fusion(bf16[2,6,128,5120,1]{3,2,1,0,4:T(8,128)(2,1)} %bitcast.167, bf16[4,64,5120]{2,1,0:T(8,128)(2,1)S(1)} %copy-done, f32[5120]{0:T(1024)S(1)} %bitcast.175, f32[4,64]{1,0:T(4,128)S(1)} %add_rsqrt_fusion.5), kind=kOutput, calls=%fused_computation.35 | convolution fusion | flops 4031774720 | bytes 19944448 | tf_op jit(solution)/shard_map/dot_general | solution.py:98
  395.8 4.7 fusion.59
  401.7 5.8 bitcast_reduce_fusion.1
  408.1 1.9 fusion.44
  410.4 1.7 copy.142
  413.1 4.6 fusion.34
  418.8 32.2 %all-gather.5.cloned.1.call-done = bf16[2,5120,1024]{2,1,0:T(8,128)(2,1)} async-done(((bf16[2,640,1024]{2,1,0:T(8,128)(2,1)}), bf16[2,5120,1024]{2,1,0:T(8,128)(2,1)}) %all-gather.5.cloned.1.call-update) | async-done | bytes 20971536 | tf_op jit(solution)/shard_map/all_gather | solution.py:88
  451.0 9.2 %fusion.1 = f32[256,5120]{1,0:T(8,128)} fusion(bf16[256,1024]{1,0:T(8,128)(2,1)S(1)} %reshape.207, bf16[2,5120,1024]{2,1,0:T(8,128)(2,1)} %all-gather.5.cloned.1.call-done), kind=kOutput, calls=%fused_computation.5 | convolution fusion | flops 2684354560 | bytes 16252928 | tf_op jit(solution)/shard_map/dot_general | solution.py:117
  460.3 20.6 %copy.147 = bf16[1536,5120]{1,0:T(8,128)(2,1)} copy(bf16[1536,5120]{0,1:T(8,128)(2,1)} %get-tuple-element.8) | data formatting | bytes 31457280 | tf_op jit(solution)/shard_map/dot_general | solution.py:98
  480.9 168.5 %all-reduce.3.cloned.1.call-done = f32[4,64,5120]{2,1,0:T(8,128)} async-done(((f32[4,64,5120]{2,1,0:T(8,128)}), f32[4,64,5120]{2,1,0:T(8,128)}) %all-reduce.3.cloned.1.call-update) | async-done | bytes 5242896 | tf_op jit(solution)/shard_map/psum | solution.py:123
  649.3 4.4 fusion.18
  653.7 8.2 fusion.23
  663.9 7.2 bitcast_reduce_fusion
  671.2 5.7 fusion.56
  676.9 1.8 copy.152
  679.6 3.2 fusion.45
  683.0 5.9 fusion.37
  690.9 1.7 fusion.43
  694.0 9.4 %fusion = f32[256,5120]{1,0:T(8,128)} fusion(bf16[256,1024]{1,0:T(8,128)(2,1)} %reshape.209, bf16[2,5120,1024]{2,1,0:T(8,128)(2,1)} %all-gather.5.cloned.1.call-done), kind=kOutput, calls=%fused_computation.3 | convolution fusion | flops 2684354560 | bytes 16252928 | tf_op jit(solution)/shard_map/dot_general | solution.py:117
  703.4 188.0 %all-reduce.5.cloned.1.call-done = f32[4,64,5120]{2,1,0:T(8,128)} async-done(((f32[4,64,5120]{2,1,0:T(8,128)}), f32[4,64,5120]{2,1,0:T(8,128)}) %all-reduce.5.cloned.1.call-update) | async-done | bytes 5242896 | tf_op jit(solution)/shard_map/psum | solution.py:123
  891.4 4.7 fusion.21
  (84 shorter events, 17.5 us)
Async XLA Ops:
  6.5 335.0 %all-gather.3.cloned.1.call-start = ((), (), s32[]{:S(2)}) async-start(), calls=%async_computation.2 | async-start | bytes 35389440 | tf_op jit(solution)/shard_map/all_gather | solution.py:87
  190.2 1.7 copy-start.3
  190.3 260.8 %all-gather.5.cloned.1.call-start = ((), (), s32[]{:S(2)}) async-start(), calls=%async_computation.3 | async-start | bytes 23592960 | tf_op jit(solution)/shard_map/all_gather | solution.py:88
  311.1 0.7 copy-start.7
  311.1 0.7 copy-start.8
  311.1 0.7 copy-start.6
  311.1 1.8 copy-start
  311.2 3.0 copy-start.5
  311.2 338.2 %all-reduce.3.cloned.1.call-start = ((), (), s32[]{:S(2)}) async-start(), calls=%async_computation.4 | async-start | bytes 10485760 | tf_op jit(solution)/shard_map/psum | solution.py:123
  393.7 1.3 copy-start.2
  413.1 4.6 copy-start.4
  460.3 431.2 %all-reduce.5.cloned.1.call-start = ((), (), s32[]{:S(2)}) async-start(), calls=%async_computation.5 | async-start | bytes 10485760 | tf_op jit(solution)/shard_map/psum | solution.py:123
  661.9 1.7 copy-start.1
Sparse Core Ops, SparseCore 0:
  190.4 151.0 all-gather.2
  343.4 107.5 all-gather.4
  460.4 188.9 all-reduce.2
  703.5 187.8 all-reduce.4
where the time goes:
time: 909 us; the launch traced here: 903 us
  waiting for transfers between devices  416 us (46%)
  blocking collectives  245 us (27%)
  local copies, waits for them, and re-layouts  135 us (15%)
  matrix products  72 us (8%)
  other arithmetic  20.6 us (2%)
  between operations  14 us (2%)
    psum x2, waiting for transfers between devices, on_device(): summed = lax.psum(projected, 'tp')  357 us
    all_to_all x1, blocking collectives, on_device(): lax.all_to_all(qkv_weight, 'tp', split_axis=2, concat_axis=1, tiled=True)  146 us
    all_to_all x1, blocking collectives, on_device(): lax.all_to_all(out_weight, 'tp', split_axis=2, concat_axis=1, tiled=True)  98.6 us
    dot_general x3, local copies, waits for them, and re-layouts, on_device(): jnp.dot(normed, rows_qkv[layer_index], preferred_element_type=jnp.float32)  63.6 us
    all_gather x1, waiting for transfers between devices, on_device(): lax.all_gather(block_out, 'rep', axis=1, tiled=True)  32.2 us
    all_gather x1, waiting for transfers between devices, on_device(): lax.all_gather(block_qkv, 'rep', axis=1, tiled=True)  27.3 us
    unnamed x20, local copies, waits for them, and re-layouts  26.4 us
    all_to_all x2, local copies, waits for them, and re-layouts, on_device(): lax.all_to_all(qkv_weight, 'tp', split_axis=2, concat_axis=1, tiled=True)  21.5 us
  transfers between devices with their start and end apart: 4, of which 4 were waited for; matrix products, arithmetic and copies ran while one was open for 13% of the time, Pallas kernels for 0%

commit v1 on v0

v1 whole, which is shorter than its diff:
```python
import functools

import jax
import jax.numpy as jnp
from jax import lax
from jax.experimental import pallas as pl
from jax.experimental.pallas import tpu as pltpu
from jax.sharding import PartitionSpec as P

epsilon = 1e-06
rope_base = 1000000.0
MIB = 1024 * 1024
VMEM = pltpu.VMEM
SMEM = pltpu.SMEM


def vmem_spec():
    return pl.BlockSpec(memory_space=VMEM)


def smem_spec():
    return pl.BlockSpec(memory_space=SMEM)


def any_spec():
    return pl.BlockSpec(memory_space=pl.ANY)


def tiles(width, size=256):
    return [(start, min(size, width - start)) for start in range(0, width, size)]


def split_kernel(parts, replicas, piece, place_ref, whole_ref, blocks_ref):
    for part in range(parts):
        columns = [
            whole_ref[:, (r * parts + part) * piece : (r * parts + part + 1) * piece]
            for r in range(replicas)
        ]
        blocks_ref[place_ref[part]] = jnp.concatenate(columns, axis=1)


def split_parts(whole, place, parts, replicas, piece):
    rows = whole.shape[0]
    return pl.pallas_call(
        functools.partial(split_kernel, parts, replicas, piece),
        out_shape=jax.ShapeDtypeStruct((parts, rows, replicas * piece), whole.dtype),
        in_specs=[smem_spec(), vmem_spec()],
        out_specs=vmem_spec(),
        compiler_params=pltpu.CompilerParams(vmem_limit_bytes=24 * MIB),
    )(place, whole)


def share_kernel(shares, core_ref, whole_ref, mine_ref, theirs_ref, squares_ref):
    width = mine_ref.shape[1] // shares
    core = core_ref[0]
    squares = None
    for share in range(shares):
        columns = slice(share * width, (share + 1) * width)
        for whose, to_ref in ((core, mine_ref), (1 - core, theirs_ref)):
            start = pl.multiple_of((2 * share + whose) * width, 128)
            some = whole_ref[:, pl.ds(start, width)]
            to_ref[:, columns] = some
            wide = some.astype(jnp.float32)
            term = jnp.sum(wide * wide, axis=1, keepdims=True)
            squares = term if squares is None else squares + term
    squares_ref[...] = squares


def share_features(whole, core, shares):
    rows, width = whole.shape
    part = jax.ShapeDtypeStruct((rows, width // 2), whole.dtype)
    return pl.pallas_call(
        functools.partial(share_kernel, shares),
        out_shape=(part, part, jax.ShapeDtypeStruct((rows, 1), jnp.float32)),
        in_specs=[smem_spec(), vmem_spec()],
        out_specs=(vmem_spec(), vmem_spec(), vmem_spec()),
        compiler_params=pltpu.CompilerParams(vmem_limit_bytes=24 * MIB),
    )(core, whole)


def join_kernel(parts, replicas, piece, place_ref, *refs):
    block_refs, whole_ref, held, sems = refs[:parts], refs[parts], refs[parts + 1], refs[parts + 2]
    copies = [
        pltpu.make_async_copy(block_refs[shift], held.at[place_ref[shift]], sems.at[shift])
        for shift in range(parts)
    ]
    for copy in copies:
        copy.start()
    for copy in copies:
        copy.wait()
    for r in range(replicas):
        columns = [held[part, :, r * piece : (r + 1) * piece] for part in range(parts)]
        whole_ref[:, r * parts * piece : (r + 1) * parts * piece] = jnp.concatenate(columns, axis=1)


def join_parts(blocks, place, replicas, piece):
    parts = len(blocks)
    rows = blocks[0].shape[0]
    return pl.pallas_call(
        functools.partial(join_kernel, parts, replicas, piece),
        out_shape=jax.ShapeDtypeStruct((rows, parts * replicas * piece), blocks[0].dtype),
        in_specs=[smem_spec()] + [any_spec()] * parts,
        out_specs=vmem_spec(),
        scratch_shapes=[
            VMEM((parts, rows, replicas * piece), blocks[0].dtype),
            pltpu.SemaphoreType.DMA((parts,)),
        ],
        compiler_params=pltpu.CompilerParams(vmem_limit_bytes=24 * MIB),
    )(place, *blocks)


def qkv_kernel(count, shifts, pieces, arrays, continued, rows_ref, *refs):
    block_refs, refs = refs[:count], refs[count:]
    gain_ref, scale_ref, refs = refs[0], refs[1], refs[2:]
    weight_refs, refs = refs[:arrays], refs[arrays:]
    outputs = (len(refs) - 3) // (2 if continued else 1)
    if continued:
        before_refs, refs = refs[:outputs], refs[outputs:]
    mixed_refs, refs = refs[:outputs], refs[outputs:]
    held, normed, sems = refs
    each = mixed_refs[0].shape[0]
    copies = []
    for index, (array, first, size, place) in enumerate(pieces):
        to = pl.multiple_of(rows_ref[index], 16)
        copies.append(
            pltpu.make_async_copy(
                weight_refs[array].at[pl.ds(first, size)],
                held.at[place, pl.ds(to, size)],
                sems.at[index],
            )
        )
        copies[-1].start()
    step = 32

    @pl.loop(0, normed.shape[1] // step)
    def _(tile):
        rows = pl.ds(pl.multiple_of(tile * step, step), step)
        scale = scale_ref[rows, :]
        for place, shift in enumerate(shifts):
            wide = block_refs[place][rows, :].astype(jnp.float32)
            normed[place, rows, :] = (wide * scale * gain_ref[shift]).astype(jnp.bfloat16)

    for place in range(count):
        for index in range(len(pieces)):
            if pieces[index][3] == place:
                copies[index].wait()
        for start, size in tiles(mixed_refs[0].shape[1]):
            columns = slice(start, start + size)
            terms = jnp.dot(
                normed[place], held[place, :, columns], preferred_element_type=jnp.float32
            )
            for index in range(outputs):
                term = terms[index * each : (index + 1) * each]
                if place > 0:
                    mixed_refs[index][:, columns] += term
                elif continued:
                    mixed_refs[index][:, columns] = before_refs[index][:, columns] + term
                else:
                    mixed_refs[index][:, columns] = term


def project_qkv(
    blocks, shifts, gains, scale, weights, pieces, rows, before=None, outputs=1
):
    count = len(shifts)
    row_total, width = blocks[0].shape
    columns = weights[0].shape[1]
    continued = before is not None
    operands = [rows] + [blocks[shift] for shift in shifts] + [gains, scale] + list(weights)
    in_specs = [smem_spec()] + [vmem_spec()] * (count + 2) + [any_spec()] * len(weights)
    if continued:
        operands += list(before)
        in_specs += [vmem_spec()] * outputs
    mixed = jax.ShapeDtypeStruct((row_total // outputs, columns), jnp.float32)
    return pl.pallas_call(
        functools.partial(qkv_kernel, count, shifts, pieces, len(weights), continued),
        out_shape=[mixed] * outputs,
        in_specs=in_specs,
        out_specs=[vmem_spec()] * outputs,
        scratch_shapes=[
            VMEM((count, width, columns), jnp.bfloat16),
            VMEM((count, row_total, width), jnp.bfloat16),
            pltpu.SemaphoreType.DMA((len(pieces),)),
        ],
        compiler_params=pltpu.CompilerParams(vmem_limit_bytes=52 * MIB),
        cost_estimate=pl.CostEstimate(
            flops=2 * row_total * count * width * columns,
            bytes_accessed=2 * count * width * columns,
            transcendentals=0,
        ),
    )(*operands)


def whole_out_kernel(count, column_ref, *refs):
    attended_refs, refs = refs[:count], refs[count:]
    weight_ref, residual_ref, hidden_ref, held, total, sems = refs
    width = attended_refs[0].shape[1]
    copies = []
    for shift in range(count):
        start = pl.multiple_of(column_ref[shift], 128)
        copies.append(
            pltpu.make_async_copy(
                weight_ref.at[:, pl.ds(start, width)], held.at[shift], sems.at[shift]
            )
        )
        copies[-1].start()
    for shift in range(count):
        copies[shift].wait()
        for start, size in tiles(hidden_ref.shape[1]):
            features = slice(start, start + size)
            term = lax.dot_general(
                attended_refs[shift][...],
                held[shift, features, :],
                (((1,), (1,)), ((), ())),
                preferred_element_type=jnp.float32,
            )
            if shift > 0:
                term = total[:, features] + term
            if shift < count - 1:
                total[:, features] = term
            else:
                hidden_ref[:, features] = (
                    residual_ref[:, features].astype(jnp.float32) + term
                ).astype(hidden_ref.dtype)


def project_out_whole(attended, weight, columns, residual):
    count = len(attended)
    row_total, width = attended[0].shape
    features = weight.shape[0]
    return pl.pallas_call(
        functools.partial(whole_out_kernel, count),
        out_shape=jax.ShapeDtypeStruct((row_total, features), residual.dtype),
        in_specs=[smem_spec()] + [vmem_spec()] * count + [any_spec(), vmem_spec()],
        out_specs=vmem_spec(),
        scratch_shapes=[
            VMEM((count, features, width), jnp.bfloat16),
            VMEM((row_total, features), jnp.float32),
            pltpu.SemaphoreType.DMA((count,)),
        ],
        compiler_params=pltpu.CompilerParams(vmem_limit_bytes=50 * MIB),
        cost_estimate=pl.CostEstimate(
            flops=2 * row_total * count * width * features,
            bytes_accessed=2 * count * width * features,
            transcendentals=0,
        ),
    )(columns, *attended, weight, residual)


def out_kernel(count, shifts, column_ref, *refs):
    attended_refs, refs = refs[:count], refs[count:]
    weight_ref, refs = refs[0], refs[1:]
    last = len(refs) > 3
    if last:
        before_ref, residual_ref, refs = refs[0], refs[1], refs[2:]
    sum_ref, held, sems = refs[0], refs[-2], refs[-1]
    width = attended_refs[0].shape[1]
    copies = []
    for place, shift in enumerate(shifts):
        start = pl.multiple_of(column_ref[shift], 128)
        copies.append(
            pltpu.make_async_copy(
                weight_ref.at[:, pl.ds(start, width)], held.at[place], sems.at[place]
            )
        )
        copies[-1].start()
    for place in range(count):
        copies[place].wait()
        for start, size in tiles(sum_ref.shape[1]):
            features = slice(start, start + size)
            term = lax.dot_general(
                attended_refs[place][...],
                held[place, features, :],
                (((1,), (1,)), ((), ())),
                preferred_element_type=jnp.float32,
            )
            if last:
                total = before_ref[:, features] + term
                total = residual_ref[:, features].astype(jnp.float32) + total
                sum_ref[:, features] = total.astype(sum_ref.dtype)
            elif place > 0:
                sum_ref[:, features] += term
            else:
                sum_ref[:, features] = term


def project_out(attended, shifts, weight, columns, before=None, residual=None):
    count = len(shifts)
    row_total, width = attended[0].shape
    features = weight.shape[0]
    last = residual is not None
    operands = [columns] + [attended[shift] for shift in shifts] + [weight]
    in_specs = [smem_spec()] + [vmem_spec()] * count + [any_spec()]
    if last:
        operands += [before, residual]
        in_specs += [vmem_spec()] * 2
    return pl.pallas_call(
        functools.partial(out_kernel, count, shifts),
        out_shape=jax.ShapeDtypeStruct(
            (row_total, features), residual.dtype if last else jnp.float32
        ),
        in_specs=in_specs,
        out_specs=vmem_spec(),
        scratch_shapes=[
            VMEM((count, features, width), jnp.bfloat16),
            pltpu.SemaphoreType.DMA((count,)),
        ],
        compiler_params=pltpu.CompilerParams(vmem_limit_bytes=50 * MIB),
        cost_estimate=pl.CostEstimate(
            flops=2 * row_total * count * width * features,
            bytes_accessed=2 * count * width * features,
            transcendentals=0,
        ),
    )(*operands)


def attention_kernel(heads, lengths_ref, *refs):
    mixed_refs, refs = refs[:-9], refs[-9:]
    cosine_ref, sine_ref, query_gain_ref, key_gain_ref, keys_ref, values_ref = refs[:6]
    attended_ref, query_rows, result_rows = refs[6:]
    steps, rows, _ = mixed_refs[0].shape
    slots, size = keys_ref.shape[-2:]
    step_rows = steps * rows
    per_row = heads * steps
    first_row = pl.program_id(0) * rows
    scale = size ** (-0.5)
    cosine = cosine_ref[...]
    sine = sine_ref[...]

    def projected(vector):
        columns = slice(vector * size, (vector + 1) * size)
        return sum(ref[:, :, columns] for ref in mixed_refs)

    def turned(vectors, gain):
        mean = jnp.mean(vectors * vectors, axis=-1, keepdims=True)
        normal = vectors * lax.rsqrt(mean + epsilon) * gain
        swapped = jnp.concatenate([normal[..., size // 2 :], normal[..., : size // 2]], axis=-1)
        return normal * cosine + swapped * sine

    for head in range(heads):
        vectors = projected(head)
        query = turned(vectors, query_gain_ref[...])
        query_rows[head * step_rows : (head + 1) * step_rows, :] = query.reshape(step_rows, size)
    new_key = turned(projected(heads), key_gain_ref[...])
    new_key = new_key.reshape(step_rows, size).astype(jnp.bfloat16)
    new_value = projected(heads + 1)
    new_value = new_value.reshape(step_rows, size).astype(jnp.bfloat16)

    queries = [
        query_rows[pl.ds(r, per_row, stride=rows), :].astype(jnp.bfloat16) for r in range(rows)
    ]
    nt = (((1,), (1,)), ((), ()))
    column = lax.broadcasted_iota(jnp.int32, (per_row, slots), 1)
    old = []
    for r in range(rows):
        score = lax.dot_general(
            queries[r], keys_ref[r], nt, preferred_element_type=jnp.float32
        )
        old.append(jnp.where(column < lengths_ref[first_row + r], score * scale, -jnp.inf))
    old = jnp.concatenate(old, axis=0)
    new = lax.dot_general(
        jnp.concatenate(queries, axis=0), new_key, nt, preferred_element_type=jnp.float32
    )
    at = lax.broadcasted_iota(jnp.int32, (rows * per_row, step_rows), 0)
    to = lax.broadcasted_iota(jnp.int32, (rows * per_row, step_rows), 1)
    seen = (at // per_row == to % rows) & (to // rows <= at % steps)
    new = jnp.where(seen, new * scale, -jnp.inf)
    highest = jnp.maximum(
        jnp.max(old, axis=-1, keepdims=True), jnp.max(new, axis=-1, keepdims=True)
    )
    old = jnp.exp(old - highest)
    new = jnp.exp(new - highest)
    total = jnp.sum(old, axis=-1, keepdims=True) + jnp.sum(new, axis=-1, keepdims=True)
    old = (old / total).astype(jnp.bfloat16)
    new = (new / total).astype(jnp.bfloat16)
    from_new = jnp.dot(new, new_value, preferred_element_type=jnp.float32)
    for r in range(rows):
        part = slice(r * per_row, (r + 1) * per_row)
        result = jnp.dot(old[part], values_ref[r], preferred_element_type=jnp.float32)
        result_rows[pl.ds(r, per_row, stride=rows), :] = result + from_new[part]
    for head in range(heads):
        result = result_rows[head * step_rows : (head + 1) * step_rows, :]
        attended_ref[:, :, head * size : (head + 1) * size] = result.reshape(
            steps, rows, size
        ).astype(jnp.bfloat16)


def attend(mixed, cosine, sine, query_gain, key_gain, keys, values, lengths, layer):
    steps, row_total, columns = mixed[0].shape
    groups, slots, size = keys.shape[2:]
    per_group = columns // (groups * size)
    heads = per_group - 2
    rows = 16
    cache_spec = pl.BlockSpec(
        (None, rows, None, slots, size), lambda i, g, _: (layer, i, g, 0, 0)
    )
    turn_spec = pl.BlockSpec((steps, rows, size), lambda i, g, _: (0, i, 0))
    gain_spec = pl.BlockSpec((1, size), lambda i, g, _: (0, 0))
    return pl.pallas_call(
        functools.partial(attention_kernel, heads),
        out_shape=jax.ShapeDtypeStruct((steps, row_total, groups * heads * size), jnp.bfloat16),
        grid_spec=pltpu.PrefetchScalarGridSpec(
            num_scalar_prefetch=1,
            grid=(row_total // rows, groups),
            in_specs=[pl.BlockSpec((steps, rows, per_group * size), lambda i, g, _: (0, i, g))]
            * len(mixed)
            + [
                turn_spec,
                turn_spec,
                gain_spec,
                gain_spec,
                cache_spec,
                cache_spec,
            ],
            out_specs=pl.BlockSpec((steps, rows, heads * size), lambda i, g, _: (0, i, g)),
            scratch_shapes=[
                VMEM((heads * steps * rows, size), jnp.float32),
                VMEM((heads * steps * rows, size), jnp.float32),
            ],
        ),
        compiler_params=pltpu.CompilerParams(vmem_limit_bytes=49 * MIB),
        cost_estimate=pl.CostEstimate(
            flops=4 * row_total * groups * heads * steps * slots * size,
            bytes_accessed=4 * row_total * groups * slots * size,
            transcendentals=row_total * groups * heads * steps * slots,
        ),
    )(lengths, *mixed, cosine, sine, query_gain, key_gain, keys, values)


def on_device(
    inputs,
    qkv_weight,
    out_weight,
    norm_gain,
    query_gain,
    key_gain,
    stored_rotated_keys,
    stored_cache_values,
    lengths,
):
    step_count, row_count, model_width = inputs.shape
    flat_rows = step_count * row_count
    layers = qkv_weight.shape[0]
    head_dim = stored_rotated_keys.shape[4]
    parts = lax.axis_size("tp")
    replicas = lax.axis_size("rep")
    me = lax.axis_index("tp")
    piece = qkv_weight.shape[1]
    slice_width = replicas * piece
    block_width = qkv_weight.shape[2] // parts
    head_width = out_weight.shape[2] // parts
    merge = piece % 16 == 0

    def shifted(block, shift):
        if shift == 0:
            return block
        return lax.ppermute(block, "tp", [(i, (i + shift) % parts) for i in range(parts)])

    def all_parts(block, *earlier):
        if parts != 4:
            return [shifted(block, shift) for shift in range(parts)]
        one, three = shifted(block, 1), shifted(block, 3)
        from_left, from_right = one, three
        if earlier:
            from_left, from_right = lax.optimization_barrier((one, three) + earlier)[:2]
        rightwards = lax.ppermute(from_left, "tp", [(1, 2), (2, 3)])
        leftwards = lax.ppermute(from_right, "tp", [(1, 0), (2, 1)])
        return [block, one, jnp.where(me >= 2, rightwards, leftwards), three]

    def outgoing(layer, shift):
        target = lax.rem(me + shift, parts)
        return lax.dynamic_slice(
            qkv_weight, (layer, 0, target * block_width), (1, piece, block_width)
        )[0]

    source = lax.rem(me - jnp.arange(parts, dtype=jnp.int32) + parts, parts)
    seat = lax.axis_index("rep")
    by_links = merge and replicas == 8 and parts == 4 and layers == 2

    def after(array, *earlier):
        return lax.optimization_barrier((array,) + earlier)[0]

    def swapped(block, mask):
        return lax.ppermute(block, "rep", [(i, i ^ mask) for i in range(replicas)])

    def spread_first(block, *earlier):
        block = after(block, *earlier) if earlier else block
        return [(0, 0, block), (2, 0, swapped(block, 2)), (4, 0, swapped(block, 4))]

    def spread_second(spread):
        by_x, by_y = spread[1][2], spread[2][2]
        half = by_x.shape[0] // 2
        return spread + [(6, 0, swapped(by_x[:half], 4)), (6, half, swapped(by_y[half:], 2))]

    def listed(spreads, shifts):
        arrays, pieces, rows = [], [], []
        for spread, its_shifts in zip(spreads, shifts):
            for mask, first, array in spread:
                at = 0
                while at < array.shape[0]:
                    place, offset = divmod(first + at, piece)
                    count = min(piece - offset, array.shape[0] - at)
                    pieces.append((len(arrays), at, count, its_shifts[place]))
                    rows.append(((seat ^ mask) // 2) * piece + offset)
                    at += count
                arrays.append(array)
        return arrays, pieces, jnp.stack(rows).astype(jnp.int32)

    positions = lengths[None, :] + jnp.arange(step_count, dtype=jnp.int32)[:, None]
    half = head_dim // 2
    frequency = rope_base ** (-jnp.arange(half, dtype=jnp.float32) / half)
    angles = positions.astype(jnp.float32)[..., None] * frequency
    cosine, sine = jnp.cos(angles), jnp.sin(angles)
    cosine = jnp.concatenate([cosine, cosine], axis=-1)
    sine = jnp.concatenate([-sine, sine], axis=-1)

    gains = jnp.take(norm_gain.reshape(layers, replicas, parts, piece), source, axis=2)
    gains = jnp.moveaxis(gains, 2, 1).reshape(layers, parts, 1, slice_width)

    flat = inputs.reshape(flat_rows, model_width)
    blocks = split_parts(flat, source, parts, replicas, piece)
    hidden = [blocks[shift] for shift in range(parts)]

    def from_calls(layer):
        arrays = [
            lax.all_gather(shifted(outgoing(layer, shift), shift), "rep", axis=0, tiled=True)
            for shift in range(parts)
        ]
        pieces = [(shift, 0, slice_width, shift) for shift in range(parts)]
        return arrays, pieces, jnp.zeros((parts,), jnp.int32)

    def from_call(came):
        array = lax.all_gather(came, "rep", axis=0, tiled=True)
        pieces = [
            (0, (r * parts + shift) * piece, piece, shift)
            for r in range(replicas)
            for shift in range(parts)
        ]
        rows = jnp.array([r * piece for r in range(replicas) for _ in range(parts)], jnp.int32)
        return [array], pieces, rows

    stages = [[0, 1, 3], [2]]

    def row_scale(squares):
        return lax.rsqrt(squares / model_width + epsilon)

    if by_links:
        core = lax.rem(seat, 2)
        mine, theirs, squares = share_features(
            flat, jnp.full((1,), core, jnp.int32), replicas // 2
        )
        both = jnp.concatenate([mine, swapped(theirs, 1)], axis=0)
        both = split_parts(both, source, parts, replicas // 2, piece)
        both = [both[shift] for shift in range(parts)]
        other = swapped(squares.reshape(-1, 128), 1).reshape(flat_rows, 1)
        scale = row_scale(jnp.concatenate([squares, other], axis=0))
        core_gains = lax.dynamic_index_in_dim(
            gains[0].reshape(parts, replicas // 2, 2, piece), core, 2, keepdims=False
        ).reshape(parts, 1, slice_width // 2)
        one, three = shifted(outgoing(0, 1), 1), shifted(outgoing(0, 3), 3)
        two = shifted(after(outgoing(0, 2), one, three), 2)
        head = spread_first(outgoing(0, 0))
        body = spread_first(
            jnp.concatenate([one, three], axis=0), head[1][2], head[2][2]
        )
        head = spread_second(head)
        turned = [array for _, _, array in head[3:5]]
        tail = spread_first(two, body[1][2], body[2][2], *turned)
        ahead = [array for _, _, array in body[1:3]]
        across = [array for _, _, array in tail[1:3]]
        body = spread_second(body)
        tail = spread_second(tail)
        gathers = [[listed([head, body], [[0], [1, 2]]), listed([tail], [[0]])]]
        later_one = shifted(after(outgoing(1, 1), two), 1)
        later_two = shifted(after(outgoing(1, 2), across[0], across[1]), 2)
        later_three = shifted(after(outgoing(1, 3), later_two), 3)
        came = (outgoing(1, 0), later_one, later_two, later_three)
        sent = [after(out_weight[0], *ahead, *turned, two, scale, *both), out_weight[1]]
    else:
        wide = flat.astype(jnp.float32)
        squares = jnp.sum(wide * wide, axis=1, keepdims=True)
        gathers = [from_calls(layer) for layer in range(layers)]
        sent = [out_weight[layer] for layer in range(layers)]
    outs = [lax.all_gather(one, "rep", axis=0, tiled=True) for one in sent]

    columns = source * head_width
    for layer in range(layers):
        if by_links and layer == 0:
            mixed = None
            for stage, (arrays, pieces, rows) in zip(stages, gathers[0]):
                if mixed is not None:
                    mixed = lax.optimization_barrier(
                        (*mixed, later_one, later_two)
                    )[:2]
                mixed = project_qkv(
                    both, stage, core_gains, scale, arrays, pieces, rows, mixed, outputs=2
                )
            mixed = [mixed[0], swapped(mixed[1], 1)]
        else:
            mixed = project_qkv(
                hidden, list(range(parts)), gains[layer], row_scale(squares), *gathers[layer]
            )
        attended = attend(
            [one.reshape(step_count, row_count, block_width) for one in mixed],
            cosine,
            sine,
            query_gain[layer][None],
            key_gain[layer][None],
            stored_rotated_keys,
            stored_cache_values,
            lengths,
            layer,
        ).reshape(flat_rows, head_width)
        if by_links and layer + 1 < layers:
            came = lax.optimization_barrier(came + (attended,))[:parts]
            gathers.append(from_call(jnp.concatenate(came, axis=0)))
        if by_links and layer == 0:
            attended = all_parts(attended, outs[layer])
            own = project_out(attended, stages[0], outs[layer], columns)
            own = project_out(attended, stages[1], outs[layer], columns, own, hidden[0])
        else:
            own = project_out_whole(all_parts(attended), outs[layer], columns, hidden[0])
        if layer + 1 < layers:
            wide = own.astype(jnp.float32)
            mine = jnp.sum(wide * wide, axis=1).reshape(-1, 128)
            squares = sum(shifted(mine, shift) for shift in range(parts))
            hidden = all_parts(own, squares)
            squares = squares.reshape(flat_rows, 1)
        else:
            hidden = all_parts(own)
    joined = join_parts(hidden, source, replicas, piece)
    return joined.reshape(step_count, row_count, model_width)


def solution(mesh):
    return jax.shard_map(
        on_device,
        mesh=mesh,
        in_specs=(
            P(None, "rep", None),
            P(None, ("rep", "tp"), None),
            P(None, ("rep", "tp"), None),
            P(),
            P(),
            P(),
            P(None, "rep", "tp", None, None),
            P(None, "rep", "tp", None, None),
            P("rep"),
        ),
        out_specs=P(None, "rep", None),
        check_vma=False,
    )
```

time: 909 us -> 381 us (0.42)
  blocking collectives: 245 us -> 0 us
  waiting for transfers between devices: 416 us -> 191 us
  local copies, waits for them, and re-layouts: 135 us -> 29.2 us
  Pallas kernels: 0 us -> 78.7 us
  matrix products: 72 us -> 0 us
  starting transfers between devices: 0.13 us -> 56.6 us
  other arithmetic: 20.6 us -> 9.97 us
    psum x2 -> x0, waiting for transfers between devices: 357 us -> none  [on_device(): summed = lax.psum(projected, 'tp')]
    all_to_all x2 -> x0, blocking collectives: 245 us -> none  [the longest x1 146 us: on_device(): lax.all_to_all(qkv_weight, 'tp', split_axis=2, concat_axis=1, tiled=True)]
    ppermute x0 -> x40, waiting for transfers between devices: none -> 190 us  [the longest x17 102 us: shifted(): lax.ppermute(block, 'tp', [(i, (i + shift) % parts) for i in range(parts)])]
    pallas_call x0 -> x12, Pallas kernels: none -> 78.7 us  [the longest x3 29.4 us: project_qkv(): pl.pallas_call(functools.partial(qkv_kernel, count, shifts, pieces, len(w...]
    dot_general x12 -> x0, matrix products: 72 us -> none  [the longest x2 18.6 us: on_device(): lax.dot_general(attended, rows_out[layer_index], (((1,), (1,)), ((), ()))...]
    dot_general x5 -> x0, local copies, waits for them, and re-layouts: 66.2 us -> none  [the longest x3 63.6 us: on_device(): jnp.dot(normed, rows_qkv[layer_index], preferred_element_type=jnp.float32)]
    all_gather x2 -> x3, waiting for transfers between devices: 59.5 us -> 0.02 us  [the longest x2 0.02 us: on_device(): outs = [lax.all_gather(one, 'rep', axis=0, tiled=True) for one in sent]]
    ppermute x0 -> x40, starting transfers between devices: none -> 56.5 us  [the longest x17 32 us: shifted(): lax.ppermute(block, 'tp', [(i, (i + shift) % parts) for i in range(parts)])]
  transfers between devices with their start and end apart: 4 -> 43, of which waited for: 4 -> 18; matrix products, arithmetic and copies ran while one was open for 13% -> 6% of each run, Pallas kernels for 0% -> 18%
where the time goes in v1:
time: 381 us; the launch traced here: 379 us
  waiting for transfers between devices  191 us (50%)
  Pallas kernels  78.7 us (21%)
  starting transfers between devices  56.6 us (15%)
  local copies, waits for them, and re-layouts  29.2 us (8%)
  between operations  13.8 us (4%)
  other arithmetic  9.97 us (3%)
    ppermute x17, waiting for transfers between devices, shifted(): lax.ppermute(block, 'tp', [(i, (i + shift) % parts) for i in range(parts)])  102 us
    ppermute x4, waiting for transfers between devices, all_parts(): leftwards = lax.ppermute(from_right, 'tp', [(1, 0), (2, 1)])  51.8 us
    ppermute x15, waiting for transfers between devices, swapped(): return lax.ppermute(block, 'rep', [(i, i ^ mask) for i in range(replicas)])  36.1 us
    ppermute x17, starting transfers between devices, shifted(): lax.ppermute(block, 'tp', [(i, (i + shift) % parts) for i in range(parts)])  32 us
    pallas_call x3, Pallas kernels, project_qkv(): pl.pallas_call(functools.partial(qkv_kernel, count, shifts, pieces, len(w...  29.4 us
    pallas_call x2, Pallas kernels, attend(): pl.pallas_call(functools.partial(attention_kernel, heads), out_shape=jax....  25.8 us
    ppermute x15, starting transfers between devices, swapped(): return lax.ppermute(block, 'rep', [(i, i ^ mask) for i in range(replicas)])  15.6 us
    unnamed x42, local copies, waits for them, and re-layouts  10.8 us
  transfers between devices with their start and end apart: 43, of which 18 were waited for; matrix products, arithmetic and copies ran while one was open for 6% of the time, Pallas kernels for 18%

profile of v1, /device:TPU:0, one launch (start us, length us, event | category | flops | bytes accessed | tf_op | source)
XLA Modules:
  0.0 379.4 jit_solution(1064363251260137617)
XLA Ops:
  6.5 4.1 %dynamic-slice_bitcast_fusion = (bf16[160,1536]{1,0:T(8,128)(2,1)}, bf16[160,1536]{1,0:T(8,128)(2,1)}, bf16[160,1536]{1,0:T(8,128)(2,1)}, bf16[160,1536]{1,0:T(8...) fusion(bf16[2,160,6144]{2,1,0:T(8,128)(2,1)} %param.11, ...), kind=kLoop, calls=%fused_computation.15 | loop fusion | bytes 7864336 | tf_op jit(solution)/shard_map/squeeze | solution.py:472
  10.6 3.0 collective-permute-start.2
  21.6 6.5 %collective-permute-done.2 = bf16[160,1536]{1,0:T(8,128)(2,1)} collective-permute-done((bf16[160,1536]{1,0:T(8,128)(2,1)}, bf16[160,1536]{1,0:T(8,128)(2,1)}, u32[]{:S(2)}, u32[]{:S(2)}) %collective-permute-start.2) | collective-permute-done | bytes 491552 | tf_op jit(solution)/shard_map/ppermute | solution.py:457
  28.1 9.1 %collective-permute-done.3 = bf16[160,1536]{1,0:T(8,128)(2,1)} collective-permute-done((bf16[160,1536]{1,0:T(8,128)(2,1)}, bf16[160,1536]{1,0:T(8,128)(2,1)}, u32[]{:S(2)}, u32[]{:S(2)}) %collective-permute-start.3) | collective-permute-done | bytes 491552 | tf_op jit(solution)/shard_map/ppermute | solution.py:457
  42.4 3.5 fusion.5
  55.6 13.5 %collective-permute-done.9.refs_8_ = bf16[80,1536]{1,0:T(8,128)(2,1)S(1)} collective-permute-done((bf16[80,1536]{1,0:T(8,128)(2,1)S(1)}, bf16[80,1536]{1,0:T(8,128)(2,1)S(1)}, u32[]{:S(2)}, u32[]{:S(2)}) %collective-permute-start.9) | collective-permute-done | bytes 245792 | tf_op jit(solution)/shard_map/ppermute | solution.py:484
  81.2 7.1 %collective-permute-done.11.refs_4_ = bf16[160,1536]{1,0:T(8,128)(2,1)S(1)} collective-permute-done((bf16[160,1536]{1,0:T(8,128)(2,1)}, bf16[160,1536]{1,0:T(8,128)(2,1)S(1)}, u32[]{:S(2)}, u32[]{:S(2)}) %collective-permute-start.11) | collective-permute-done | bytes 491552 | tf_op jit(solution)/shard_map/ppermute | solution.py:484
  95.1 14.5 %collective-permute-done.15.refs_13_ = bf16[160,1536]{1,0:T(8,128)(2,1)} collective-permute-done((bf16[160,1536]{1,0:T(8,128)(2,1)}, bf16[160,1536]{1,0:T(8,128)(2,1)}, u32[]{:S(2)}, u32[]{:S(2)}) %collective-permute-start.15) | collective-permute-done | bytes 491552 | tf_op jit(solution)/shard_map/ppermute | solution.py:484
  114.1 9.9 %shard_map.102 = (f32[256,1536]{1,0:T(8,128)}, f32[256,1536]{1,0:T(8,128)}) custom-call(s32[13]{0:T(128)S(1)} %stack.40.rows_ref, bf16[512,640]{1,0:T(8,128)(2,1)} %get-tuple-element.67.refs_0_, bf16[512,640]{1,0:T(8,128)(2,1)} %get-tuple-element.66.refs_1_, bf16[512,640]{1,0:T(8,128)(2,1)} %get-tuple-element.65.refs_2_, ...), custom_call_target="tpu_custom_call" | custom-call | flops 3019898880 | bytes 5898240 | tf_op jit(solution)/shard_map/pallas_call | solution.py:175
  124.0 7.4 %shard_map.103 = (f32[256,1536]{1,0:T(8,128)}, f32[256,1536]{1,0:T(8,128)}) custom-call(s32[5]{0:T(128)S(1)} %stack.19.rows_ref, bf16[512,640]{1,0:T(8,128)(2,1)} %get-tuple-element.68.refs_0_, f32[4,1,640]{2,1,0:T(1,128)S(1)} %reshape.195.refs_3_.refs_1_, f32[512,1]{1,0:T(8,128)S(1)} %rsqrt.8.refs_4_.refs_2_, ...), custom_call_target="tpu_custom_call" | custom-call | flops 1006632960 | bytes 1966080 | tf_op jit(solution)/shard_map/pallas_call | solution.py:175
  131.6 4.1 %collective-permute-start.31 = (bf16[160,1536]{1,0:T(8,128)(2,1)S(1)}, bf16[160,1536]{1,0:T(8,128)(2,1)S(1)}, u32[]{:S(2)}, u32[]{:S(2)}) collective-permute-start(bf16[160,1536]{1,0:T(8,128)(2,1)S(1)} %copy-done.17), channel_id=1, source_target_pairs={{0,3},{1,0},{2,1},{3,2},{4,7},{5,4},{6,5},{7,6},{8,11},{9,8},{10,9... | collective-permute-start | bytes 1474568 | tf_op jit(solution)/shard_map/ppermute | solution.py:457
  137.8 12.7 %shard_map.104 = bf16[4,64,1024]{2,1,0:T(8,128)(2,1)S(1)} custom-call(s32[64]{0:T(128)S(1)} %copy-done.9, f32[4,64,1536]{2,1,0:T(8,128)S(1)} %bitcast.69, f32[4,64,1536]{2,1,0:T(8,128)S(1)} %bitcast.70, f32[4,64,128]{2,1,0:T(8,128)S(1)} %get-tuple-element.78.refs_2_.refs_1_, f32[4,64,128]{2,1,0:T(8,128)S(1)} %get-tuple-element.79.refs_3_.refs_2_, ...), custom_call_target="tpu_custom_call" | custom-call | flops 268435456 | bytes 16777216 | tf_op jit(solution)/shard_map/pallas_call | solution.py:399
  150.5 2.6 pad_maximum_fusion.1
  160.6 10.0 %collective-permute-done.20.refs_1_ = bf16[256,1024]{1,0:T(8,128)(2,1)} collective-permute-done((bf16[256,1024]{1,0:T(8,128)(2,1)S(1)}, bf16[256,1024]{1,0:T(8,128)(2,1)}, u32[]{:S(2)}, u32[]{:S(2)}) %collective-permute-start.20) | collective-permute-done | bytes 524320 | tf_op jit(solution)/shard_map/ppermute | solution.py:457
  170.6 9.7 %collective-permute-done.21.refs_2_ = bf16[256,1024]{1,0:T(8,128)(2,1)} collective-permute-done((bf16[256,1024]{1,0:T(8,128)(2,1)S(1)}, bf16[256,1024]{1,0:T(8,128)(2,1)}, u32[]{:S(2)}, u32[]{:S(2)}) %collective-permute-start.21) | collective-permute-done | bytes 524320 | tf_op jit(solution)/shard_map/ppermute | solution.py:457
  183.6 5.9 %shard_map.105.refs_2_ = f32[256,1280]{1,0:T(8,128)S(1)} custom-call(s32[4]{0:T(128)S(1)} %broadcast_multiply_fusion.column_ref, bf16[256,1024]{1,0:T(8,128)(2,1)S(1)} %bitcast.68, bf16[256,1024]{1,0:T(8,128)(2,1)} %collective-permute-done.20.refs_1_, bf16[256,1024]{1,0:T(8,128)(2,1)} %collective-permute-done.21.refs_2_, ...), custom_call_target="tpu_custom_call" | custom-call | flops 2013265920 | bytes 7864320 | tf_op jit(solution)/shard_map/pallas_call | solution.py:297
  189.5 7.9 %collective-permute-done.23 = bf16[256,1024]{1,0:T(8,128)(2,1)S(1)} collective-permute-done((bf16[256,1024]{1,0:T(8,128)(2,1)}, bf16[256,1024]{1,0:T(8,128)(2,1)S(1)}, u32[]{:S(2)}, u32[]{:S(2)}) %collective-permute-start.23) | collective-permute-done | bytes 524320 | tf_op jit(solution)/shard_map/ppermute | solution.py:467
  197.4 3.2 shard_map.107.refs_0_.refs_5_
  206.8 24.4 %collective-permute-done.28 = f32[2,128]{1,0:T(2,128)S(1)} collective-permute-done((f32[2,128]{1,0:T(2,128)S(1)}, f32[2,128]{1,0:T(2,128)S(1)}, u32[]{:S(2)}, u32[]{:S(2)}) %collective-permute-start.28) | collective-permute-done | bytes 1056 | tf_op jit(solution)/shard_map/ppermute | solution.py:457
  234.9 15.8 %collective-permute-done.30 = bf16[256,1280]{1,0:T(8,128)(2,1)} collective-permute-done((bf16[256,1280]{1,0:T(8,128)(2,1)S(1)}, bf16[256,1280]{1,0:T(8,128)(2,1)}, u32[]{:S(2)}, u32[]{:S(2)}) %collective-permute-start.30) | collective-permute-done | bytes 655392 | tf_op jit(solution)/shard_map/ppermute | solution.py:467
  252.7 12.2 %shard_map.108 = f32[256,1536]{1,0:T(8,128)} custom-call(s32[32]{0:T(128)S(1)} %copy-done.10, bf16[256,1280]{1,0:T(8,128)(2,1)S(1)} %shard_map.107.refs_0_.refs_5_, bf16[256,1280]{1,0:T(8,128)(2,1)S(1)} %collective-permute-done.24.refs_1_, bf16[256,1280]{1,0:T(8,128)(2,1)} %broadcast_select_fusion.1.refs_2_, bf16[256,1280]{1,0:T(8,128)(2,1)} %copy-done.16, ...), custom_call_target="tpu_custom_call" | custom-call | flops 4026531840 | bytes 15728640 | tf_op jit(solution)/shard_map/pallas_call | solution.py:175
  266.3 13.1 %shard_map.109 = bf16[4,64,1024]{2,1,0:T(8,128)(2,1)S(1)} custom-call(s32[64]{0:T(128)S(1)} %copy-done.9, f32[4,64,1536]{2,1,0:T(8,128)S(1)} %bitcast.62, f32[4,64,128]{2,1,0:T(8,128)S(1)} %get-tuple-element.78.refs_2_.refs_1_, f32[4,64,128]{2,1,0:T(8,128)S(1)} %get-tuple-element.79.refs_3_.refs_2_, f32[1,128]{1,0:T(1,128)S(1)} %get-tuple-element.81.refs_3_, ...), custom_call_target="tpu_custom_call" | custom-call | flops 268435456 | bytes 16777216 | tf_op jit(solution)/shard_map/pallas_call | solution.py:399
  280.7 2.6 collective-permute-start.34
  283.3 12.8 %collective-permute-done.32.refs_1_ = bf16[256,1024]{1,0:T(8,128)(2,1)S(1)} collective-permute-done((bf16[256,1024]{1,0:T(8,128)(2,1)S(1)}, bf16[256,1024]{1,0:T(8,128)(2,1)S(1)}, u32[]{:S(2)}, u32[]{:S(2)}) %collective-permute-start.32) | collective-permute-done | bytes 524320 | tf_op jit(solution)/shard_map/ppermute | solution.py:457
  296.9 5.7 %collective-permute-done.34.refs_3_ = bf16[256,1024]{1,0:T(8,128)(2,1)S(1)} collective-permute-done((bf16[256,1024]{1,0:T(8,128)(2,1)S(1)}, bf16[256,1024]{1,0:T(8,128)(2,1)S(1)}, u32[]{:S(2)}, u32[]{:S(2)}) %collective-permute-start.34) | collective-permute-done | bytes 524320 | tf_op jit(solution)/shard_map/ppermute | solution.py:457
  303.9 12.8 %collective-permute-done.35 = bf16[256,1024]{1,0:T(8,128)(2,1)S(1)} collective-permute-done((bf16[256,1024]{1,0:T(8,128)(2,1)S(1)}, bf16[256,1024]{1,0:T(8,128)(2,1)S(1)}, u32[]{:S(2)}, u32[]{:S(2)}) %collective-permute-start.35) | collective-permute-done | bytes 524320 | tf_op jit(solution)/shard_map/ppermute | solution.py:467
  317.8 6.3 %shard_map.110.refs_0_ = bf16[256,1280]{1,0:T(8,128)(2,1)S(1)} custom-call(s32[4]{0:T(128)S(1)} %broadcast_multiply_fusion.column_ref, bf16[256,1024]{1,0:T(8,128)(2,1)S(1)} %bitcast.65, bf16[256,1024]{1,0:T(8,128)(2,1)S(1)} %collective-permute-done.32.refs_1_, bf16[256,1024]{1,0:T(8,128)(2,1)S(1)} %broadcast_select_fusion.2.refs_2_, ...), custom_call_target="tpu_custom_call" | custom-call | flops 2684354560 | bytes 10485760 | tf_op jit(solution)/shard_map/pallas_call | solution.py:231
  324.3 3.6 collective-permute-start.38
  327.9 15.6 %collective-permute-done.36.refs_1_ = bf16[256,1280]{1,0:T(8,128)(2,1)S(1)} collective-permute-done((bf16[256,1280]{1,0:T(8,128)(2,1)S(1)}, bf16[256,1280]{1,0:T(8,128)(2,1)S(1)}, u32[]{:S(2)}, u32[]{:S(2)}) %collective-permute-start.36) | collective-permute-done | bytes 655392 | tf_op jit(solution)/shard_map/ppermute | solution.py:457
  344.3 8.0 %collective-permute-done.38.refs_3_ = bf16[256,1280]{1,0:T(8,128)(2,1)S(1)} collective-permute-done((bf16[256,1280]{1,0:T(8,128)(2,1)S(1)}, bf16[256,1280]{1,0:T(8,128)(2,1)S(1)}, u32[]{:S(2)}, u32[]{:S(2)}) %collective-permute-start.38) | collective-permute-done | bytes 655392 | tf_op jit(solution)/shard_map/ppermute | solution.py:457
  353.6 15.4 %collective-permute-done.39 = bf16[256,1280]{1,0:T(8,128)(2,1)S(1)} collective-permute-done((bf16[256,1280]{1,0:T(8,128)(2,1)S(1)}, bf16[256,1280]{1,0:T(8,128)(2,1)S(1)}, u32[]{:S(2)}, u32[]{:S(2)}) %collective-permute-start.39) | collective-permute-done | bytes 655392 | tf_op jit(solution)/shard_map/ppermute | solution.py:467
  369.1 3.8 shard_map.111
  (157 shorter events, 79.0 us)
Async XLA Ops:
  6.5 173.8 %all-gather.5.cloned.1.call-start = ((), (), s32[]{:S(2)}) async-start(), calls=%async_computation | async-start | bytes 11796480 | tf_op jit(solution)/shard_map/all_gather | solution.py:584
  10.6 17.5 %collective-permute-start.2 = (bf16[160,1536]{1,0:T(8,128)(2,1)}, bf16[160,1536]{1,0:T(8,128)(2,1)}, u32[]{:S(2)}, u32[]{:S(2)}) collective-permute-start(bf16[160,1536]{1,0:T(8,128)(2,1)} %get-tuple-element.60), channel_id=1, source_target_pairs={{0,1},{1,2},{2,3},{3,0},{4,5},{5,6},{6,7},{7,4},{8,9},{9,10},{10,1... | collective-permute-start | bytes 1474568 | tf_op jit(solution)/shard_map/ppermute | solution.py:457
  13.6 23.5 %collective-permute-start.3 = (bf16[160,1536]{1,0:T(8,128)(2,1)}, bf16[160,1536]{1,0:T(8,128)(2,1)}, u32[]{:S(2)}, u32[]{:S(2)}) collective-permute-start(bf16[160,1536]{1,0:T(8,128)(2,1)} %get-tuple-element.59), channel_id=1, source_target_pairs={{0,3},{1,0},{2,1},{3,2},{4,7},{5,4},{6,5},{7,6},{8,11},{9,8},{10,9... | collective-permute-start | bytes 1474568 | tf_op jit(solution)/shard_map/ppermute | solution.py:457
  15.7 23.7 %collective-permute-start.5 = (bf16[160,1536]{1,0:T(8,128)(2,1)S(1)}, bf16[160,1536]{1,0:T(8,128)(2,1)}, u32[]{:S(2)}, u32[]{:S(2)}) collective-permute-start(bf16[160,1536]{1,0:T(8,128)(2,1)S(1)} %get-tuple-element.58.refs_5_), channel_id=1, source_target_pairs={{0,8},{4,12},{8,0},{12,4},{16,24},{20,28},{24,16},{28,20},{1,9},{5... | collective-permute-start | bytes 1474568 | tf_op jit(solution)/shard_map/ppermute | solution.py:484
  17.4 22.0 %collective-permute-start.6 = (bf16[160,1536]{1,0:T(8,128)(2,1)S(1)}, bf16[160,1536]{1,0:T(8,128)(2,1)}, u32[]{:S(2)}, u32[]{:S(2)}) collective-permute-start(bf16[160,1536]{1,0:T(8,128)(2,1)S(1)} %get-tuple-element.58.refs_5_), channel_id=1, source_target_pairs={{0,16},{4,20},{8,24},{12,28},{16,0},{20,4},{24,8},{28,12},{1,17},{... | collective-permute-start | bytes 1474568 | tf_op jit(solution)/shard_map/ppermute | solution.py:484
  21.5 28.6 %collective-permute-start = (bf16[256,2560]{1,0:T(8,128)(2,1)}, bf16[256,2560]{1,0:T(8,128)(2,1)}, u32[]{:S(2)}, u32[]{:S(2)}) collective-permute-start(bf16[256,2560]{1,0:T(8,128)(2,1)} %get-tuple-element.30), channel_id=1, source_target_pairs={{0,4},{4,0},{8,12},{12,8},{16,20},{20,16},{24,28},{28,24},{1,5},{5... | collective-permute-start | bytes 3932168 | tf_op jit(solution)/shard_map/ppermute | solution.py:484
  28.1 17.9 %collective-permute-start.1 = (f32[2,128]{1,0:T(2,128)S(1)}, f32[2,128]{1,0:T(2,128)S(1)}, u32[]{:S(2)}, u32[]{:S(2)}) collective-permute-start(f32[2,128]{1,0:T(2,128)S(1)} %bitcast.76), channel_id=1, source_target_pairs={{0,4},{4,0},{8,12},{12,8},{16,20},{20,16},{24,28},{28,24},{1,5},{5... | collective-permute-start | bytes 3080 | tf_op jit(solution)/shard_map/ppermute | solution.py:484
  39.4 31.1 %collective-permute-start.7 = (bf16[320,1536]{1,0:T(8,128)(2,1)}, bf16[320,1536]{1,0:T(8,128)(2,1)}, u32[]{:S(2)}, u32[]{:S(2)}) collective-permute-start(bf16[320,1536]{1,0:T(8,128)(2,1)} %pad_maximum_fusion.2.refs_10_), channel_id=1, source_target_pairs={{0,8},{4,12},{8,0},{12,4},{16,24},{20,28},{24,16},{28,20},{1,9},{5... | collective-permute-start | bytes 2949128 | tf_op jit(solution)/shard_map/ppermute | solution.py:484
  40.9 29.7 %collective-permute-start.8 = (bf16[320,1536]{1,0:T(8,128)(2,1)}, bf16[320,1536]{1,0:T(8,128)(2,1)}, u32[]{:S(2)}, u32[]{:S(2)}) collective-permute-start(bf16[320,1536]{1,0:T(8,128)(2,1)} %pad_maximum_fusion.2.refs_10_), channel_id=1, source_target_pairs={{0,16},{4,20},{8,24},{12,28},{16,0},{20,4},{24,8},{28,12},{1,17},{... | collective-permute-start | bytes 2949128 | tf_op jit(solution)/shard_map/ppermute | solution.py:484
  46.2 24.3 %collective-permute-start.4 = (bf16[160,1536]{1,0:T(8,128)(2,1)}, bf16[160,1536]{1,0:T(8,128)(2,1)}, u32[]{:S(2)}, u32[]{:S(2)}) collective-permute-start(bf16[160,1536]{1,0:T(8,128)(2,1)} %get-tuple-element.32), channel_id=1, source_target_pairs={{0,2},{1,3},{2,0},{3,1},{4,6},{5,7},{6,4},{7,5},{8,10},{9,11},{10,... | collective-permute-start | bytes 1474568 | tf_op jit(solution)/shard_map/ppermute | solution.py:457
  48.6 20.6 %collective-permute-start.9 = (bf16[80,1536]{1,0:T(8,128)(2,1)S(1)}, bf16[80,1536]{1,0:T(8,128)(2,1)S(1)}, u32[]{:S(2)}, u32[]{:S(2)}) collective-permute-start(bf16[80,1536]{1,0:T(8,128)(2,1)S(1)} %slice.82), channel_id=1, source_target_pairs={{0,16},{4,20},{8,24},{12,28},{16,0},{20,4},{24,8},{28,12},{1,17},{... | collective-permute-start | bytes 737288 | tf_op jit(solution)/shard_map/ppermute | solution.py:484
  50.1 19.7 %collective-permute-start.10 = (bf16[80,1536]{1,0:T(8,128)(2,1)S(1)}, bf16[80,1536]{1,0:T(8,128)(2,1)S(1)}, u32[]{:S(2)}, u32[]{:S(2)}) collective-permute-start(bf16[80,1536]{1,0:T(8,128)(2,1)S(1)} %slice.83), channel_id=1, source_target_pairs={{0,8},{4,12},{8,0},{12,4},{16,24},{20,28},{24,16},{28,20},{1,9},{5... | collective-permute-start | bytes 737288 | tf_op jit(solution)/shard_map/ppermute | solution.py:484
  70.5 182.2 %all-gather.7.cloned.1.call-start = ((), (), s32[]{:S(2)}) async-start(), calls=%async_computation.1 | async-start | bytes 17694720 | tf_op jit(solution)/shard_map/all_gather | solution.py:533
  70.6 17.7 %collective-permute-start.11 = (bf16[160,1536]{1,0:T(8,128)(2,1)}, bf16[160,1536]{1,0:T(8,128)(2,1)S(1)}, u32[]{:S(2)}, u32[]{:S(2)}) collective-permute-start(bf16[160,1536]{1,0:T(8,128)(2,1)} %collective-permute-done.4.refs_3_), channel_id=1, source_target_pairs={{0,8},{4,12},{8,0},{12,4},{16,24},{20,28},{24,16},{28,20},{1,9},{5... | collective-permute-start | bytes 1474568 | tf_op jit(solution)/shard_map/ppermute | solution.py:484
  71.2 18.0 %collective-permute-start.12 = (bf16[160,1536]{1,0:T(8,128)(2,1)}, bf16[160,1536]{1,0:T(8,128)(2,1)}, u32[]{:S(2)}, u32[]{:S(2)}) collective-permute-start(bf16[160,1536]{1,0:T(8,128)(2,1)} %collective-permute-done.4.refs_3_), channel_id=1, source_target_pairs={{0,16},{4,20},{8,24},{12,28},{16,0},{20,4},{24,8},{28,12},{1,17},{... | collective-permute-start | bytes 1474568 | tf_op jit(solution)/shard_map/ppermute | solution.py:484
  74.6 35.0 %collective-permute-start.15 = (bf16[160,1536]{1,0:T(8,128)(2,1)}, bf16[160,1536]{1,0:T(8,128)(2,1)}, u32[]{:S(2)}, u32[]{:S(2)}) collective-permute-start(bf16[160,1536]{1,0:T(8,128)(2,1)} %slice.89), channel_id=1, source_target_pairs={{0,16},{4,20},{8,24},{12,28},{16,0},{20,4},{24,8},{28,12},{1,17},{... | collective-permute-start | bytes 1474568 | tf_op jit(solution)/shard_map/ppermute | solution.py:484
  76.9 34.2 %collective-permute-start.16 = (bf16[160,1536]{1,0:T(8,128)(2,1)}, bf16[160,1536]{1,0:T(8,128)(2,1)}, u32[]{:S(2)}, u32[]{:S(2)}) collective-permute-start(bf16[160,1536]{1,0:T(8,128)(2,1)} %slice.90), channel_id=1, source_target_pairs={{0,8},{4,12},{8,0},{12,4},{16,24},{20,28},{24,16},{28,20},{1,9},{5... | collective-permute-start | bytes 1474568 | tf_op jit(solution)/shard_map/ppermute | solution.py:484
  79.5 44.5 %collective-permute-start.17 = (bf16[160,1536]{1,0:T(8,128)(2,1)}, bf16[160,1536]{1,0:T(8,128)(2,1)}, u32[]{:S(2)}, u32[]{:S(2)}) collective-permute-start(bf16[160,1536]{1,0:T(8,128)(2,1)} %get-tuple-element.37), channel_id=1, source_target_pairs={{0,1},{1,2},{2,3},{3,0},{4,5},{5,6},{6,7},{7,4},{8,9},{9,10},{10,1... | collective-permute-start | bytes 1474568 | tf_op jit(solution)/shard_map/ppermute | solution.py:457
  89.2 34.8 %collective-permute-start.18 = (bf16[160,1536]{1,0:T(8,128)(2,1)}, bf16[160,1536]{1,0:T(8,128)(2,1)}, u32[]{:S(2)}, u32[]{:S(2)}) collective-permute-start(bf16[160,1536]{1,0:T(8,128)(2,1)} %get-tuple-element.38), channel_id=1, source_target_pairs={{0,2},{1,3},{2,0},{3,1},{4,6},{5,7},{6,4},{7,5},{8,10},{9,11},{10,... | collective-permute-start | bytes 1474568 | tf_op jit(solution)/shard_map/ppermute | solution.py:457
  91.6 32.4 %collective-permute-start.13 = (bf16[80,1536]{1,0:T(8,128)(2,1)S(1)}, bf16[80,1536]{1,0:T(8,128)(2,1)S(1)}, u32[]{:S(2)}, u32[]{:S(2)}) collective-permute-start(bf16[80,1536]{1,0:T(8,128)(2,1)S(1)} %slice.84), channel_id=1, source_target_pairs={{0,16},{4,20},{8,24},{12,28},{16,0},{20,4},{24,8},{28,12},{1,17},{... | collective-permute-start | bytes 737288 | tf_op jit(solution)/shard_map/ppermute | solution.py:484
  131.6 18.9 %collective-permute-start.31 = (bf16[160,1536]{1,0:T(8,128)(2,1)S(1)}, bf16[160,1536]{1,0:T(8,128)(2,1)S(1)}, u32[]{:S(2)}, u32[]{:S(2)}) collective-permute-start(bf16[160,1536]{1,0:T(8,128)(2,1)S(1)} %copy-done.17), channel_id=1, source_target_pairs={{0,3},{1,0},{2,1},{3,2},{4,7},{5,4},{6,5},{7,6},{8,11},{9,8},{10,9... | collective-permute-start | bytes 1474568 | tf_op jit(solution)/shard_map/ppermute | solution.py:457
  153.1 163.6 %all-gather.9.cloned.1.call-start = ((), (), s32[]{:S(2)}) async-start(), calls=%async_computation.2 | async-start | bytes 11796480 | tf_op jit(solution)/shard_map/all_gather | solution.py:584
  155.2 25.1 %collective-permute-start.21 = (bf16[256,1024]{1,0:T(8,128)(2,1)S(1)}, bf16[256,1024]{1,0:T(8,128)(2,1)}, u32[]{:S(2)}, u32[]{:S(2)}) collective-permute-start(bf16[256,1024]{1,0:T(8,128)(2,1)S(1)} %bitcast.67), channel_id=1, source_target_pairs={{0,3},{1,0},{2,1},{3,2},{4,7},{5,4},{6,5},{7,6},{8,11},{9,8},{10,9... | collective-permute-start | bytes 1572872 | tf_op jit(solution)/shard_map/ppermute | solution.py:457
  200.6 31.2 %collective-permute-start.24 = (bf16[256,1280]{1,0:T(8,128)(2,1)S(1)}, bf16[256,1280]{1,0:T(8,128)(2,1)S(1)}, u32[]{:S(2)}, u32[]{:S(2)}) collective-permute-start(bf16[256,1280]{1,0:T(8,128)(2,1)S(1)} %shard_map.107.refs_0_.refs_5_), channel_id=1, source_target_pairs={{0,1},{1,2},{2,3},{3,0},{4,5},{5,6},{6,7},{7,4},{8,9},{9,10},{10,1... | collective-permute-start | bytes 1966088 | tf_op jit(solution)/shard_map/ppermute | solution.py:457
  202.4 29.4 %collective-permute-start.25 = (bf16[256,1280]{1,0:T(8,128)(2,1)S(1)}, bf16[256,1280]{1,0:T(8,128)(2,1)S(1)}, u32[]{:S(2)}, u32[]{:S(2)}) collective-permute-start(bf16[256,1280]{1,0:T(8,128)(2,1)S(1)} %shard_map.107.refs_0_.refs_5_), channel_id=1, source_target_pairs={{0,3},{1,0},{2,1},{3,2},{4,7},{5,4},{6,5},{7,6},{8,11},{9,8},{10,9... | collective-permute-start | bytes 1966088 | tf_op jit(solution)/shard_map/ppermute | solution.py:457
  204.7 26.4 %collective-permute-start.28 = (f32[2,128]{1,0:T(2,128)S(1)}, f32[2,128]{1,0:T(2,128)S(1)}, u32[]{:S(2)}, u32[]{:S(2)}) collective-permute-start(f32[2,128]{1,0:T(2,128)S(1)} %bitcast.72), channel_id=1, source_target_pairs={{0,3},{1,0},{2,1},{3,2},{4,7},{5,4},{6,5},{7,6},{8,11},{9,8},{10,9... | collective-permute-start | bytes 3080 | tf_op jit(solution)/shard_map/ppermute | solution.py:457
  204.8 26.4 %collective-permute-start.27 = (f32[2,128]{1,0:T(2,128)S(1)}, f32[2,128]{1,0:T(2,128)S(1)}, u32[]{:S(2)}, u32[]{:S(2)}) collective-permute-start(f32[2,128]{1,0:T(2,128)S(1)} %bitcast.73), channel_id=1, source_target_pairs={{0,2},{1,3},{2,0},{3,1},{4,6},{5,7},{6,4},{7,5},{8,10},{9,11},{10,... | collective-permute-start | bytes 3080 | tf_op jit(solution)/shard_map/ppermute | solution.py:457
  206.2 25.6 %collective-permute-start.26 = (f32[2,128]{1,0:T(2,128)S(1)}, f32[2,128]{1,0:T(2,128)S(1)}, u32[]{:S(2)}, u32[]{:S(2)}) collective-permute-start(f32[2,128]{1,0:T(2,128)S(1)} %bitcast.74), channel_id=1, source_target_pairs={{0,1},{1,2},{2,3},{3,0},{4,5},{5,6},{6,7},{7,4},{8,9},{9,10},{10,1... | collective-permute-start | bytes 3080 | tf_op jit(solution)/shard_map/ppermute | solution.py:457
  233.4 17.3 %collective-permute-start.30 = (bf16[256,1280]{1,0:T(8,128)(2,1)S(1)}, bf16[256,1280]{1,0:T(8,128)(2,1)}, u32[]{:S(2)}, u32[]{:S(2)}) collective-permute-start(bf16[256,1280]{1,0:T(8,128)(2,1)S(1)} %collective-permute-done.25.refs_3_), channel_id=1, source_target_pairs={{1,0},{2,1},{5,4},{6,5},{9,8},{10,9},{13,12},{14,13},{17,16},{18,1... | collective-permute-start | bytes 1966088 | tf_op jit(solution)/shard_map/ppermute | solution.py:467
  280.7 21.8 %collective-permute-start.34 = (bf16[256,1024]{1,0:T(8,128)(2,1)S(1)}, bf16[256,1024]{1,0:T(8,128)(2,1)S(1)}, u32[]{:S(2)}, u32[]{:S(2)}) collective-permute-start(bf16[256,1024]{1,0:T(8,128)(2,1)S(1)} %bitcast.64), channel_id=1, source_target_pairs={{0,3},{1,0},{2,1},{3,2},{4,7},{5,4},{6,5},{7,6},{8,11},{9,8},{10,9... | collective-permute-start | bytes 1572872 | tf_op jit(solution)/shard_map/ppermute | solution.py:457
  324.0 19.5 %collective-permute-start.36 = (bf16[256,1280]{1,0:T(8,128)(2,1)S(1)}, bf16[256,1280]{1,0:T(8,128)(2,1)S(1)}, u32[]{:S(2)}, u32[]{:S(2)}) collective-permute-start(bf16[256,1280]{1,0:T(8,128)(2,1)S(1)} %shard_map.110.refs_0_), channel_id=1, source_target_pairs={{0,1},{1,2},{2,3},{3,0},{4,5},{5,6},{6,7},{7,4},{8,9},{9,10},{10,1... | collective-permute-start | bytes 1966088 | tf_op jit(solution)/shard_map/ppermute | solution.py:457
  324.3 28.0 %collective-permute-start.38 = (bf16[256,1280]{1,0:T(8,128)(2,1)S(1)}, bf16[256,1280]{1,0:T(8,128)(2,1)S(1)}, u32[]{:S(2)}, u32[]{:S(2)}) collective-permute-start(bf16[256,1280]{1,0:T(8,128)(2,1)S(1)} %shard_map.110.refs_0_), channel_id=1, source_target_pairs={{0,3},{1,0},{2,1},{3,2},{4,7},{5,4},{6,5},{7,6},{8,11},{9,8},{10,9... | collective-permute-start | bytes 1966088 | tf_op jit(solution)/shard_map/ppermute | solution.py:457
  (32 other events, 351.1 us)
Sparse Core Ops, SparseCore 0:
  70.7 77.5 all-gather.4
  153.2 85.5 all-gather.6
  240.7 63.2 all-gather.8

commit v2 on v1

--- a/solution.py
+++ b/solution.py
@@ -109,9 +109,11 @@
     )(place, *blocks)
 
 
-def qkv_kernel(count, shifts, pieces, arrays, continued, rows_ref, *refs):
+def qkv_kernel(count, shifts, pieces, arrays, scaled, continued, rows_ref, *refs):
     block_refs, refs = refs[:count], refs[count:]
-    gain_ref, scale_ref, refs = refs[0], refs[1], refs[2:]
+    gain_ref, refs = refs[0], refs[1:]
+    if scaled:
+        scale_ref, refs = refs[0], refs[1:]
     weight_refs, refs = refs[:arrays], refs[arrays:]
     outputs = (len(refs) - 3) // (2 if continued else 1)
     if continued:
@@ -135,7 +137,15 @@
     @pl.loop(0, normed.shape[1] // step)
     def _(tile):
         rows = pl.ds(pl.multiple_of(tile * step, step), step)
-        scale = scale_ref[rows, :]
+        if scaled:
+            scale = scale_ref[rows, :]
+        else:
+            squares = None
+            for ref in block_refs:
+                wide = ref[rows, :].astype(jnp.float32)
+                term = jnp.sum(wide * wide, axis=-1, keepdims=True)
+                squares = term if squares is None else squares + term
+            scale = lax.rsqrt(squares / (count * normed.shape[2]) + epsilon)
         for place, shift in enumerate(shifts):
             wide = block_refs[place][rows, :].astype(jnp.float32)
             normed[place, rows, :] = (wide * scale * gain_ref[shift]).astype(jnp.bfloat16)
@@ -166,14 +176,18 @@
     row_total, width = blocks[0].shape
     columns = weights[0].shape[1]
     continued = before is not None
-    operands = [rows] + [blocks[shift] for shift in shifts] + [gains, scale] + list(weights)
-    in_specs = [smem_spec()] + [vmem_spec()] * (count + 2) + [any_spec()] * len(weights)
+    scaled = scale is not None
+    operands = [rows] + [blocks[shift] for shift in shifts] + [gains] + [scale] * scaled
+    in_specs = [smem_spec()] + [vmem_spec()] * (len(operands) - 1) + [any_spec()] * len(weights)
+    operands += list(weights)
     if continued:
         operands += list(before)
         in_specs += [vmem_spec()] * outputs
     mixed = jax.ShapeDtypeStruct((row_total // outputs, columns), jnp.float32)
     return pl.pallas_call(
-        functools.partial(qkv_kernel, count, shifts, pieces, len(weights), continued),
+        functools.partial(
+            qkv_kernel, count, shifts, pieces, len(weights), scaled, continued
+        ),
         out_shape=[mixed] * outputs,
         in_specs=in_specs,
         out_specs=[vmem_spec()] * outputs,
@@ -182,7 +196,7 @@
             VMEM((count, row_total, width), jnp.bfloat16),
             pltpu.SemaphoreType.DMA((len(pieces),)),
         ],
-        compiler_params=pltpu.CompilerParams(vmem_limit_bytes=52 * MIB),
+        compiler_params=pltpu.CompilerParams(vmem_limit_bytes=(52 if scaled else 40) * MIB),
         cost_estimate=pl.CostEstimate(
             flops=2 * row_total * count * width * columns,
             bytes_accessed=2 * count * width * columns,
@@ -569,16 +583,16 @@
         ahead = [array for _, _, array in body[1:3]]
         across = [array for _, _, array in tail[1:3]]
         body = spread_second(body)
+        turned += [array for _, _, array in body[3:5]]
         tail = spread_second(tail)
         gathers = [[listed([head, body], [[0], [1, 2]]), listed([tail], [[0]])]]
-        later_one = shifted(after(outgoing(1, 1), two), 1)
-        later_two = shifted(after(outgoing(1, 2), across[0], across[1]), 2)
-        later_three = shifted(after(outgoing(1, 3), later_two), 3)
+        later_two = shifted(after(outgoing(1, 2), two), 2)
+        later_one = shifted(after(outgoing(1, 1), *across), 1)
+        later_three = shifted(after(outgoing(1, 3), later_one), 3)
         came = (outgoing(1, 0), later_one, later_two, later_three)
-        sent = [after(out_weight[0], *ahead, *turned, two, scale, *both), out_weight[1]]
+        ready = (scale, core_gains, gathers[0][0][2], gathers[0][1][2], *both)
+        sent = [after(out_weight[0], *across, *turned, later_two, *ready), out_weight[1]]
     else:
-        wide = flat.astype(jnp.float32)
-        squares = jnp.sum(wide * wide, axis=1, keepdims=True)
         gathers = [from_calls(layer) for layer in range(layers)]
         sent = [out_weight[layer] for layer in range(layers)]
     outs = [lax.all_gather(one, "rep", axis=0, tiled=True) for one in sent]
@@ -598,7 +612,7 @@
             mixed = [mixed[0], swapped(mixed[1], 1)]
         else:
             mixed = project_qkv(
-                hidden, list(range(parts)), gains[layer], row_scale(squares), *gathers[layer]
+                hidden, list(range(parts)), gains[layer], None, *gathers[layer]
             )
         attended = attend(
             [one.reshape(step_count, row_count, block_width) for one in mixed],
@@ -611,23 +625,15 @@
             lengths,
             layer,
         ).reshape(flat_rows, head_width)
-        if by_links and layer + 1 < layers:
-            came = lax.optimization_barrier(came + (attended,))[:parts]
+        if by_links and layer == 0:
+            came = lax.optimization_barrier((*came, attended))[:parts]
             gathers.append(from_call(jnp.concatenate(came, axis=0)))
-        if by_links and layer == 0:
             attended = all_parts(attended, outs[layer])
             own = project_out(attended, stages[0], outs[layer], columns)
             own = project_out(attended, stages[1], outs[layer], columns, own, hidden[0])
         else:
             own = project_out_whole(all_parts(attended), outs[layer], columns, hidden[0])
-        if layer + 1 < layers:
-            wide = own.astype(jnp.float32)
-            mine = jnp.sum(wide * wide, axis=1).reshape(-1, 128)
-            squares = sum(shifted(mine, shift) for shift in range(parts))
-            hidden = all_parts(own, squares)
-            squares = squares.reshape(flat_rows, 1)
-        else:
-            hidden = all_parts(own)
+        hidden = all_parts(own)
     joined = join_parts(hidden, source, replicas, piece)
     return joined.reshape(step_count, row_count, model_width)
 

time: 381 us -> 387 us (1.016)
  waiting for transfers between devices: 191 us -> 211 us
  starting transfers between devices: 56.6 us -> 51.9 us
  local copies, waits for them, and re-layouts: 29.2 us -> 24.6 us
    ppermute x17 -> x14, waiting for transfers between devices: 102 us -> 142 us  [shifted(): lax.ppermute(block, 'tp', [(i, (i + shift) % parts) for i in range(parts)])]
    ppermute x15, waiting for transfers between devices: 36.1 us -> 2.68 us  [swapped(): return lax.ppermute(block, 'rep', [(i, i ^ mask) for i in range(replicas)])]
    all_gather x1, waiting for transfers between devices: 0.01 us -> 10.9 us  [from_call(): array = lax.all_gather(came, 'rep', axis=0, tiled=True)]
    unnamed x42, local copies, waits for them, and re-layouts: 10.8 us -> 6.37 us
    ppermute x17 -> x14, starting transfers between devices: 32 us -> 28 us  [shifted(): lax.ppermute(block, 'tp', [(i, (i + shift) % parts) for i in range(parts)])]
  transfers between devices with their start and end apart: 43 -> 40, of which waited for: 18 -> 20; matrix products, arithmetic and copies ran while one was open for 6% -> 6% of each run, Pallas kernels for 18% -> 18%
where the time goes in v2:
time: 387 us; the launch traced here: 386 us
  waiting for transfers between devices  211 us (55%)
  Pallas kernels  77.8 us (20%)
  starting transfers between devices  51.9 us (13%)
  local copies, waits for them, and re-layouts  24.6 us (6%)
  between operations  13.7 us (4%)
  other arithmetic  7.35 us (2%)
    ppermute x14, waiting for transfers between devices, shifted(): lax.ppermute(block, 'tp', [(i, (i + shift) % parts) for i in range(parts)])  142 us
    ppermute x4, waiting for transfers between devices, all_parts(): leftwards = lax.ppermute(from_right, 'tp', [(1, 0), (2, 1)])  54.5 us
    ppermute x14, starting transfers between devices, shifted(): lax.ppermute(block, 'tp', [(i, (i + shift) % parts) for i in range(parts)])  28 us
    pallas_call x3, Pallas kernels, project_qkv(): pl.pallas_call(functools.partial(qkv_kernel, count, shifts, pieces, len(w...  27.4 us
    pallas_call x2, Pallas kernels, attend(): pl.pallas_call(functools.partial(attention_kernel, heads), out_shape=jax....  26.3 us
    ppermute x15, starting transfers between devices, swapped(): return lax.ppermute(block, 'rep', [(i, i ^ mask) for i in range(replicas)])  15 us
    all_gather x1, waiting for transfers between devices, from_call(): array = lax.all_gather(came, 'rep', axis=0, tiled=True)  10.9 us
    pallas_call x2, Pallas kernels, project_out(): pl.pallas_call(functools.partial(out_kernel, count, shifts), out_shape=ja...  9.72 us
  transfers between devices with their start and end apart: 40, of which 20 were waited for; matrix products, arithmetic and copies ran while one was open for 6% of the time, Pallas kernels for 18%

profile of v2, /device:TPU:0, one launch (start us, length us, event | category | flops | bytes accessed | tf_op | source)
XLA Modules:
  0.0 386.1 jit_solution(753258995941673230)
XLA Ops:
  6.5 4.0 %dynamic-slice_bitcast_fusion = (bf16[160,1536]{1,0:T(8,128)(2,1)}, bf16[160,1536]{1,0:T(8,128)(2,1)}, bf16[160,1536]{1,0:T(8,128)(2,1)}, bf16[160,1536]{1,0:T(8...) fusion(bf16[2,160,6144]{2,1,0:T(8,128)(2,1)} %param.11, ...), kind=kLoop, calls=%fused_computation.14 | loop fusion | bytes 7864336 | tf_op jit(solution)/shard_map/squeeze | solution.py:486
  10.6 2.9 collective-permute-start.5
  22.4 10.4 %collective-permute-done.2 = bf16[160,1536]{1,0:T(8,128)(2,1)} collective-permute-done((bf16[160,1536]{1,0:T(8,128)(2,1)}, bf16[160,1536]{1,0:T(8,128)(2,1)}, u32[]{:S(2)}, u32[]{:S(2)}) %collective-permute-start.2) | collective-permute-done | bytes 491552 | tf_op jit(solution)/shard_map/ppermute | solution.py:471
  32.8 9.6 %collective-permute-done.3 = bf16[160,1536]{1,0:T(8,128)(2,1)} collective-permute-done((bf16[160,1536]{1,0:T(8,128)(2,1)}, bf16[160,1536]{1,0:T(8,128)(2,1)}, u32[]{:S(2)}, u32[]{:S(2)}) %collective-permute-start.3) | collective-permute-done | bytes 491552 | tf_op jit(solution)/shard_map/ppermute | solution.py:471
  52.6 16.8 %collective-permute-done.4.refs_3_ = bf16[160,1536]{1,0:T(8,128)(2,1)S(1)} collective-permute-done((bf16[160,1536]{1,0:T(8,128)(2,1)}, bf16[160,1536]{1,0:T(8,128)(2,1)S(1)}, u32[]{:S(2)}, u32[]{:S(2)}) %collective-permute-start.4) | collective-permute-done | bytes 491552 | tf_op jit(solution)/shard_map/ppermute | solution.py:471
  73.6 2.3 collective-permute-start.18
  87.2 10.2 %collective-permute-done.18 = bf16[160,1536]{1,0:T(8,128)(2,1)S(1)} collective-permute-done((bf16[160,1536]{1,0:T(8,128)(2,1)}, bf16[160,1536]{1,0:T(8,128)(2,1)S(1)}, u32[]{:S(2)}, u32[]{:S(2)}) %collective-permute-start.18) | collective-permute-done | bytes 491552 | tf_op jit(solution)/shard_map/ppermute | solution.py:471
  108.2 9.4 %shard_map.102 = (f32[256,1536]{1,0:T(8,128)}, f32[256,1536]{1,0:T(8,128)}) custom-call(s32[13]{0:T(128)S(1)} %stack.40.rows_ref, bf16[512,640]{1,0:T(8,128)(2,1)} %get-tuple-element.61.refs_0_, bf16[512,640]{1,0:T(8,128)(2,1)} %get-tuple-element.60.refs_1_, bf16[512,640]{1,0:T(8,128)(2,1)} %get-tuple-element.59.refs_2_, ...), custom_call_target="tpu_custom_call" | custom-call | flops 3019898880 | bytes 5898240 | tf_op jit(solution)/shard_map/pallas_call | solution.py:187
  117.6 7.7 %shard_map.103 = (f32[256,1536]{1,0:T(8,128)}, f32[256,1536]{1,0:T(8,128)}) custom-call(s32[5]{0:T(128)S(1)} %stack.19.rows_ref, bf16[512,640]{1,0:T(8,128)(2,1)} %get-tuple-element.62.refs_0_, f32[4,1,640]{2,1,0:T(1,128)S(1)} %reshape.165.refs_3_.refs_1_, f32[512,1]{1,0:T(8,128)S(1)} %rsqrt.3.refs_4_.refs_2_, bf16[160,1536]{1,0:T(8,128)(2,1)S(1)} %copy-done.8, ...), custom_call_target="tpu_custom_call" | custom-call | flops 1006632960 | bytes 1966080 | tf_op jit(solution)/shard_map/pallas_call | solution.py:187
  125.5 2.9 collective-permute-start.28
  130.5 13.4 %shard_map.104 = bf16[4,64,1024]{2,1,0:T(8,128)(2,1)S(1)} custom-call(s32[64]{0:T(128)S(1)} %copy-done.9, f32[4,64,1536]{2,1,0:T(8,128)S(1)} %bitcast.65, f32[4,64,1536]{2,1,0:T(8,128)S(1)} %bitcast.66, f32[4,64,128]{2,1,0:T(8,128)S(1)} %get-tuple-element.72.refs_2_.refs_1_, f32[4,64,128]{2,1,0:T(8,128)S(1)} %get-tuple-element.73.refs_3_.refs_2_, ...), custom_call_target="tpu_custom_call" | custom-call | flops 268435456 | bytes 16777216 | tf_op jit(solution)/shard_map/pallas_call | solution.py:413
  146.2 3.8 collective-permute-start.21
  152.9 10.0 %collective-permute-done.20.refs_1_ = bf16[256,1024]{1,0:T(8,128)(2,1)} collective-permute-done((bf16[256,1024]{1,0:T(8,128)(2,1)S(1)}, bf16[256,1024]{1,0:T(8,128)(2,1)}, u32[]{:S(2)}, u32[]{:S(2)}) %collective-permute-start.20) | collective-permute-done | bytes 524320 | tf_op jit(solution)/shard_map/ppermute | solution.py:471
  162.9 10.3 %collective-permute-done.21.refs_2_ = bf16[256,1024]{1,0:T(8,128)(2,1)} collective-permute-done((bf16[256,1024]{1,0:T(8,128)(2,1)S(1)}, bf16[256,1024]{1,0:T(8,128)(2,1)}, u32[]{:S(2)}, u32[]{:S(2)}) %collective-permute-start.21) | collective-permute-done | bytes 524320 | tf_op jit(solution)/shard_map/ppermute | solution.py:471
  176.6 6.5 %shard_map.105.refs_2_ = f32[256,1280]{1,0:T(8,128)S(1)} custom-call(s32[4]{0:T(128)S(1)} %broadcast_multiply_fusion.column_ref, bf16[256,1024]{1,0:T(8,128)(2,1)S(1)} %bitcast.64, bf16[256,1024]{1,0:T(8,128)(2,1)} %collective-permute-done.20.refs_1_, bf16[256,1024]{1,0:T(8,128)(2,1)} %collective-permute-done.21.refs_2_, ...), custom_call_target="tpu_custom_call" | custom-call | flops 2013265920 | bytes 7864320 | tf_op jit(solution)/shard_map/pallas_call | solution.py:311
  183.1 7.3 %collective-permute-done.23 = bf16[256,1024]{1,0:T(8,128)(2,1)S(1)} collective-permute-done((bf16[256,1024]{1,0:T(8,128)(2,1)}, bf16[256,1024]{1,0:T(8,128)(2,1)S(1)}, u32[]{:S(2)}, u32[]{:S(2)}) %collective-permute-start.23) | collective-permute-done | bytes 524320 | tf_op jit(solution)/shard_map/ppermute | solution.py:481
  190.5 3.2 shard_map.107.refs_0_.refs_5_
  197.6 15.7 %collective-permute-done.24.refs_1_ = bf16[256,1280]{1,0:T(8,128)(2,1)S(1)} collective-permute-done((bf16[256,1280]{1,0:T(8,128)(2,1)S(1)}, bf16[256,1280]{1,0:T(8,128)(2,1)S(1)}, u32[]{:S(2)}, u32[]{:S(2)}) %collective-permute-start.24) | collective-permute-done | bytes 655392 | tf_op jit(solution)/shard_map/ppermute | solution.py:471
  214.7 9.4 %collective-permute-done.26.refs_3_ = bf16[256,1280]{1,0:T(8,128)(2,1)S(1)} collective-permute-done((bf16[256,1280]{1,0:T(8,128)(2,1)S(1)}, bf16[256,1280]{1,0:T(8,128)(2,1)S(1)}, u32[]{:S(2)}, u32[]{:S(2)}) %collective-permute-start.26) | collective-permute-done | bytes 655392 | tf_op jit(solution)/shard_map/ppermute | solution.py:471
  225.5 16.6 %collective-permute-done.27 = bf16[256,1280]{1,0:T(8,128)(2,1)} collective-permute-done((bf16[256,1280]{1,0:T(8,128)(2,1)S(1)}, bf16[256,1280]{1,0:T(8,128)(2,1)}, u32[]{:S(2)}, u32[]{:S(2)}) %collective-permute-start.27) | collective-permute-done | bytes 655392 | tf_op jit(solution)/shard_map/ppermute | solution.py:481
  243.3 10.9 %all-gather.7.cloned.1.call-done.refs_5_ = bf16[5120,1536]{1,0:T(8,128)(2,1)} async-done(((bf16[640,1536]{1,0:T(8,128)(2,1)}), bf16[5120,1536]{1,0:T(8,128)(2,1)}) %all-gather.7.cloned.1.call-update) | async-done | bytes 15728656 | tf_op jit(solution)/shard_map/all_gather | solution.py:547
  254.1 10.3 %shard_map.108 = f32[256,1536]{1,0:T(8,128)S(1)} custom-call(s32[32]{0:T(128)S(1)} %copy-done.10, bf16[256,1280]{1,0:T(8,128)(2,1)S(1)} %shard_map.107.refs_0_.refs_5_, bf16[256,1280]{1,0:T(8,128)(2,1)S(1)} %collective-permute-done.24.refs_1_, bf16[256,1280]{1,0:T(8,128)(2,1)S(1)} %broadcast_select_fusion.1.refs_2_, ...), custom_call_target="tpu_custom_call" | custom-call | flops 4026531840 | bytes 15728640 | tf_op jit(solution)/shard_map/pallas_call | solution.py:187
  264.4 12.9 %shard_map.109 = bf16[4,64,1024]{2,1,0:T(8,128)(2,1)S(1)} custom-call(s32[64]{0:T(128)S(1)} %copy-done.9, f32[4,64,1536]{2,1,0:T(8,128)S(1)} %bitcast.58, f32[4,64,128]{2,1,0:T(8,128)S(1)} %get-tuple-element.72.refs_2_.refs_1_, f32[4,64,128]{2,1,0:T(8,128)S(1)} %get-tuple-element.73.refs_3_.refs_2_, f32[1,128]{1,0:T(1,128)S(1)} %get-tuple-element.75.refs_3_, ...), custom_call_target="tpu_custom_call" | custom-call | flops 268435456 | bytes 16777216 | tf_op jit(solution)/shard_map/pallas_call | solution.py:413
  278.8 2.5 collective-permute-start.31
  281.2 12.8 %collective-permute-done.29.refs_1_ = bf16[256,1024]{1,0:T(8,128)(2,1)S(1)} collective-permute-done((bf16[256,1024]{1,0:T(8,128)(2,1)S(1)}, bf16[256,1024]{1,0:T(8,128)(2,1)S(1)}, u32[]{:S(2)}, u32[]{:S(2)}) %collective-permute-start.29) | collective-permute-done | bytes 524320 | tf_op jit(solution)/shard_map/ppermute | solution.py:471
  294.7 9.2 %collective-permute-done.31.refs_3_ = bf16[256,1024]{1,0:T(8,128)(2,1)S(1)} collective-permute-done((bf16[256,1024]{1,0:T(8,128)(2,1)S(1)}, bf16[256,1024]{1,0:T(8,128)(2,1)S(1)}, u32[]{:S(2)}, u32[]{:S(2)}) %collective-permute-start.31) | collective-permute-done | bytes 524320 | tf_op jit(solution)/shard_map/ppermute | solution.py:471
  305.2 14.0 %collective-permute-done.32 = bf16[256,1024]{1,0:T(8,128)(2,1)S(1)} collective-permute-done((bf16[256,1024]{1,0:T(8,128)(2,1)S(1)}, bf16[256,1024]{1,0:T(8,128)(2,1)S(1)}, u32[]{:S(2)}, u32[]{:S(2)}) %collective-permute-start.32) | collective-permute-done | bytes 524320 | tf_op jit(solution)/shard_map/ppermute | solution.py:481
  319.3 6.3 %shard_map.110.refs_0_ = bf16[256,1280]{1,0:T(8,128)(2,1)S(1)} custom-call(s32[4]{0:T(128)S(1)} %broadcast_multiply_fusion.column_ref, bf16[256,1024]{1,0:T(8,128)(2,1)S(1)} %bitcast.61, bf16[256,1024]{1,0:T(8,128)(2,1)S(1)} %collective-permute-done.29.refs_1_, bf16[256,1024]{1,0:T(8,128)(2,1)S(1)} %broadcast_select_fusion.2.refs_2_, ...), custom_call_target="tpu_custom_call" | custom-call | flops 2684354560 | bytes 10485760 | tf_op jit(solution)/shard_map/pallas_call | solution.py:245
  329.4 15.6 %collective-permute-done.33.refs_1_ = bf16[256,1280]{1,0:T(8,128)(2,1)S(1)} collective-permute-done((bf16[256,1280]{1,0:T(8,128)(2,1)S(1)}, bf16[256,1280]{1,0:T(8,128)(2,1)S(1)}, u32[]{:S(2)}, u32[]{:S(2)}) %collective-permute-start.33) | collective-permute-done | bytes 655392 | tf_op jit(solution)/shard_map/ppermute | solution.py:471
  345.7 12.1 %collective-permute-done.35.refs_3_ = bf16[256,1280]{1,0:T(8,128)(2,1)S(1)} collective-permute-done((bf16[256,1280]{1,0:T(8,128)(2,1)S(1)}, bf16[256,1280]{1,0:T(8,128)(2,1)S(1)}, u32[]{:S(2)}, u32[]{:S(2)}) %collective-permute-start.35) | collective-permute-done | bytes 655392 | tf_op jit(solution)/shard_map/ppermute | solution.py:471
  359.1 16.6 %collective-permute-done.36 = bf16[256,1280]{1,0:T(8,128)(2,1)S(1)} collective-permute-done((bf16[256,1280]{1,0:T(8,128)(2,1)S(1)}, bf16[256,1280]{1,0:T(8,128)(2,1)S(1)}, u32[]{:S(2)}, u32[]{:S(2)}) %collective-permute-start.36) | collective-permute-done | bytes 655392 | tf_op jit(solution)/shard_map/ppermute | solution.py:481
  375.8 3.8 shard_map.111
  (148 shorter events, 73.2 us)
Async XLA Ops:
  6.5 166.7 %all-gather.5.cloned.1.call-start = ((), (), s32[]{:S(2)}) async-start(), calls=%async_computation | async-start | bytes 11796480 | tf_op jit(solution)/shard_map/all_gather | solution.py:598
  10.6 34.0 %collective-permute-start.5 = (bf16[160,1536]{1,0:T(8,128)(2,1)S(1)}, bf16[160,1536]{1,0:T(8,128)(2,1)}, u32[]{:S(2)}, u32[]{:S(2)}) collective-permute-start(bf16[160,1536]{1,0:T(8,128)(2,1)S(1)} %get-tuple-element.52.refs_5_), channel_id=1, source_target_pairs={{0,8},{4,12},{8,0},{12,4},{16,24},{20,28},{24,16},{28,20},{1,9},{5... | collective-permute-start | bytes 1474568 | tf_op jit(solution)/shard_map/ppermute | solution.py:498
  13.5 31.1 %collective-permute-start.6 = (bf16[160,1536]{1,0:T(8,128)(2,1)S(1)}, bf16[160,1536]{1,0:T(8,128)(2,1)}, u32[]{:S(2)}, u32[]{:S(2)}) collective-permute-start(bf16[160,1536]{1,0:T(8,128)(2,1)S(1)} %get-tuple-element.52.refs_5_), channel_id=1, source_target_pairs={{0,16},{4,20},{8,24},{12,28},{16,0},{20,4},{24,8},{28,12},{1,17},{... | collective-permute-start | bytes 1474568 | tf_op jit(solution)/shard_map/ppermute | solution.py:498
  16.6 65.5 %collective-permute-start = (bf16[256,2560]{1,0:T(8,128)(2,1)}, bf16[256,2560]{1,0:T(8,128)(2,1)}, u32[]{:S(2)}, u32[]{:S(2)}) collective-permute-start(bf16[256,2560]{1,0:T(8,128)(2,1)} %get-tuple-element.28), channel_id=1, source_target_pairs={{0,4},{4,0},{8,12},{12,8},{16,20},{20,16},{24,28},{28,24},{1,5},{5... | collective-permute-start | bytes 3932168 | tf_op jit(solution)/shard_map/ppermute | solution.py:498
  16.6 16.2 %collective-permute-start.2 = (bf16[160,1536]{1,0:T(8,128)(2,1)}, bf16[160,1536]{1,0:T(8,128)(2,1)}, u32[]{:S(2)}, u32[]{:S(2)}) collective-permute-start(bf16[160,1536]{1,0:T(8,128)(2,1)} %get-tuple-element.54), channel_id=1, source_target_pairs={{0,1},{1,2},{2,3},{3,0},{4,5},{5,6},{6,7},{7,4},{8,9},{9,10},{10,1... | collective-permute-start | bytes 1474568 | tf_op jit(solution)/shard_map/ppermute | solution.py:471
  18.2 24.2 %collective-permute-start.3 = (bf16[160,1536]{1,0:T(8,128)(2,1)}, bf16[160,1536]{1,0:T(8,128)(2,1)}, u32[]{:S(2)}, u32[]{:S(2)}) collective-permute-start(bf16[160,1536]{1,0:T(8,128)(2,1)} %get-tuple-element.53), channel_id=1, source_target_pairs={{0,3},{1,0},{2,1},{3,2},{4,7},{5,4},{6,5},{7,6},{8,11},{9,8},{10,9... | collective-permute-start | bytes 1474568 | tf_op jit(solution)/shard_map/ppermute | solution.py:471
  32.8 18.3 %collective-permute-start.1 = (f32[2,128]{1,0:T(2,128)S(1)}, f32[2,128]{1,0:T(2,128)S(1)}, u32[]{:S(2)}, u32[]{:S(2)}) collective-permute-start(f32[2,128]{1,0:T(2,128)S(1)} %bitcast.68), channel_id=1, source_target_pairs={{0,4},{4,0},{8,12},{12,8},{16,20},{20,16},{24,28},{28,24},{1,5},{5... | collective-permute-start | bytes 3080 | tf_op jit(solution)/shard_map/ppermute | solution.py:498
  44.6 31.8 %collective-permute-start.7 = (bf16[320,1536]{1,0:T(8,128)(2,1)}, bf16[320,1536]{1,0:T(8,128)(2,1)}, u32[]{:S(2)}, u32[]{:S(2)}) collective-permute-start(bf16[320,1536]{1,0:T(8,128)(2,1)} %pad_maximum_fusion.2.refs_10_), channel_id=1, source_target_pairs={{0,8},{4,12},{8,0},{12,4},{16,24},{20,28},{24,16},{28,20},{1,9},{5... | collective-permute-start | bytes 2949128 | tf_op jit(solution)/shard_map/ppermute | solution.py:498
  45.1 31.2 %collective-permute-start.8 = (bf16[320,1536]{1,0:T(8,128)(2,1)}, bf16[320,1536]{1,0:T(8,128)(2,1)}, u32[]{:S(2)}, u32[]{:S(2)}) collective-permute-start(bf16[320,1536]{1,0:T(8,128)(2,1)} %pad_maximum_fusion.2.refs_10_), channel_id=1, source_target_pairs={{0,16},{4,20},{8,24},{12,28},{16,0},{20,4},{24,8},{28,12},{1,17},{... | collective-permute-start | bytes 2949128 | tf_op jit(solution)/shard_map/ppermute | solution.py:498
  45.6 23.7 %collective-permute-start.4 = (bf16[160,1536]{1,0:T(8,128)(2,1)}, bf16[160,1536]{1,0:T(8,128)(2,1)S(1)}, u32[]{:S(2)}, u32[]{:S(2)}) collective-permute-start(bf16[160,1536]{1,0:T(8,128)(2,1)} %get-tuple-element.30), channel_id=1, source_target_pairs={{0,2},{1,3},{2,0},{3,1},{4,6},{5,7},{6,4},{7,5},{8,10},{9,11},{10,... | collective-permute-start | bytes 1474568 | tf_op jit(solution)/shard_map/ppermute | solution.py:471
  51.1 22.5 %collective-permute-start.9 = (bf16[80,1536]{1,0:T(8,128)(2,1)}, bf16[80,1536]{1,0:T(8,128)(2,1)}, u32[]{:S(2)}, u32[]{:S(2)}) collective-permute-start(bf16[80,1536]{1,0:T(8,128)(2,1)} %slice.82), channel_id=1, source_target_pairs={{0,16},{4,20},{8,24},{12,28},{16,0},{20,4},{24,8},{28,12},{1,17},{... | collective-permute-start | bytes 737288 | tf_op jit(solution)/shard_map/ppermute | solution.py:498
  73.6 23.8 %collective-permute-start.18 = (bf16[160,1536]{1,0:T(8,128)(2,1)}, bf16[160,1536]{1,0:T(8,128)(2,1)S(1)}, u32[]{:S(2)}, u32[]{:S(2)}) collective-permute-start(bf16[160,1536]{1,0:T(8,128)(2,1)} %get-tuple-element.36), channel_id=1, source_target_pairs={{0,2},{1,3},{2,0},{3,1},{4,6},{5,7},{6,4},{7,5},{8,10},{9,11},{10,... | collective-permute-start | bytes 1474568 | tf_op jit(solution)/shard_map/ppermute | solution.py:471
  76.4 21.1 %collective-permute-start.11 = (bf16[160,1536]{1,0:T(8,128)(2,1)}, bf16[160,1536]{1,0:T(8,128)(2,1)S(1)}, u32[]{:S(2)}, u32[]{:S(2)}) collective-permute-start(bf16[160,1536]{1,0:T(8,128)(2,1)} %copy-done.7), channel_id=1, source_target_pairs={{0,8},{4,12},{8,0},{12,4},{16,24},{20,28},{24,16},{28,20},{1,9},{5... | collective-permute-start | bytes 1474568 | tf_op jit(solution)/shard_map/ppermute | solution.py:498
  77.8 20.4 %collective-permute-start.12 = (bf16[160,1536]{1,0:T(8,128)(2,1)}, bf16[160,1536]{1,0:T(8,128)(2,1)}, u32[]{:S(2)}, u32[]{:S(2)}) collective-permute-start(bf16[160,1536]{1,0:T(8,128)(2,1)} %copy-done.7), channel_id=1, source_target_pairs={{0,16},{4,20},{8,24},{12,28},{16,0},{20,4},{24,8},{28,12},{1,17},{... | collective-permute-start | bytes 1474568 | tf_op jit(solution)/shard_map/ppermute | solution.py:498
  80.4 19.7 %collective-permute-start.15 = (bf16[160,1536]{1,0:T(8,128)(2,1)S(1)}, bf16[160,1536]{1,0:T(8,128)(2,1)S(1)}, u32[]{:S(2)}, u32[]{:S(2)}) collective-permute-start(bf16[160,1536]{1,0:T(8,128)(2,1)S(1)} %slice.89), channel_id=1, source_target_pairs={{0,16},{4,20},{8,24},{12,28},{16,0},{20,4},{24,8},{28,12},{1,17},{... | collective-permute-start | bytes 1474568 | tf_op jit(solution)/shard_map/ppermute | solution.py:498
  82.1 18.1 %collective-permute-start.16 = (bf16[160,1536]{1,0:T(8,128)(2,1)S(1)}, bf16[160,1536]{1,0:T(8,128)(2,1)S(1)}, u32[]{:S(2)}, u32[]{:S(2)}) collective-permute-start(bf16[160,1536]{1,0:T(8,128)(2,1)S(1)} %slice.90), channel_id=1, source_target_pairs={{0,8},{4,12},{8,0},{12,4},{16,24},{20,28},{24,16},{28,20},{1,9},{5... | collective-permute-start | bytes 1474568 | tf_op jit(solution)/shard_map/ppermute | solution.py:498
  101.8 152.3 %all-gather.7.cloned.1.call-start = ((), (), s32[]{:S(2)}) async-start(), calls=%async_computation.1 | async-start | bytes 17694720 | tf_op jit(solution)/shard_map/all_gather | solution.py:547
  101.8 15.7 %collective-permute-start.17 = (bf16[160,1536]{1,0:T(8,128)(2,1)}, bf16[160,1536]{1,0:T(8,128)(2,1)S(1)}, u32[]{:S(2)}, u32[]{:S(2)}) collective-permute-start(bf16[160,1536]{1,0:T(8,128)(2,1)} %get-tuple-element.35), channel_id=1, source_target_pairs={{0,1},{1,2},{2,3},{3,0},{4,5},{5,6},{6,7},{7,4},{8,9},{9,10},{10,1... | collective-permute-start | bytes 1474568 | tf_op jit(solution)/shard_map/ppermute | solution.py:471
  125.5 18.4 %collective-permute-start.28 = (bf16[160,1536]{1,0:T(8,128)(2,1)S(1)}, bf16[160,1536]{1,0:T(8,128)(2,1)S(1)}, u32[]{:S(2)}, u32[]{:S(2)}) collective-permute-start(bf16[160,1536]{1,0:T(8,128)(2,1)S(1)} %copy-done.13), channel_id=1, source_target_pairs={{0,3},{1,0},{2,1},{3,2},{4,7},{5,4},{6,5},{7,6},{8,11},{9,8},{10,9... | collective-permute-start | bytes 1474568 | tf_op jit(solution)/shard_map/ppermute | solution.py:471
  145.4 173.9 %all-gather.9.cloned.1.call-start = ((), (), s32[]{:S(2)}) async-start(), calls=%async_computation.2 | async-start | bytes 11796480 | tf_op jit(solution)/shard_map/all_gather | solution.py:598
  146.1 16.8 %collective-permute-start.20 = (bf16[256,1024]{1,0:T(8,128)(2,1)S(1)}, bf16[256,1024]{1,0:T(8,128)(2,1)}, u32[]{:S(2)}, u32[]{:S(2)}) collective-permute-start(bf16[256,1024]{1,0:T(8,128)(2,1)S(1)} %bitcast.62), channel_id=1, source_target_pairs={{0,1},{1,2},{2,3},{3,0},{4,5},{5,6},{6,7},{7,4},{8,9},{9,10},{10,1... | collective-permute-start | bytes 1572872 | tf_op jit(solution)/shard_map/ppermute | solution.py:471
  146.2 27.0 %collective-permute-start.21 = (bf16[256,1024]{1,0:T(8,128)(2,1)S(1)}, bf16[256,1024]{1,0:T(8,128)(2,1)}, u32[]{:S(2)}, u32[]{:S(2)}) collective-permute-start(bf16[256,1024]{1,0:T(8,128)(2,1)S(1)} %bitcast.63), channel_id=1, source_target_pairs={{0,3},{1,0},{2,1},{3,2},{4,7},{5,4},{6,5},{7,6},{8,11},{9,8},{10,9... | collective-permute-start | bytes 1572872 | tf_op jit(solution)/shard_map/ppermute | solution.py:471
  173.9 16.5 %collective-permute-start.23 = (bf16[256,1024]{1,0:T(8,128)(2,1)}, bf16[256,1024]{1,0:T(8,128)(2,1)S(1)}, u32[]{:S(2)}, u32[]{:S(2)}) collective-permute-start(bf16[256,1024]{1,0:T(8,128)(2,1)} %collective-permute-done.21.refs_2_), channel_id=1, source_target_pairs={{1,0},{2,1},{5,4},{6,5},{9,8},{10,9},{13,12},{14,13},{17,16},{18,1... | collective-permute-start | bytes 1572872 | tf_op jit(solution)/shard_map/ppermute | solution.py:481
  193.7 19.5 %collective-permute-start.24 = (bf16[256,1280]{1,0:T(8,128)(2,1)S(1)}, bf16[256,1280]{1,0:T(8,128)(2,1)S(1)}, u32[]{:S(2)}, u32[]{:S(2)}) collective-permute-start(bf16[256,1280]{1,0:T(8,128)(2,1)S(1)} %shard_map.107.refs_0_.refs_5_), channel_id=1, source_target_pairs={{0,1},{1,2},{2,3},{3,0},{4,5},{5,6},{6,7},{7,4},{8,9},{9,10},{10,1... | collective-permute-start | bytes 1966088 | tf_op jit(solution)/shard_map/ppermute | solution.py:471
  195.5 28.6 %collective-permute-start.26 = (bf16[256,1280]{1,0:T(8,128)(2,1)S(1)}, bf16[256,1280]{1,0:T(8,128)(2,1)S(1)}, u32[]{:S(2)}, u32[]{:S(2)}) collective-permute-start(bf16[256,1280]{1,0:T(8,128)(2,1)S(1)} %shard_map.107.refs_0_.refs_5_), channel_id=1, source_target_pairs={{0,3},{1,0},{2,1},{3,2},{4,7},{5,4},{6,5},{7,6},{8,11},{9,8},{10,9... | collective-permute-start | bytes 1966088 | tf_op jit(solution)/shard_map/ppermute | solution.py:471
  224.1 18.0 %collective-permute-start.27 = (bf16[256,1280]{1,0:T(8,128)(2,1)S(1)}, bf16[256,1280]{1,0:T(8,128)(2,1)}, u32[]{:S(2)}, u32[]{:S(2)}) collective-permute-start(bf16[256,1280]{1,0:T(8,128)(2,1)S(1)} %collective-permute-done.26.refs_3_), channel_id=1, source_target_pairs={{1,0},{2,1},{5,4},{6,5},{9,8},{10,9},{13,12},{14,13},{17,16},{18,1... | collective-permute-start | bytes 1966088 | tf_op jit(solution)/shard_map/ppermute | solution.py:481
  277.4 16.7 %collective-permute-start.29 = (bf16[256,1024]{1,0:T(8,128)(2,1)S(1)}, bf16[256,1024]{1,0:T(8,128)(2,1)S(1)}, u32[]{:S(2)}, u32[]{:S(2)}) collective-permute-start(bf16[256,1024]{1,0:T(8,128)(2,1)S(1)} %bitcast.59), channel_id=1, source_target_pairs={{0,1},{1,2},{2,3},{3,0},{4,5},{5,6},{6,7},{7,4},{8,9},{9,10},{10,1... | collective-permute-start | bytes 1572872 | tf_op jit(solution)/shard_map/ppermute | solution.py:471
  278.8 25.1 %collective-permute-start.31 = (bf16[256,1024]{1,0:T(8,128)(2,1)S(1)}, bf16[256,1024]{1,0:T(8,128)(2,1)S(1)}, u32[]{:S(2)}, u32[]{:S(2)}) collective-permute-start(bf16[256,1024]{1,0:T(8,128)(2,1)S(1)} %bitcast.60), channel_id=1, source_target_pairs={{0,3},{1,0},{2,1},{3,2},{4,7},{5,4},{6,5},{7,6},{8,11},{9,8},{10,9... | collective-permute-start | bytes 1572872 | tf_op jit(solution)/shard_map/ppermute | solution.py:471
  303.9 15.3 %collective-permute-start.32 = (bf16[256,1024]{1,0:T(8,128)(2,1)S(1)}, bf16[256,1024]{1,0:T(8,128)(2,1)S(1)}, u32[]{:S(2)}, u32[]{:S(2)}) collective-permute-start(bf16[256,1024]{1,0:T(8,128)(2,1)S(1)} %collective-permute-done.31.refs_3_), channel_id=1, source_target_pairs={{1,0},{2,1},{5,4},{6,5},{9,8},{10,9},{13,12},{14,13},{17,16},{18,1... | collective-permute-start | bytes 1572872 | tf_op jit(solution)/shard_map/ppermute | solution.py:481
  325.6 19.5 %collective-permute-start.33 = (bf16[256,1280]{1,0:T(8,128)(2,1)S(1)}, bf16[256,1280]{1,0:T(8,128)(2,1)S(1)}, u32[]{:S(2)}, u32[]{:S(2)}) collective-permute-start(bf16[256,1280]{1,0:T(8,128)(2,1)S(1)} %shard_map.110.refs_0_), channel_id=1, source_target_pairs={{0,1},{1,2},{2,3},{3,0},{4,5},{5,6},{6,7},{7,4},{8,9},{9,10},{10,1... | collective-permute-start | bytes 1966088 | tf_op jit(solution)/shard_map/ppermute | solution.py:471
  327.4 30.4 %collective-permute-start.35 = (bf16[256,1280]{1,0:T(8,128)(2,1)S(1)}, bf16[256,1280]{1,0:T(8,128)(2,1)S(1)}, u32[]{:S(2)}, u32[]{:S(2)}) collective-permute-start(bf16[256,1280]{1,0:T(8,128)(2,1)S(1)} %shard_map.110.refs_0_), channel_id=1, source_target_pairs={{0,3},{1,0},{2,1},{3,2},{4,7},{5,4},{6,5},{7,6},{8,11},{9,8},{10,9... | collective-permute-start | bytes 1966088 | tf_op jit(solution)/shard_map/ppermute | solution.py:471
  357.8 17.9 %collective-permute-start.36 = (bf16[256,1280]{1,0:T(8,128)(2,1)S(1)}, bf16[256,1280]{1,0:T(8,128)(2,1)S(1)}, u32[]{:S(2)}, u32[]{:S(2)}) collective-permute-start(bf16[256,1280]{1,0:T(8,128)(2,1)S(1)} %collective-permute-done.35.refs_3_), channel_id=1, source_target_pairs={{1,0},{2,1},{5,4},{6,5},{9,8},{10,9},{13,12},{14,13},{17,16},{18,1... | collective-permute-start | bytes 1966088 | tf_op jit(solution)/shard_map/ppermute | solution.py:481
  (29 other events, 300.3 us)
Sparse Core Ops, SparseCore 0:
  101.9 64.7 all-gather.4
  168.6 85.4 all-gather.6
  256.0 63.2 all-gather.8

commit v3 on v2

--- a/solution.py
+++ b/solution.py
@@ -563,7 +563,8 @@
         mine, theirs, squares = share_features(
             flat, jnp.full((1,), core, jnp.int32), replicas // 2
         )
-        both = jnp.concatenate([mine, swapped(theirs, 1)], axis=0)
+        swapped_share = swapped(theirs, 1)
+        both = jnp.concatenate([mine, swapped_share], axis=0)
         both = split_parts(both, source, parts, replicas // 2, piece)
         both = [both[shift] for shift in range(parts)]
         other = swapped(squares.reshape(-1, 128), 1).reshape(flat_rows, 1)
@@ -572,7 +573,7 @@
             gains[0].reshape(parts, replicas // 2, 2, piece), core, 2, keepdims=False
         ).reshape(parts, 1, slice_width // 2)
         one, three = shifted(outgoing(0, 1), 1), shifted(outgoing(0, 3), 3)
-        two = shifted(after(outgoing(0, 2), one, three), 2)
+        two = shifted(after(outgoing(0, 2), one, three, swapped_share), 2)
         head = spread_first(outgoing(0, 0))
         body = spread_first(
             jnp.concatenate([one, three], axis=0), head[1][2], head[2][2]
@@ -583,15 +584,14 @@
         ahead = [array for _, _, array in body[1:3]]
         across = [array for _, _, array in tail[1:3]]
         body = spread_second(body)
-        turned += [array for _, _, array in body[3:5]]
         tail = spread_second(tail)
         gathers = [[listed([head, body], [[0], [1, 2]]), listed([tail], [[0]])]]
-        later_two = shifted(after(outgoing(1, 2), two), 2)
-        later_one = shifted(after(outgoing(1, 1), *across), 1)
-        later_three = shifted(after(outgoing(1, 3), later_one), 3)
+        later_one = shifted(after(outgoing(1, 1), two), 1)
+        later_two = shifted(after(outgoing(1, 2), *across), 2)
+        later_three = shifted(after(outgoing(1, 3), later_two), 3)
         came = (outgoing(1, 0), later_one, later_two, later_three)
         ready = (scale, core_gains, gathers[0][0][2], gathers[0][1][2], *both)
-        sent = [after(out_weight[0], *across, *turned, later_two, *ready), out_weight[1]]
+        sent = [after(out_weight[0], *across, *turned, later_one, *ready), out_weight[1]]
     else:
         gathers = [from_calls(layer) for layer in range(layers)]
         sent = [out_weight[layer] for layer in range(layers)]

time: 387 us -> 383 us (0.990)
  starting transfers between devices: 51.9 us -> 46.2 us
  waiting for transfers between devices: 211 us -> 206 us
    ppermute x15, waiting for transfers between devices: 2.68 us -> 41.6 us  [swapped(): return lax.ppermute(block, 'rep', [(i, i ^ mask) for i in range(replicas)])]
    ppermute x14, waiting for transfers between devices: 142 us -> 109 us  [shifted(): lax.ppermute(block, 'tp', [(i, (i + shift) % parts) for i in range(parts)])]
    all_gather x1, waiting for transfers between devices: 10.9 us -> 0.02 us  [from_call(): array = lax.all_gather(came, 'rep', axis=0, tiled=True)]
    ppermute x14, starting transfers between devices: 28 us -> 23.1 us  [shifted(): lax.ppermute(block, 'tp', [(i, (i + shift) % parts) for i in range(parts)])]
    unnamed x42 -> x48, local copies, waits for them, and re-layouts: 6.37 us -> 9.59 us
  transfers between devices with their start and end apart: 40 -> 40, of which waited for: 20 -> 21; matrix products, arithmetic and copies ran while one was open for 6% -> 6% of each run, Pallas kernels for 18% -> 18%
where the time goes in v3:
time: 383 us; the launch traced here: 381 us
  waiting for transfers between devices  206 us (54%)
  Pallas kernels  78.8 us (21%)
  starting transfers between devices  46.2 us (12%)
  local copies, waits for them, and re-layouts  27.8 us (7%)
  between operations  13.8 us (4%)
  other arithmetic  8.78 us (2%)
    ppermute x14, waiting for transfers between devices, shifted(): lax.ppermute(block, 'tp', [(i, (i + shift) % parts) for i in range(parts)])  109 us
    ppermute x4, waiting for transfers between devices, all_parts(): leftwards = lax.ppermute(from_right, 'tp', [(1, 0), (2, 1)])  54.9 us
    ppermute x15, waiting for transfers between devices, swapped(): return lax.ppermute(block, 'rep', [(i, i ^ mask) for i in range(replicas)])  41.6 us
    pallas_call x3, Pallas kernels, project_qkv(): pl.pallas_call(functools.partial(qkv_kernel, count, shifts, pieces, len(w...  29.3 us
    pallas_call x2, Pallas kernels, attend(): pl.pallas_call(functools.partial(attention_kernel, heads), out_shape=jax....  25.3 us
    ppermute x14, starting transfers between devices, shifted(): lax.ppermute(block, 'tp', [(i, (i + shift) % parts) for i in range(parts)])  23.1 us
    ppermute x15, starting transfers between devices, swapped(): return lax.ppermute(block, 'rep', [(i, i ^ mask) for i in range(replicas)])  14.9 us
    pallas_call x2, Pallas kernels, project_out(): pl.pallas_call(functools.partial(out_kernel, count, shifts), out_shape=ja...  9.75 us
  transfers between devices with their start and end apart: 40, of which 21 were waited for; matrix products, arithmetic and copies ran while one was open for 6% of the time, Pallas kernels for 18%

profile of v3, /device:TPU:0, one launch (start us, length us, event | category | flops | bytes accessed | tf_op | source)
XLA Modules:
  0.0 381.4 jit_solution(7512301725804178305)
XLA Ops:
  6.5 4.1 %dynamic-slice_bitcast_fusion = (bf16[160,1536]{1,0:T(8,128)(2,1)}, bf16[160,1536]{1,0:T(8,128)(2,1)}, bf16[160,1536]{1,0:T(8,128)(2,1)}, bf16[160,1536]{1,0:T(8...) fusion(bf16[2,160,6144]{2,1,0:T(8,128)(2,1)} %param.11, ...), kind=kLoop, calls=%fused_computation.14 | loop fusion | bytes 7864336 | tf_op jit(solution)/shard_map/squeeze | solution.py:486
  10.6 2.9 collective-permute-start.5
  23.6 10.3 %collective-permute-done.2 = bf16[160,1536]{1,0:T(8,128)(2,1)} collective-permute-done((bf16[160,1536]{1,0:T(8,128)(2,1)}, bf16[160,1536]{1,0:T(8,128)(2,1)}, u32[]{:S(2)}, u32[]{:S(2)}) %collective-permute-start.2) | collective-permute-done | bytes 491552 | tf_op jit(solution)/shard_map/ppermute | solution.py:471
  33.9 9.6 %collective-permute-done.3 = bf16[160,1536]{1,0:T(8,128)(2,1)} collective-permute-done((bf16[160,1536]{1,0:T(8,128)(2,1)}, bf16[160,1536]{1,0:T(8,128)(2,1)}, u32[]{:S(2)}, u32[]{:S(2)}) %collective-permute-start.3) | collective-permute-done | bytes 491552 | tf_op jit(solution)/shard_map/ppermute | solution.py:471
  57.5 17.1 %collective-permute-done.9.refs_8_ = bf16[80,1536]{1,0:T(8,128)(2,1)S(1)} collective-permute-done((bf16[80,1536]{1,0:T(8,128)(2,1)}, bf16[80,1536]{1,0:T(8,128)(2,1)S(1)}, u32[]{:S(2)}, u32[]{:S(2)}) %collective-permute-start.9) | collective-permute-done | bytes 245792 | tf_op jit(solution)/shard_map/ppermute | solution.py:498
  83.9 3.2 collective-permute-done.11.refs_4_
  99.6 11.9 %collective-permute-done.15.refs_13_ = bf16[160,1536]{1,0:T(8,128)(2,1)S(1)} collective-permute-done((bf16[160,1536]{1,0:T(8,128)(2,1)S(1)}, bf16[160,1536]{1,0:T(8,128)(2,1)S(1)}, u32[]{:S(2)}, u32[]{:S(2)}) %collective-permute-start.15) | collective-permute-done | bytes 491552 | tf_op jit(solution)/shard_map/ppermute | solution.py:498
  111.5 5.3 %collective-permute-done.16.refs_14_ = bf16[160,1536]{1,0:T(8,128)(2,1)S(1)} collective-permute-done((bf16[160,1536]{1,0:T(8,128)(2,1)S(1)}, bf16[160,1536]{1,0:T(8,128)(2,1)S(1)}, u32[]{:S(2)}, u32[]{:S(2)}) %collective-permute-start.16) | collective-permute-done | bytes 491552 | tf_op jit(solution)/shard_map/ppermute | solution.py:498
  117.7 9.5 %shard_map.102 = (f32[256,1536]{1,0:T(8,128)}, f32[256,1536]{1,0:T(8,128)}) custom-call(s32[13]{0:T(128)S(1)} %stack.40.rows_ref, bf16[512,640]{1,0:T(8,128)(2,1)} %get-tuple-element.61.refs_0_, bf16[512,640]{1,0:T(8,128)(2,1)} %get-tuple-element.60.refs_1_, bf16[512,640]{1,0:T(8,128)(2,1)} %get-tuple-element.59.refs_2_, ...), custom_call_target="tpu_custom_call" | custom-call | flops 3019898880 | bytes 5898240 | tf_op jit(solution)/shard_map/pallas_call | solution.py:187
  127.3 8.1 %shard_map.103 = (f32[256,1536]{1,0:T(8,128)}, f32[256,1536]{1,0:T(8,128)}) custom-call(s32[5]{0:T(128)S(1)} %stack.19.rows_ref, bf16[512,640]{1,0:T(8,128)(2,1)} %get-tuple-element.62.refs_0_, f32[4,1,640]{2,1,0:T(1,128)S(1)} %reshape.165.refs_3_.refs_1_, f32[512,1]{1,0:T(8,128)S(1)} %rsqrt.3.refs_4_.refs_2_, ...), custom_call_target="tpu_custom_call" | custom-call | flops 1006632960 | bytes 1966080 | tf_op jit(solution)/shard_map/pallas_call | solution.py:187
  140.5 12.8 %shard_map.104 = bf16[4,64,1024]{2,1,0:T(8,128)(2,1)S(1)} custom-call(s32[64]{0:T(128)S(1)} %copy-done.12, f32[4,64,1536]{2,1,0:T(8,128)S(1)} %bitcast.65, f32[4,64,1536]{2,1,0:T(8,128)S(1)} %bitcast.66, f32[4,64,128]{2,1,0:T(8,128)S(1)} %get-tuple-element.72.refs_2_.refs_1_, f32[4,64,128]{2,1,0:T(8,128)S(1)} %get-tuple-element.73.refs_3_.refs_2_, ...), custom_call_target="tpu_custom_call" | custom-call | flops 268435456 | bytes 16777216 | tf_op jit(solution)/shard_map/pallas_call | solution.py:413
  156.6 3.8 collective-permute-start.21
  163.3 10.0 %collective-permute-done.20.refs_1_ = bf16[256,1024]{1,0:T(8,128)(2,1)} collective-permute-done((bf16[256,1024]{1,0:T(8,128)(2,1)S(1)}, bf16[256,1024]{1,0:T(8,128)(2,1)}, u32[]{:S(2)}, u32[]{:S(2)}) %collective-permute-start.20) | collective-permute-done | bytes 524320 | tf_op jit(solution)/shard_map/ppermute | solution.py:471
  173.3 8.6 %collective-permute-done.21.refs_2_ = bf16[256,1024]{1,0:T(8,128)(2,1)} collective-permute-done((bf16[256,1024]{1,0:T(8,128)(2,1)S(1)}, bf16[256,1024]{1,0:T(8,128)(2,1)}, u32[]{:S(2)}, u32[]{:S(2)}) %collective-permute-start.21) | collective-permute-done | bytes 524320 | tf_op jit(solution)/shard_map/ppermute | solution.py:471
  185.2 5.9 %shard_map.105.refs_2_ = f32[256,1280]{1,0:T(8,128)S(1)} custom-call(s32[4]{0:T(128)S(1)} %broadcast_multiply_fusion.column_ref, bf16[256,1024]{1,0:T(8,128)(2,1)S(1)} %bitcast.64, bf16[256,1024]{1,0:T(8,128)(2,1)} %collective-permute-done.20.refs_1_, bf16[256,1024]{1,0:T(8,128)(2,1)} %collective-permute-done.21.refs_2_, ...), custom_call_target="tpu_custom_call" | custom-call | flops 2013265920 | bytes 7864320 | tf_op jit(solution)/shard_map/pallas_call | solution.py:311
  191.1 8.8 %collective-permute-done.23 = bf16[256,1024]{1,0:T(8,128)(2,1)S(1)} collective-permute-done((bf16[256,1024]{1,0:T(8,128)(2,1)}, bf16[256,1024]{1,0:T(8,128)(2,1)S(1)}, u32[]{:S(2)}, u32[]{:S(2)}) %collective-permute-start.23) | collective-permute-done | bytes 524320 | tf_op jit(solution)/shard_map/ppermute | solution.py:481
  200.1 3.9 %shard_map.107.refs_0_.refs_5_ = bf16[256,1280]{1,0:T(8,128)(2,1)S(1)} custom-call(s32[4]{0:T(128)S(1)} %broadcast_multiply_fusion.column_ref, bf16[256,1024]{1,0:T(8,128)(2,1)S(1)} %broadcast_select_fusion.3.refs_0_, bf16[1280,4096]{1,0:T(8,128)(2,1)} %all-gather.5.cloned.1.call-done.refs_3_.refs_1_, f32[256,1280]{1,0:T(8,128)S(1)} %shard_map.105.refs_2_, ...), custom_call_target="tpu_custom_call" | custom-call | flops 671088640 | bytes 2621440 | tf_op jit(solution)/shard_map/pallas_call | solution.py:311
  207.8 15.7 %collective-permute-done.24.refs_1_ = bf16[256,1280]{1,0:T(8,128)(2,1)S(1)} collective-permute-done((bf16[256,1280]{1,0:T(8,128)(2,1)S(1)}, bf16[256,1280]{1,0:T(8,128)(2,1)S(1)}, u32[]{:S(2)}, u32[]{:S(2)}) %collective-permute-start.24) | collective-permute-done | bytes 655392 | tf_op jit(solution)/shard_map/ppermute | solution.py:471
  225.0 8.5 %collective-permute-done.26.refs_3_ = bf16[256,1280]{1,0:T(8,128)(2,1)S(1)} collective-permute-done((bf16[256,1280]{1,0:T(8,128)(2,1)S(1)}, bf16[256,1280]{1,0:T(8,128)(2,1)S(1)}, u32[]{:S(2)}, u32[]{:S(2)}) %collective-permute-start.26) | collective-permute-done | bytes 655392 | tf_op jit(solution)/shard_map/ppermute | solution.py:471
  234.9 16.6 %collective-permute-done.27 = bf16[256,1280]{1,0:T(8,128)(2,1)} collective-permute-done((bf16[256,1280]{1,0:T(8,128)(2,1)S(1)}, bf16[256,1280]{1,0:T(8,128)(2,1)}, u32[]{:S(2)}, u32[]{:S(2)}) %collective-permute-start.27) | collective-permute-done | bytes 655392 | tf_op jit(solution)/shard_map/ppermute | solution.py:481
  254.9 11.6 %shard_map.108 = f32[256,1536]{1,0:T(8,128)S(1)} custom-call(s32[32]{0:T(128)S(1)} %copy-done.13, bf16[256,1280]{1,0:T(8,128)(2,1)S(1)} %shard_map.107.refs_0_.refs_5_, bf16[256,1280]{1,0:T(8,128)(2,1)S(1)} %copy-done.5, bf16[256,1280]{1,0:T(8,128)(2,1)S(1)} %broadcast_select_fusion.1.refs_2_, bf16[256,1280]{1,0:T(8,128)(2,1)S(1)} %copy-done.7, ...), custom_call_target="tpu_custom_call" | custom-call | flops 4026531840 | bytes 15728640 | tf_op jit(solution)/shard_map/pallas_call | solution.py:187
  266.6 12.6 %shard_map.109 = bf16[4,64,1024]{2,1,0:T(8,128)(2,1)S(1)} custom-call(s32[64]{0:T(128)S(1)} %copy-done.12, f32[4,64,1536]{2,1,0:T(8,128)S(1)} %bitcast.58, f32[4,64,128]{2,1,0:T(8,128)S(1)} %get-tuple-element.72.refs_2_.refs_1_, f32[4,64,128]{2,1,0:T(8,128)S(1)} %get-tuple-element.73.refs_3_.refs_2_, f32[1,128]{1,0:T(1,128)S(1)} %get-tuple-element.75.refs_3_, ...), custom_call_target="tpu_custom_call" | custom-call | flops 268435456 | bytes 16777216 | tf_op jit(solution)/shard_map/pallas_call | solution.py:413
  279.2 3.8 collective-permute-start.31
  283.0 12.8 %collective-permute-done.29.refs_1_ = bf16[256,1024]{1,0:T(8,128)(2,1)S(1)} collective-permute-done((bf16[256,1024]{1,0:T(8,128)(2,1)S(1)}, bf16[256,1024]{1,0:T(8,128)(2,1)S(1)}, u32[]{:S(2)}, u32[]{:S(2)}) %collective-permute-start.29) | collective-permute-done | bytes 524320 | tf_op jit(solution)/shard_map/ppermute | solution.py:471
  296.6 5.8 %collective-permute-done.31.refs_3_ = bf16[256,1024]{1,0:T(8,128)(2,1)S(1)} collective-permute-done((bf16[256,1024]{1,0:T(8,128)(2,1)S(1)}, bf16[256,1024]{1,0:T(8,128)(2,1)S(1)}, u32[]{:S(2)}, u32[]{:S(2)}) %collective-permute-start.31) | collective-permute-done | bytes 524320 | tf_op jit(solution)/shard_map/ppermute | solution.py:471
  303.7 12.7 %collective-permute-done.32 = bf16[256,1024]{1,0:T(8,128)(2,1)S(1)} collective-permute-done((bf16[256,1024]{1,0:T(8,128)(2,1)S(1)}, bf16[256,1024]{1,0:T(8,128)(2,1)S(1)}, u32[]{:S(2)}, u32[]{:S(2)}) %collective-permute-start.32) | collective-permute-done | bytes 524320 | tf_op jit(solution)/shard_map/ppermute | solution.py:481
  317.5 6.2 %shard_map.110.refs_0_ = bf16[256,1280]{1,0:T(8,128)(2,1)S(1)} custom-call(s32[4]{0:T(128)S(1)} %broadcast_multiply_fusion.column_ref, bf16[256,1024]{1,0:T(8,128)(2,1)S(1)} %bitcast.61, bf16[256,1024]{1,0:T(8,128)(2,1)S(1)} %collective-permute-done.29.refs_1_, bf16[256,1024]{1,0:T(8,128)(2,1)S(1)} %broadcast_select_fusion.2.refs_2_, ...), custom_call_target="tpu_custom_call" | custom-call | flops 2684354560 | bytes 10485760 | tf_op jit(solution)/shard_map/pallas_call | solution.py:245
  323.8 3.8 collective-permute-start.35
  327.6 15.6 %collective-permute-done.33.refs_1_ = bf16[256,1280]{1,0:T(8,128)(2,1)S(1)} collective-permute-done((bf16[256,1280]{1,0:T(8,128)(2,1)S(1)}, bf16[256,1280]{1,0:T(8,128)(2,1)S(1)}, u32[]{:S(2)}, u32[]{:S(2)}) %collective-permute-start.33) | collective-permute-done | bytes 655392 | tf_op jit(solution)/shard_map/ppermute | solution.py:471
  344.0 9.0 %collective-permute-done.35.refs_3_ = bf16[256,1280]{1,0:T(8,128)(2,1)S(1)} collective-permute-done((bf16[256,1280]{1,0:T(8,128)(2,1)S(1)}, bf16[256,1280]{1,0:T(8,128)(2,1)S(1)}, u32[]{:S(2)}, u32[]{:S(2)}) %collective-permute-start.35) | collective-permute-done | bytes 655392 | tf_op jit(solution)/shard_map/ppermute | solution.py:471
  354.2 16.7 %collective-permute-done.36 = bf16[256,1280]{1,0:T(8,128)(2,1)S(1)} collective-permute-done((bf16[256,1280]{1,0:T(8,128)(2,1)S(1)}, bf16[256,1280]{1,0:T(8,128)(2,1)S(1)}, u32[]{:S(2)}, u32[]{:S(2)}) %collective-permute-start.36) | collective-permute-done | bytes 655392 | tf_op jit(solution)/shard_map/ppermute | solution.py:481
  371.1 3.8 shard_map.111
  (154 shorter events, 76.4 us)
Async XLA Ops:
  6.5 175.4 %all-gather.5.cloned.1.call-start = ((), (), s32[]{:S(2)}) async-start(), calls=%async_computation | async-start | bytes 11796480 | tf_op jit(solution)/shard_map/all_gather | solution.py:598
  10.6 35.1 %collective-permute-start.5 = (bf16[160,1536]{1,0:T(8,128)(2,1)S(1)}, bf16[160,1536]{1,0:T(8,128)(2,1)}, u32[]{:S(2)}, u32[]{:S(2)}) collective-permute-start(bf16[160,1536]{1,0:T(8,128)(2,1)S(1)} %get-tuple-element.52.refs_5_), channel_id=1, source_target_pairs={{0,8},{4,12},{8,0},{12,4},{16,24},{20,28},{24,16},{28,20},{1,9},{5... | collective-permute-start | bytes 1474568 | tf_op jit(solution)/shard_map/ppermute | solution.py:498
  13.6 32.1 %collective-permute-start.6 = (bf16[160,1536]{1,0:T(8,128)(2,1)S(1)}, bf16[160,1536]{1,0:T(8,128)(2,1)}, u32[]{:S(2)}, u32[]{:S(2)}) collective-permute-start(bf16[160,1536]{1,0:T(8,128)(2,1)S(1)} %get-tuple-element.52.refs_5_), channel_id=1, source_target_pairs={{0,16},{4,20},{8,24},{12,28},{16,0},{20,4},{24,8},{28,12},{1,17},{... | collective-permute-start | bytes 1474568 | tf_op jit(solution)/shard_map/ppermute | solution.py:498
  17.7 29.6 %collective-permute-start = (bf16[256,2560]{1,0:T(8,128)(2,1)}, bf16[256,2560]{1,0:T(8,128)(2,1)}, u32[]{:S(2)}, u32[]{:S(2)}) collective-permute-start(bf16[256,2560]{1,0:T(8,128)(2,1)} %get-tuple-element.28), channel_id=1, source_target_pairs={{0,4},{4,0},{8,12},{12,8},{16,20},{20,16},{24,28},{28,24},{1,5},{5... | collective-permute-start | bytes 3932168 | tf_op jit(solution)/shard_map/ppermute | solution.py:498
  17.7 16.2 %collective-permute-start.2 = (bf16[160,1536]{1,0:T(8,128)(2,1)}, bf16[160,1536]{1,0:T(8,128)(2,1)}, u32[]{:S(2)}, u32[]{:S(2)}) collective-permute-start(bf16[160,1536]{1,0:T(8,128)(2,1)} %get-tuple-element.54), channel_id=1, source_target_pairs={{0,1},{1,2},{2,3},{3,0},{4,5},{5,6},{6,7},{7,4},{8,9},{9,10},{10,1... | collective-permute-start | bytes 1474568 | tf_op jit(solution)/shard_map/ppermute | solution.py:471
  19.3 24.2 %collective-permute-start.3 = (bf16[160,1536]{1,0:T(8,128)(2,1)}, bf16[160,1536]{1,0:T(8,128)(2,1)}, u32[]{:S(2)}, u32[]{:S(2)}) collective-permute-start(bf16[160,1536]{1,0:T(8,128)(2,1)} %get-tuple-element.53), channel_id=1, source_target_pairs={{0,3},{1,0},{2,1},{3,2},{4,7},{5,4},{6,5},{7,6},{8,11},{9,8},{10,9... | collective-permute-start | bytes 1474568 | tf_op jit(solution)/shard_map/ppermute | solution.py:471
  33.9 19.8 %collective-permute-start.1 = (f32[2,128]{1,0:T(2,128)S(1)}, f32[2,128]{1,0:T(2,128)S(1)}, u32[]{:S(2)}, u32[]{:S(2)}) collective-permute-start(f32[2,128]{1,0:T(2,128)S(1)} %bitcast.68), channel_id=1, source_target_pairs={{0,4},{4,0},{8,12},{12,8},{16,20},{20,16},{24,28},{28,24},{1,5},{5... | collective-permute-start | bytes 3080 | tf_op jit(solution)/shard_map/ppermute | solution.py:498
  45.7 29.6 %collective-permute-start.7 = (bf16[320,1536]{1,0:T(8,128)(2,1)}, bf16[320,1536]{1,0:T(8,128)(2,1)}, u32[]{:S(2)}, u32[]{:S(2)}) collective-permute-start(bf16[320,1536]{1,0:T(8,128)(2,1)} %pad_maximum_fusion.2.refs_10_), channel_id=1, source_target_pairs={{0,8},{4,12},{8,0},{12,4},{16,24},{20,28},{24,16},{28,20},{1,9},{5... | collective-permute-start | bytes 2949128 | tf_op jit(solution)/shard_map/ppermute | solution.py:498
  46.2 29.1 %collective-permute-start.8 = (bf16[320,1536]{1,0:T(8,128)(2,1)}, bf16[320,1536]{1,0:T(8,128)(2,1)}, u32[]{:S(2)}, u32[]{:S(2)}) collective-permute-start(bf16[320,1536]{1,0:T(8,128)(2,1)} %pad_maximum_fusion.2.refs_10_), channel_id=1, source_target_pairs={{0,16},{4,20},{8,24},{12,28},{16,0},{20,4},{24,8},{28,12},{1,17},{... | collective-permute-start | bytes 2949128 | tf_op jit(solution)/shard_map/ppermute | solution.py:498
  47.4 27.9 %collective-permute-start.4 = (bf16[160,1536]{1,0:T(8,128)(2,1)}, bf16[160,1536]{1,0:T(8,128)(2,1)}, u32[]{:S(2)}, u32[]{:S(2)}) collective-permute-start(bf16[160,1536]{1,0:T(8,128)(2,1)} %get-tuple-element.30), channel_id=1, source_target_pairs={{0,2},{1,3},{2,0},{3,1},{4,6},{5,7},{6,4},{7,5},{8,10},{9,11},{10,... | collective-permute-start | bytes 1474568 | tf_op jit(solution)/shard_map/ppermute | solution.py:471
  50.5 24.1 %collective-permute-start.9 = (bf16[80,1536]{1,0:T(8,128)(2,1)}, bf16[80,1536]{1,0:T(8,128)(2,1)S(1)}, u32[]{:S(2)}, u32[]{:S(2)}) collective-permute-start(bf16[80,1536]{1,0:T(8,128)(2,1)} %slice.82), channel_id=1, source_target_pairs={{0,16},{4,20},{8,24},{12,28},{16,0},{20,4},{24,8},{28,12},{1,17},{... | collective-permute-start | bytes 737288 | tf_op jit(solution)/shard_map/ppermute | solution.py:498
  53.7 21.6 %collective-permute-start.10 = (bf16[80,1536]{1,0:T(8,128)(2,1)}, bf16[80,1536]{1,0:T(8,128)(2,1)}, u32[]{:S(2)}, u32[]{:S(2)}) collective-permute-start(bf16[80,1536]{1,0:T(8,128)(2,1)} %slice.83), channel_id=1, source_target_pairs={{0,8},{4,12},{8,0},{12,4},{16,24},{20,28},{24,16},{28,20},{1,9},{5... | collective-permute-start | bytes 737288 | tf_op jit(solution)/shard_map/ppermute | solution.py:498
  91.3 161.5 %all-gather.7.cloned.1.call-start = ((), (), s32[]{:S(2)}) async-start(), calls=%async_computation.1 | async-start | bytes 17694720 | tf_op jit(solution)/shard_map/all_gather | solution.py:547
  92.5 19.1 %collective-permute-start.15 = (bf16[160,1536]{1,0:T(8,128)(2,1)S(1)}, bf16[160,1536]{1,0:T(8,128)(2,1)S(1)}, u32[]{:S(2)}, u32[]{:S(2)}) collective-permute-start(bf16[160,1536]{1,0:T(8,128)(2,1)S(1)} %slice.89), channel_id=1, source_target_pairs={{0,16},{4,20},{8,24},{12,28},{16,0},{20,4},{24,8},{28,12},{1,17},{... | collective-permute-start | bytes 1474568 | tf_op jit(solution)/shard_map/ppermute | solution.py:498
  95.1 21.7 %collective-permute-start.16 = (bf16[160,1536]{1,0:T(8,128)(2,1)S(1)}, bf16[160,1536]{1,0:T(8,128)(2,1)S(1)}, u32[]{:S(2)}, u32[]{:S(2)}) collective-permute-start(bf16[160,1536]{1,0:T(8,128)(2,1)S(1)} %slice.90), channel_id=1, source_target_pairs={{0,8},{4,12},{8,0},{12,4},{16,24},{20,28},{24,16},{28,20},{1,9},{5... | collective-permute-start | bytes 1474568 | tf_op jit(solution)/shard_map/ppermute | solution.py:498
  95.8 31.4 %collective-permute-start.18 = (bf16[160,1536]{1,0:T(8,128)(2,1)}, bf16[160,1536]{1,0:T(8,128)(2,1)S(1)}, u32[]{:S(2)}, u32[]{:S(2)}) collective-permute-start(bf16[160,1536]{1,0:T(8,128)(2,1)} %get-tuple-element.36), channel_id=1, source_target_pairs={{0,2},{1,3},{2,0},{3,1},{4,6},{5,7},{6,4},{7,5},{8,10},{9,11},{10,... | collective-permute-start | bytes 1474568 | tf_op jit(solution)/shard_map/ppermute | solution.py:471
  96.6 30.7 %collective-permute-start.13 = (bf16[80,1536]{1,0:T(8,128)(2,1)S(1)}, bf16[80,1536]{1,0:T(8,128)(2,1)S(1)}, u32[]{:S(2)}, u32[]{:S(2)}) collective-permute-start(bf16[80,1536]{1,0:T(8,128)(2,1)S(1)} %slice.84), channel_id=1, source_target_pairs={{0,16},{4,20},{8,24},{12,28},{16,0},{20,4},{24,8},{28,12},{1,17},{... | collective-permute-start | bytes 737288 | tf_op jit(solution)/shard_map/ppermute | solution.py:498
  98.2 29.1 %collective-permute-start.14 = (bf16[80,1536]{1,0:T(8,128)(2,1)S(1)}, bf16[80,1536]{1,0:T(8,128)(2,1)S(1)}, u32[]{:S(2)}, u32[]{:S(2)}) collective-permute-start(bf16[80,1536]{1,0:T(8,128)(2,1)S(1)} %slice.85), channel_id=1, source_target_pairs={{0,8},{4,12},{8,0},{12,4},{16,24},{20,28},{24,16},{28,20},{1,9},{5... | collective-permute-start | bytes 737288 | tf_op jit(solution)/shard_map/ppermute | solution.py:498
  135.5 17.7 %collective-permute-start.28 = (bf16[160,1536]{1,0:T(8,128)(2,1)S(1)}, bf16[160,1536]{1,0:T(8,128)(2,1)S(1)}, u32[]{:S(2)}, u32[]{:S(2)}) collective-permute-start(bf16[160,1536]{1,0:T(8,128)(2,1)S(1)} %copy-done.18), channel_id=1, source_target_pairs={{0,3},{1,0},{2,1},{3,2},{4,7},{5,4},{6,5},{7,6},{8,11},{9,8},{10,9... | collective-permute-start | bytes 1474568 | tf_op jit(solution)/shard_map/ppermute | solution.py:471
  155.8 160.6 %all-gather.9.cloned.1.call-start = ((), (), s32[]{:S(2)}) async-start(), calls=%async_computation.2 | async-start | bytes 11796480 | tf_op jit(solution)/shard_map/all_gather | solution.py:598
  156.5 16.8 %collective-permute-start.20 = (bf16[256,1024]{1,0:T(8,128)(2,1)S(1)}, bf16[256,1024]{1,0:T(8,128)(2,1)}, u32[]{:S(2)}, u32[]{:S(2)}) collective-permute-start(bf16[256,1024]{1,0:T(8,128)(2,1)S(1)} %bitcast.62), channel_id=1, source_target_pairs={{0,1},{1,2},{2,3},{3,0},{4,5},{5,6},{6,7},{7,4},{8,9},{9,10},{10,1... | collective-permute-start | bytes 1572872 | tf_op jit(solution)/shard_map/ppermute | solution.py:471
  156.6 25.4 %collective-permute-start.21 = (bf16[256,1024]{1,0:T(8,128)(2,1)S(1)}, bf16[256,1024]{1,0:T(8,128)(2,1)}, u32[]{:S(2)}, u32[]{:S(2)}) collective-permute-start(bf16[256,1024]{1,0:T(8,128)(2,1)S(1)} %bitcast.63), channel_id=1, source_target_pairs={{0,3},{1,0},{2,1},{3,2},{4,7},{5,4},{6,5},{7,6},{8,11},{9,8},{10,9... | collective-permute-start | bytes 1572872 | tf_op jit(solution)/shard_map/ppermute | solution.py:471
  182.6 17.4 %collective-permute-start.23 = (bf16[256,1024]{1,0:T(8,128)(2,1)}, bf16[256,1024]{1,0:T(8,128)(2,1)S(1)}, u32[]{:S(2)}, u32[]{:S(2)}) collective-permute-start(bf16[256,1024]{1,0:T(8,128)(2,1)} %collective-permute-done.21.refs_2_), channel_id=1, source_target_pairs={{1,0},{2,1},{5,4},{6,5},{9,8},{10,9},{13,12},{14,13},{17,16},{18,1... | collective-permute-start | bytes 1572872 | tf_op jit(solution)/shard_map/ppermute | solution.py:481
  203.9 19.5 %collective-permute-start.24 = (bf16[256,1280]{1,0:T(8,128)(2,1)S(1)}, bf16[256,1280]{1,0:T(8,128)(2,1)S(1)}, u32[]{:S(2)}, u32[]{:S(2)}) collective-permute-start(bf16[256,1280]{1,0:T(8,128)(2,1)S(1)} %shard_map.107.refs_0_.refs_5_), channel_id=1, source_target_pairs={{0,1},{1,2},{2,3},{3,0},{4,5},{5,6},{6,7},{7,4},{8,9},{9,10},{10,1... | collective-permute-start | bytes 1966088 | tf_op jit(solution)/shard_map/ppermute | solution.py:471
  205.6 27.9 %collective-permute-start.26 = (bf16[256,1280]{1,0:T(8,128)(2,1)S(1)}, bf16[256,1280]{1,0:T(8,128)(2,1)S(1)}, u32[]{:S(2)}, u32[]{:S(2)}) collective-permute-start(bf16[256,1280]{1,0:T(8,128)(2,1)S(1)} %shard_map.107.refs_0_.refs_5_), channel_id=1, source_target_pairs={{0,3},{1,0},{2,1},{3,2},{4,7},{5,4},{6,5},{7,6},{8,11},{9,8},{10,9... | collective-permute-start | bytes 1966088 | tf_op jit(solution)/shard_map/ppermute | solution.py:471
  233.5 18.0 %collective-permute-start.27 = (bf16[256,1280]{1,0:T(8,128)(2,1)S(1)}, bf16[256,1280]{1,0:T(8,128)(2,1)}, u32[]{:S(2)}, u32[]{:S(2)}) collective-permute-start(bf16[256,1280]{1,0:T(8,128)(2,1)S(1)} %collective-permute-done.26.refs_3_), channel_id=1, source_target_pairs={{1,0},{2,1},{5,4},{6,5},{9,8},{10,9},{13,12},{14,13},{17,16},{18,1... | collective-permute-start | bytes 1966088 | tf_op jit(solution)/shard_map/ppermute | solution.py:481
  279.1 16.7 %collective-permute-start.29 = (bf16[256,1024]{1,0:T(8,128)(2,1)S(1)}, bf16[256,1024]{1,0:T(8,128)(2,1)S(1)}, u32[]{:S(2)}, u32[]{:S(2)}) collective-permute-start(bf16[256,1024]{1,0:T(8,128)(2,1)S(1)} %bitcast.59), channel_id=1, source_target_pairs={{0,1},{1,2},{2,3},{3,0},{4,5},{5,6},{6,7},{7,4},{8,9},{9,10},{10,1... | collective-permute-start | bytes 1572872 | tf_op jit(solution)/shard_map/ppermute | solution.py:471
  279.2 23.2 %collective-permute-start.31 = (bf16[256,1024]{1,0:T(8,128)(2,1)S(1)}, bf16[256,1024]{1,0:T(8,128)(2,1)S(1)}, u32[]{:S(2)}, u32[]{:S(2)}) collective-permute-start(bf16[256,1024]{1,0:T(8,128)(2,1)S(1)} %bitcast.60), channel_id=1, source_target_pairs={{0,3},{1,0},{2,1},{3,2},{4,7},{5,4},{6,5},{7,6},{8,11},{9,8},{10,9... | collective-permute-start | bytes 1572872 | tf_op jit(solution)/shard_map/ppermute | solution.py:471
  302.4 14.0 %collective-permute-start.32 = (bf16[256,1024]{1,0:T(8,128)(2,1)S(1)}, bf16[256,1024]{1,0:T(8,128)(2,1)S(1)}, u32[]{:S(2)}, u32[]{:S(2)}) collective-permute-start(bf16[256,1024]{1,0:T(8,128)(2,1)S(1)} %collective-permute-done.31.refs_3_), channel_id=1, source_target_pairs={{1,0},{2,1},{5,4},{6,5},{9,8},{10,9},{13,12},{14,13},{17,16},{18,1... | collective-permute-start | bytes 1572872 | tf_op jit(solution)/shard_map/ppermute | solution.py:481
  323.7 19.5 %collective-permute-start.33 = (bf16[256,1280]{1,0:T(8,128)(2,1)S(1)}, bf16[256,1280]{1,0:T(8,128)(2,1)S(1)}, u32[]{:S(2)}, u32[]{:S(2)}) collective-permute-start(bf16[256,1280]{1,0:T(8,128)(2,1)S(1)} %shard_map.110.refs_0_), channel_id=1, source_target_pairs={{0,1},{1,2},{2,3},{3,0},{4,5},{5,6},{6,7},{7,4},{8,9},{9,10},{10,1... | collective-permute-start | bytes 1966088 | tf_op jit(solution)/shard_map/ppermute | solution.py:471
  323.8 29.1 %collective-permute-start.35 = (bf16[256,1280]{1,0:T(8,128)(2,1)S(1)}, bf16[256,1280]{1,0:T(8,128)(2,1)S(1)}, u32[]{:S(2)}, u32[]{:S(2)}) collective-permute-start(bf16[256,1280]{1,0:T(8,128)(2,1)S(1)} %shard_map.110.refs_0_), channel_id=1, source_target_pairs={{0,3},{1,0},{2,1},{3,2},{4,7},{5,4},{6,5},{7,6},{8,11},{9,8},{10,9... | collective-permute-start | bytes 1966088 | tf_op jit(solution)/shard_map/ppermute | solution.py:471
  352.9 18.0 %collective-permute-start.36 = (bf16[256,1280]{1,0:T(8,128)(2,1)S(1)}, bf16[256,1280]{1,0:T(8,128)(2,1)S(1)}, u32[]{:S(2)}, u32[]{:S(2)}) collective-permute-start(bf16[256,1280]{1,0:T(8,128)(2,1)S(1)} %collective-permute-done.35.refs_3_), channel_id=1, source_target_pairs={{1,0},{2,1},{5,4},{6,5},{9,8},{10,9},{13,12},{14,13},{17,16},{18,1... | collective-permute-start | bytes 1966088 | tf_op jit(solution)/shard_map/ppermute | solution.py:481
  (32 other events, 313.2 us)
Sparse Core Ops, SparseCore 0:
  91.4 69.4 all-gather.4
  162.8 85.4 all-gather.6
  250.1 63.2 all-gather.8

commit v4 on v3

--- a/solution.py
+++ b/solution.py
@@ -591,7 +591,7 @@
         later_three = shifted(after(outgoing(1, 3), later_two), 3)
         came = (outgoing(1, 0), later_one, later_two, later_three)
         ready = (scale, core_gains, gathers[0][0][2], gathers[0][1][2], *both)
-        sent = [after(out_weight[0], *across, *turned, later_one, *ready), out_weight[1]]
+        sent = [after(out_weight[0], *ahead, *turned, two, *ready), out_weight[1]]
     else:
         gathers = [from_calls(layer) for layer in range(layers)]
         sent = [out_weight[layer] for layer in range(layers)]

time: 383 us -> 380 us (level)
    unnamed x48 -> x50, local copies, waits for them, and re-layouts: 9.59 us -> 9.16 us
  transfers between devices with their start and end apart: 40 -> 40, of which waited for: 21 -> 19; matrix products, arithmetic and copies ran while one was open for 6% -> 5% of each run, Pallas kernels for 18% -> 18%
where the time goes in v4:
time: 380 us; the launch traced here: 379 us
  waiting for transfers between devices  207 us (54%)
  Pallas kernels  77 us (20%)
  starting transfers between devices  48.5 us (13%)
  local copies, waits for them, and re-layouts  24.9 us (7%)
  between operations  13.8 us (4%)
  other arithmetic  7.9 us (2%)
    ppermute x14, waiting for transfers between devices, shifted(): lax.ppermute(block, 'tp', [(i, (i + shift) % parts) for i in range(parts)])  107 us
    ppermute x4, waiting for transfers between devices, all_parts(): leftwards = lax.ppermute(from_right, 'tp', [(1, 0), (2, 1)])  53.5 us
    ppermute x15, waiting for transfers between devices, swapped(): return lax.ppermute(block, 'rep', [(i, i ^ mask) for i in range(replicas)])  45.3 us
    pallas_call x3, Pallas kernels, project_qkv(): pl.pallas_call(functools.partial(qkv_kernel, count, shifts, pieces, len(w...  27.7 us
    pallas_call x2, Pallas kernels, attend(): pl.pallas_call(functools.partial(attention_kernel, heads), out_shape=jax....  25.9 us
    ppermute x14, starting transfers between devices, shifted(): lax.ppermute(block, 'tp', [(i, (i + shift) % parts) for i in range(parts)])  25.4 us
    ppermute x15, starting transfers between devices, swapped(): return lax.ppermute(block, 'rep', [(i, i ^ mask) for i in range(replicas)])  15 us
    unnamed x50, local copies, waits for them, and re-layouts  9.16 us
  transfers between devices with their start and end apart: 40, of which 19 were waited for; matrix products, arithmetic and copies ran while one was open for 5% of the time, Pallas kernels for 18%

profile of v4, /device:TPU:0, one launch (start us, length us, event | category | flops | bytes accessed | tf_op | source)
XLA Modules:
  0.0 378.7 jit_solution(14313265275867151395)
XLA Ops:
  6.5 4.1 %dynamic-slice_bitcast_fusion = (bf16[160,1536]{1,0:T(8,128)(2,1)}, bf16[160,1536]{1,0:T(8,128)(2,1)}, bf16[160,1536]{1,0:T(8,128)(2,1)}, bf16[160,1536]{1,0:T(8...) fusion(bf16[2,160,6144]{2,1,0:T(8,128)(2,1)} %param.11, ...), kind=kLoop, calls=%fused_computation.14 | loop fusion | bytes 7864336 | tf_op jit(solution)/shard_map/squeeze | solution.py:486
  10.6 2.9 collective-permute-start.5
  23.2 9.6 %collective-permute-done.2 = bf16[160,1536]{1,0:T(8,128)(2,1)} collective-permute-done((bf16[160,1536]{1,0:T(8,128)(2,1)}, bf16[160,1536]{1,0:T(8,128)(2,1)}, u32[]{:S(2)}, u32[]{:S(2)}) %collective-permute-start.2) | collective-permute-done | bytes 491552 | tf_op jit(solution)/shard_map/ppermute | solution.py:471
  32.8 9.6 %collective-permute-done.3 = bf16[160,1536]{1,0:T(8,128)(2,1)} collective-permute-done((bf16[160,1536]{1,0:T(8,128)(2,1)}, bf16[160,1536]{1,0:T(8,128)(2,1)}, u32[]{:S(2)}, u32[]{:S(2)}) %collective-permute-start.3) | collective-permute-done | bytes 491552 | tf_op jit(solution)/shard_map/ppermute | solution.py:471
  59.3 14.2 %collective-permute-done.9.refs_8_ = bf16[80,1536]{1,0:T(8,128)(2,1)S(1)} collective-permute-done((bf16[80,1536]{1,0:T(8,128)(2,1)S(1)}, bf16[80,1536]{1,0:T(8,128)(2,1)S(1)}, u32[]{:S(2)}, u32[]{:S(2)}) %collective-permute-start.9) | collective-permute-done | bytes 245792 | tf_op jit(solution)/shard_map/ppermute | solution.py:498
  83.2 12.1 %collective-permute-done.11.refs_4_ = bf16[160,1536]{1,0:T(8,128)(2,1)S(1)} collective-permute-done((bf16[160,1536]{1,0:T(8,128)(2,1)}, bf16[160,1536]{1,0:T(8,128)(2,1)S(1)}, u32[]{:S(2)}, u32[]{:S(2)}) %collective-permute-start.11) | collective-permute-done | bytes 491552 | tf_op jit(solution)/shard_map/ppermute | solution.py:498
  97.6 18.4 %collective-permute-done.15.refs_13_ = bf16[160,1536]{1,0:T(8,128)(2,1)S(1)} collective-permute-done((bf16[160,1536]{1,0:T(8,128)(2,1)S(1)}, bf16[160,1536]{1,0:T(8,128)(2,1)S(1)}, u32[]{:S(2)}, u32[]{:S(2)}) %collective-permute-start.15) | collective-permute-done | bytes 491552 | tf_op jit(solution)/shard_map/ppermute | solution.py:498
  118.3 10.0 %shard_map.102 = (f32[256,1536]{1,0:T(8,128)}, f32[256,1536]{1,0:T(8,128)}) custom-call(s32[13]{0:T(128)S(1)} %stack.40.rows_ref, bf16[512,640]{1,0:T(8,128)(2,1)} %get-tuple-element.61.refs_0_, bf16[512,640]{1,0:T(8,128)(2,1)} %get-tuple-element.60.refs_1_, bf16[512,640]{1,0:T(8,128)(2,1)} %get-tuple-element.59.refs_2_, ...), custom_call_target="tpu_custom_call" | custom-call | flops 3019898880 | bytes 5898240 | tf_op jit(solution)/shard_map/pallas_call | solution.py:187
  128.4 7.4 %shard_map.103 = (f32[256,1536]{1,0:T(8,128)}, f32[256,1536]{1,0:T(8,128)}) custom-call(s32[5]{0:T(128)S(1)} %stack.19.rows_ref, bf16[512,640]{1,0:T(8,128)(2,1)} %get-tuple-element.62.refs_0_, f32[4,1,640]{2,1,0:T(1,128)S(1)} %reshape.165.refs_3_.refs_1_, f32[512,1]{1,0:T(8,128)S(1)} %rsqrt.3.refs_4_.refs_2_, ...), custom_call_target="tpu_custom_call" | custom-call | flops 1006632960 | bytes 1966080 | tf_op jit(solution)/shard_map/pallas_call | solution.py:187
  135.9 3.2 collective-permute-start.28
  141.3 12.8 %shard_map.104 = bf16[4,64,1024]{2,1,0:T(8,128)(2,1)S(1)} custom-call(s32[64]{0:T(128)S(1)} %copy-done.10, f32[4,64,1536]{2,1,0:T(8,128)S(1)} %bitcast.65, f32[4,64,1536]{2,1,0:T(8,128)S(1)} %bitcast.66, f32[4,64,128]{2,1,0:T(8,128)S(1)} %get-tuple-element.72.refs_2_.refs_1_, f32[4,64,128]{2,1,0:T(8,128)S(1)} %get-tuple-element.73.refs_3_.refs_2_, ...), custom_call_target="tpu_custom_call" | custom-call | flops 268435456 | bytes 16777216 | tf_op jit(solution)/shard_map/pallas_call | solution.py:413
  156.4 3.8 %collective-permute-start.21 = (bf16[256,1024]{1,0:T(8,128)(2,1)S(1)}, bf16[256,1024]{1,0:T(8,128)(2,1)}, u32[]{:S(2)}, u32[]{:S(2)}) collective-permute-start(bf16[256,1024]{1,0:T(8,128)(2,1)S(1)} %bitcast.63), channel_id=1, source_target_pairs={{0,3},{1,0},{2,1},{3,2},{4,7},{5,4},{6,5},{7,6},{8,11},{9,8},{10,9... | collective-permute-start | bytes 1572872 | tf_op jit(solution)/shard_map/ppermute | solution.py:471
  163.1 10.0 %collective-permute-done.20.refs_1_ = bf16[256,1024]{1,0:T(8,128)(2,1)} collective-permute-done((bf16[256,1024]{1,0:T(8,128)(2,1)S(1)}, bf16[256,1024]{1,0:T(8,128)(2,1)}, u32[]{:S(2)}, u32[]{:S(2)}) %collective-permute-start.20) | collective-permute-done | bytes 524320 | tf_op jit(solution)/shard_map/ppermute | solution.py:471
  173.1 8.6 %collective-permute-done.21.refs_2_ = bf16[256,1024]{1,0:T(8,128)(2,1)} collective-permute-done((bf16[256,1024]{1,0:T(8,128)(2,1)S(1)}, bf16[256,1024]{1,0:T(8,128)(2,1)}, u32[]{:S(2)}, u32[]{:S(2)}) %collective-permute-start.21) | collective-permute-done | bytes 524320 | tf_op jit(solution)/shard_map/ppermute | solution.py:471
  185.0 5.9 %shard_map.105.refs_2_ = f32[256,1280]{1,0:T(8,128)S(1)} custom-call(s32[4]{0:T(128)S(1)} %broadcast_multiply_fusion.column_ref, bf16[256,1024]{1,0:T(8,128)(2,1)S(1)} %bitcast.64, bf16[256,1024]{1,0:T(8,128)(2,1)} %collective-permute-done.20.refs_1_, bf16[256,1024]{1,0:T(8,128)(2,1)} %collective-permute-done.21.refs_2_, ...), custom_call_target="tpu_custom_call" | custom-call | flops 2013265920 | bytes 7864320 | tf_op jit(solution)/shard_map/pallas_call | solution.py:311
  190.9 8.8 %collective-permute-done.23 = bf16[256,1024]{1,0:T(8,128)(2,1)S(1)} collective-permute-done((bf16[256,1024]{1,0:T(8,128)(2,1)}, bf16[256,1024]{1,0:T(8,128)(2,1)S(1)}, u32[]{:S(2)}, u32[]{:S(2)}) %collective-permute-start.23) | collective-permute-done | bytes 524320 | tf_op jit(solution)/shard_map/ppermute | solution.py:481
  199.8 3.2 shard_map.107.refs_0_.refs_5_
  206.8 15.6 %collective-permute-done.24.refs_1_ = bf16[256,1280]{1,0:T(8,128)(2,1)S(1)} collective-permute-done((bf16[256,1280]{1,0:T(8,128)(2,1)S(1)}, bf16[256,1280]{1,0:T(8,128)(2,1)S(1)}, u32[]{:S(2)}, u32[]{:S(2)}) %collective-permute-start.24) | collective-permute-done | bytes 655392 | tf_op jit(solution)/shard_map/ppermute | solution.py:471
  224.0 9.3 %collective-permute-done.26.refs_3_ = bf16[256,1280]{1,0:T(8,128)(2,1)S(1)} collective-permute-done((bf16[256,1280]{1,0:T(8,128)(2,1)S(1)}, bf16[256,1280]{1,0:T(8,128)(2,1)S(1)}, u32[]{:S(2)}, u32[]{:S(2)}) %collective-permute-start.26) | collective-permute-done | bytes 655392 | tf_op jit(solution)/shard_map/ppermute | solution.py:471
  234.7 16.6 %collective-permute-done.27 = bf16[256,1280]{1,0:T(8,128)(2,1)} collective-permute-done((bf16[256,1280]{1,0:T(8,128)(2,1)S(1)}, bf16[256,1280]{1,0:T(8,128)(2,1)}, u32[]{:S(2)}, u32[]{:S(2)}) %collective-permute-start.27) | collective-permute-done | bytes 655392 | tf_op jit(solution)/shard_map/ppermute | solution.py:481
  254.8 10.3 %shard_map.108 = f32[256,1536]{1,0:T(8,128)S(1)} custom-call(s32[32]{0:T(128)S(1)} %copy-done.11, bf16[256,1280]{1,0:T(8,128)(2,1)S(1)} %shard_map.107.refs_0_.refs_5_, bf16[256,1280]{1,0:T(8,128)(2,1)S(1)} %copy-done.5, bf16[256,1280]{1,0:T(8,128)(2,1)S(1)} %broadcast_select_fusion.1.refs_2_, bf16[256,1280]{1,0:T(8,128)(2,1)S(1)} %copy-done.7, ...), custom_call_target="tpu_custom_call" | custom-call | flops 4026531840 | bytes 15728640 | tf_op jit(solution)/shard_map/pallas_call | solution.py:187
  265.1 13.1 %shard_map.109 = bf16[4,64,1024]{2,1,0:T(8,128)(2,1)S(1)} custom-call(s32[64]{0:T(128)S(1)} %copy-done.10, f32[4,64,1536]{2,1,0:T(8,128)S(1)} %bitcast.58, f32[4,64,128]{2,1,0:T(8,128)S(1)} %get-tuple-element.72.refs_2_.refs_1_, f32[4,64,128]{2,1,0:T(8,128)S(1)} %get-tuple-element.73.refs_3_.refs_2_, f32[1,128]{1,0:T(1,128)S(1)} %get-tuple-element.75.refs_3_, ...), custom_call_target="tpu_custom_call" | custom-call | flops 268435456 | bytes 16777216 | tf_op jit(solution)/shard_map/pallas_call | solution.py:413
  278.6 3.5 collective-permute-start.31
  282.1 12.8 %collective-permute-done.29.refs_1_ = bf16[256,1024]{1,0:T(8,128)(2,1)S(1)} collective-permute-done((bf16[256,1024]{1,0:T(8,128)(2,1)S(1)}, bf16[256,1024]{1,0:T(8,128)(2,1)S(1)}, u32[]{:S(2)}, u32[]{:S(2)}) %collective-permute-start.29) | collective-permute-done | bytes 524320 | tf_op jit(solution)/shard_map/ppermute | solution.py:471
  295.6 6.4 %collective-permute-done.31.refs_3_ = bf16[256,1024]{1,0:T(8,128)(2,1)S(1)} collective-permute-done((bf16[256,1024]{1,0:T(8,128)(2,1)S(1)}, bf16[256,1024]{1,0:T(8,128)(2,1)S(1)}, u32[]{:S(2)}, u32[]{:S(2)}) %collective-permute-start.31) | collective-permute-done | bytes 524320 | tf_op jit(solution)/shard_map/ppermute | solution.py:471
  303.3 12.7 %collective-permute-done.32 = bf16[256,1024]{1,0:T(8,128)(2,1)S(1)} collective-permute-done((bf16[256,1024]{1,0:T(8,128)(2,1)S(1)}, bf16[256,1024]{1,0:T(8,128)(2,1)S(1)}, u32[]{:S(2)}, u32[]{:S(2)}) %collective-permute-start.32) | collective-permute-done | bytes 524320 | tf_op jit(solution)/shard_map/ppermute | solution.py:481
  317.2 6.3 %shard_map.110.refs_0_ = bf16[256,1280]{1,0:T(8,128)(2,1)S(1)} custom-call(s32[4]{0:T(128)S(1)} %broadcast_multiply_fusion.column_ref, bf16[256,1024]{1,0:T(8,128)(2,1)S(1)} %bitcast.61, bf16[256,1024]{1,0:T(8,128)(2,1)S(1)} %collective-permute-done.29.refs_1_, bf16[256,1024]{1,0:T(8,128)(2,1)S(1)} %broadcast_select_fusion.2.refs_2_, ...), custom_call_target="tpu_custom_call" | custom-call | flops 2684354560 | bytes 10485760 | tf_op jit(solution)/shard_map/pallas_call | solution.py:245
  323.6 3.7 collective-permute-start.35
  327.3 15.6 %collective-permute-done.33.refs_1_ = bf16[256,1280]{1,0:T(8,128)(2,1)S(1)} collective-permute-done((bf16[256,1280]{1,0:T(8,128)(2,1)S(1)}, bf16[256,1280]{1,0:T(8,128)(2,1)S(1)}, u32[]{:S(2)}, u32[]{:S(2)}) %collective-permute-start.33) | collective-permute-done | bytes 655392 | tf_op jit(solution)/shard_map/ppermute | solution.py:471
  343.6 7.9 %collective-permute-done.35.refs_3_ = bf16[256,1280]{1,0:T(8,128)(2,1)S(1)} collective-permute-done((bf16[256,1280]{1,0:T(8,128)(2,1)S(1)}, bf16[256,1280]{1,0:T(8,128)(2,1)S(1)}, u32[]{:S(2)}, u32[]{:S(2)}) %collective-permute-start.35) | collective-permute-done | bytes 655392 | tf_op jit(solution)/shard_map/ppermute | solution.py:471
  352.9 15.4 %collective-permute-done.36 = bf16[256,1280]{1,0:T(8,128)(2,1)S(1)} collective-permute-done((bf16[256,1280]{1,0:T(8,128)(2,1)S(1)}, bf16[256,1280]{1,0:T(8,128)(2,1)S(1)}, u32[]{:S(2)}, u32[]{:S(2)}) %collective-permute-start.36) | collective-permute-done | bytes 655392 | tf_op jit(solution)/shard_map/ppermute | solution.py:481
  368.3 3.8 shard_map.111
  (156 shorter events, 67.2 us)
Async XLA Ops:
  6.5 175.2 %all-gather.5.cloned.1.call-start = ((), (), s32[]{:S(2)}) async-start(), calls=%async_computation | async-start | bytes 11796480 | tf_op jit(solution)/shard_map/all_gather | solution.py:598
  10.6 34.0 %collective-permute-start.5 = (bf16[160,1536]{1,0:T(8,128)(2,1)S(1)}, bf16[160,1536]{1,0:T(8,128)(2,1)}, u32[]{:S(2)}, u32[]{:S(2)}) collective-permute-start(bf16[160,1536]{1,0:T(8,128)(2,1)S(1)} %get-tuple-element.52.refs_5_), channel_id=1, source_target_pairs={{0,8},{4,12},{8,0},{12,4},{16,24},{20,28},{24,16},{28,20},{1,9},{5... | collective-permute-start | bytes 1474568 | tf_op jit(solution)/shard_map/ppermute | solution.py:498
  13.6 31.0 %collective-permute-start.6 = (bf16[160,1536]{1,0:T(8,128)(2,1)S(1)}, bf16[160,1536]{1,0:T(8,128)(2,1)}, u32[]{:S(2)}, u32[]{:S(2)}) collective-permute-start(bf16[160,1536]{1,0:T(8,128)(2,1)S(1)} %get-tuple-element.52.refs_5_), channel_id=1, source_target_pairs={{0,16},{4,20},{8,24},{12,28},{16,0},{20,4},{24,8},{28,12},{1,17},{... | collective-permute-start | bytes 1474568 | tf_op jit(solution)/shard_map/ppermute | solution.py:498
  16.6 36.5 %collective-permute-start = (bf16[256,2560]{1,0:T(8,128)(2,1)}, bf16[256,2560]{1,0:T(8,128)(2,1)}, u32[]{:S(2)}, u32[]{:S(2)}) collective-permute-start(bf16[256,2560]{1,0:T(8,128)(2,1)} %get-tuple-element.28), channel_id=1, source_target_pairs={{0,4},{4,0},{8,12},{12,8},{16,20},{20,16},{24,28},{28,24},{1,5},{5... | collective-permute-start | bytes 3932168 | tf_op jit(solution)/shard_map/ppermute | solution.py:498
  16.6 16.2 %collective-permute-start.2 = (bf16[160,1536]{1,0:T(8,128)(2,1)}, bf16[160,1536]{1,0:T(8,128)(2,1)}, u32[]{:S(2)}, u32[]{:S(2)}) collective-permute-start(bf16[160,1536]{1,0:T(8,128)(2,1)} %get-tuple-element.54), channel_id=1, source_target_pairs={{0,1},{1,2},{2,3},{3,0},{4,5},{5,6},{6,7},{7,4},{8,9},{9,10},{10,1... | collective-permute-start | bytes 1474568 | tf_op jit(solution)/shard_map/ppermute | solution.py:471
  18.2 24.2 %collective-permute-start.3 = (bf16[160,1536]{1,0:T(8,128)(2,1)}, bf16[160,1536]{1,0:T(8,128)(2,1)}, u32[]{:S(2)}, u32[]{:S(2)}) collective-permute-start(bf16[160,1536]{1,0:T(8,128)(2,1)} %get-tuple-element.53), channel_id=1, source_target_pairs={{0,3},{1,0},{2,1},{3,2},{4,7},{5,4},{6,5},{7,6},{8,11},{9,8},{10,9... | collective-permute-start | bytes 1474568 | tf_op jit(solution)/shard_map/ppermute | solution.py:471
  44.6 30.3 %collective-permute-start.7 = (bf16[320,1536]{1,0:T(8,128)(2,1)}, bf16[320,1536]{1,0:T(8,128)(2,1)}, u32[]{:S(2)}, u32[]{:S(2)}) collective-permute-start(bf16[320,1536]{1,0:T(8,128)(2,1)} %pad_maximum_fusion.2.refs_10_), channel_id=1, source_target_pairs={{0,8},{4,12},{8,0},{12,4},{16,24},{20,28},{24,16},{28,20},{1,9},{5... | collective-permute-start | bytes 2949128 | tf_op jit(solution)/shard_map/ppermute | solution.py:498
  45.1 29.7 %collective-permute-start.8 = (bf16[320,1536]{1,0:T(8,128)(2,1)}, bf16[320,1536]{1,0:T(8,128)(2,1)}, u32[]{:S(2)}, u32[]{:S(2)}) collective-permute-start(bf16[320,1536]{1,0:T(8,128)(2,1)} %pad_maximum_fusion.2.refs_10_), channel_id=1, source_target_pairs={{0,16},{4,20},{8,24},{12,28},{16,0},{20,4},{24,8},{28,12},{1,17},{... | collective-permute-start | bytes 2949128 | tf_op jit(solution)/shard_map/ppermute | solution.py:498
  49.0 24.5 %collective-permute-start.9 = (bf16[80,1536]{1,0:T(8,128)(2,1)S(1)}, bf16[80,1536]{1,0:T(8,128)(2,1)S(1)}, u32[]{:S(2)}, u32[]{:S(2)}) collective-permute-start(bf16[80,1536]{1,0:T(8,128)(2,1)S(1)} %slice.82), channel_id=1, source_target_pairs={{0,16},{4,20},{8,24},{12,28},{16,0},{20,4},{24,8},{28,12},{1,17},{... | collective-permute-start | bytes 737288 | tf_op jit(solution)/shard_map/ppermute | solution.py:498
  51.6 22.6 %collective-permute-start.10 = (bf16[80,1536]{1,0:T(8,128)(2,1)S(1)}, bf16[80,1536]{1,0:T(8,128)(2,1)S(1)}, u32[]{:S(2)}, u32[]{:S(2)}) collective-permute-start(bf16[80,1536]{1,0:T(8,128)(2,1)S(1)} %slice.83), channel_id=1, source_target_pairs={{0,8},{4,12},{8,0},{12,4},{16,24},{20,28},{24,16},{28,20},{1,9},{5... | collective-permute-start | bytes 737288 | tf_op jit(solution)/shard_map/ppermute | solution.py:498
  53.1 23.3 %collective-permute-start.4 = (bf16[160,1536]{1,0:T(8,128)(2,1)}, bf16[160,1536]{1,0:T(8,128)(2,1)}, u32[]{:S(2)}, u32[]{:S(2)}) collective-permute-start(bf16[160,1536]{1,0:T(8,128)(2,1)} %get-tuple-element.30), channel_id=1, source_target_pairs={{0,2},{1,3},{2,0},{3,1},{4,6},{5,7},{6,4},{7,5},{8,10},{9,11},{10,... | collective-permute-start | bytes 1474568 | tf_op jit(solution)/shard_map/ppermute | solution.py:471
  76.4 176.2 %all-gather.7.cloned.1.call-start = ((), (), s32[]{:S(2)}) async-start(), calls=%async_computation.1 | async-start | bytes 17694720 | tf_op jit(solution)/shard_map/all_gather | solution.py:547
  76.5 18.9 %collective-permute-start.11 = (bf16[160,1536]{1,0:T(8,128)(2,1)}, bf16[160,1536]{1,0:T(8,128)(2,1)S(1)}, u32[]{:S(2)}, u32[]{:S(2)}) collective-permute-start(bf16[160,1536]{1,0:T(8,128)(2,1)} %collective-permute-done.4.refs_3_), channel_id=1, source_target_pairs={{0,8},{4,12},{8,0},{12,4},{16,24},{20,28},{24,16},{28,20},{1,9},{5... | collective-permute-start | bytes 1474568 | tf_op jit(solution)/shard_map/ppermute | solution.py:498
  77.1 18.8 %collective-permute-start.12 = (bf16[160,1536]{1,0:T(8,128)(2,1)}, bf16[160,1536]{1,0:T(8,128)(2,1)S(1)}, u32[]{:S(2)}, u32[]{:S(2)}) collective-permute-start(bf16[160,1536]{1,0:T(8,128)(2,1)} %collective-permute-done.4.refs_3_), channel_id=1, source_target_pairs={{0,16},{4,20},{8,24},{12,28},{16,0},{20,4},{24,8},{28,12},{1,17},{... | collective-permute-start | bytes 1474568 | tf_op jit(solution)/shard_map/ppermute | solution.py:498
  78.6 37.4 %collective-permute-start.15 = (bf16[160,1536]{1,0:T(8,128)(2,1)S(1)}, bf16[160,1536]{1,0:T(8,128)(2,1)S(1)}, u32[]{:S(2)}, u32[]{:S(2)}) collective-permute-start(bf16[160,1536]{1,0:T(8,128)(2,1)S(1)} %slice.89), channel_id=1, source_target_pairs={{0,16},{4,20},{8,24},{12,28},{16,0},{20,4},{24,8},{28,12},{1,17},{... | collective-permute-start | bytes 1474568 | tf_op jit(solution)/shard_map/ppermute | solution.py:498
  81.3 36.2 %collective-permute-start.16 = (bf16[160,1536]{1,0:T(8,128)(2,1)S(1)}, bf16[160,1536]{1,0:T(8,128)(2,1)S(1)}, u32[]{:S(2)}, u32[]{:S(2)}) collective-permute-start(bf16[160,1536]{1,0:T(8,128)(2,1)S(1)} %slice.90), channel_id=1, source_target_pairs={{0,8},{4,12},{8,0},{12,4},{16,24},{20,28},{24,16},{28,20},{1,9},{5... | collective-permute-start | bytes 1474568 | tf_op jit(solution)/shard_map/ppermute | solution.py:498
  82.8 45.5 %collective-permute-start.17 = (bf16[160,1536]{1,0:T(8,128)(2,1)}, bf16[160,1536]{1,0:T(8,128)(2,1)S(1)}, u32[]{:S(2)}, u32[]{:S(2)}) collective-permute-start(bf16[160,1536]{1,0:T(8,128)(2,1)} %get-tuple-element.35), channel_id=1, source_target_pairs={{0,1},{1,2},{2,3},{3,0},{4,5},{5,6},{6,7},{7,4},{8,9},{9,10},{10,1... | collective-permute-start | bytes 1474568 | tf_op jit(solution)/shard_map/ppermute | solution.py:471
  95.9 32.4 %collective-permute-start.18 = (bf16[160,1536]{1,0:T(8,128)(2,1)}, bf16[160,1536]{1,0:T(8,128)(2,1)S(1)}, u32[]{:S(2)}, u32[]{:S(2)}) collective-permute-start(bf16[160,1536]{1,0:T(8,128)(2,1)} %get-tuple-element.36), channel_id=1, source_target_pairs={{0,2},{1,3},{2,0},{3,1},{4,6},{5,7},{6,4},{7,5},{8,10},{9,11},{10,... | collective-permute-start | bytes 1474568 | tf_op jit(solution)/shard_map/ppermute | solution.py:471
  97.1 31.3 %collective-permute-start.13 = (bf16[80,1536]{1,0:T(8,128)(2,1)S(1)}, bf16[80,1536]{1,0:T(8,128)(2,1)S(1)}, u32[]{:S(2)}, u32[]{:S(2)}) collective-permute-start(bf16[80,1536]{1,0:T(8,128)(2,1)S(1)} %slice.84), channel_id=1, source_target_pairs={{0,16},{4,20},{8,24},{12,28},{16,0},{20,4},{24,8},{28,12},{1,17},{... | collective-permute-start | bytes 737288 | tf_op jit(solution)/shard_map/ppermute | solution.py:498
  135.9 18.2 %collective-permute-start.28 = (bf16[160,1536]{1,0:T(8,128)(2,1)S(1)}, bf16[160,1536]{1,0:T(8,128)(2,1)S(1)}, u32[]{:S(2)}, u32[]{:S(2)}) collective-permute-start(bf16[160,1536]{1,0:T(8,128)(2,1)S(1)} %copy-done.19), channel_id=1, source_target_pairs={{0,3},{1,0},{2,1},{3,2},{4,7},{5,4},{6,5},{7,6},{8,11},{9,8},{10,9... | collective-permute-start | bytes 1474568 | tf_op jit(solution)/shard_map/ppermute | solution.py:471
  155.6 160.5 %all-gather.9.cloned.1.call-start = ((), (), s32[]{:S(2)}) async-start(), calls=%async_computation.2 | async-start | bytes 11796480 | tf_op jit(solution)/shard_map/all_gather | solution.py:598
  156.3 16.8 %collective-permute-start.20 = (bf16[256,1024]{1,0:T(8,128)(2,1)S(1)}, bf16[256,1024]{1,0:T(8,128)(2,1)}, u32[]{:S(2)}, u32[]{:S(2)}) collective-permute-start(bf16[256,1024]{1,0:T(8,128)(2,1)S(1)} %bitcast.62), channel_id=1, source_target_pairs={{0,1},{1,2},{2,3},{3,0},{4,5},{5,6},{6,7},{7,4},{8,9},{9,10},{10,1... | collective-permute-start | bytes 1572872 | tf_op jit(solution)/shard_map/ppermute | solution.py:471
  156.4 25.3 %collective-permute-start.21 = (bf16[256,1024]{1,0:T(8,128)(2,1)S(1)}, bf16[256,1024]{1,0:T(8,128)(2,1)}, u32[]{:S(2)}, u32[]{:S(2)}) collective-permute-start(bf16[256,1024]{1,0:T(8,128)(2,1)S(1)} %bitcast.63), channel_id=1, source_target_pairs={{0,3},{1,0},{2,1},{3,2},{4,7},{5,4},{6,5},{7,6},{8,11},{9,8},{10,9... | collective-permute-start | bytes 1572872 | tf_op jit(solution)/shard_map/ppermute | solution.py:471
  182.4 17.3 %collective-permute-start.23 = (bf16[256,1024]{1,0:T(8,128)(2,1)}, bf16[256,1024]{1,0:T(8,128)(2,1)S(1)}, u32[]{:S(2)}, u32[]{:S(2)}) collective-permute-start(bf16[256,1024]{1,0:T(8,128)(2,1)} %collective-permute-done.21.refs_2_), channel_id=1, source_target_pairs={{1,0},{2,1},{5,4},{6,5},{9,8},{10,9},{13,12},{14,13},{17,16},{18,1... | collective-permute-start | bytes 1572872 | tf_op jit(solution)/shard_map/ppermute | solution.py:481
  203.0 19.5 %collective-permute-start.24 = (bf16[256,1280]{1,0:T(8,128)(2,1)S(1)}, bf16[256,1280]{1,0:T(8,128)(2,1)S(1)}, u32[]{:S(2)}, u32[]{:S(2)}) collective-permute-start(bf16[256,1280]{1,0:T(8,128)(2,1)S(1)} %shard_map.107.refs_0_.refs_5_), channel_id=1, source_target_pairs={{0,1},{1,2},{2,3},{3,0},{4,5},{5,6},{6,7},{7,4},{8,9},{9,10},{10,1... | collective-permute-start | bytes 1966088 | tf_op jit(solution)/shard_map/ppermute | solution.py:471
  204.7 28.6 %collective-permute-start.26 = (bf16[256,1280]{1,0:T(8,128)(2,1)S(1)}, bf16[256,1280]{1,0:T(8,128)(2,1)S(1)}, u32[]{:S(2)}, u32[]{:S(2)}) collective-permute-start(bf16[256,1280]{1,0:T(8,128)(2,1)S(1)} %shard_map.107.refs_0_.refs_5_), channel_id=1, source_target_pairs={{0,3},{1,0},{2,1},{3,2},{4,7},{5,4},{6,5},{7,6},{8,11},{9,8},{10,9... | collective-permute-start | bytes 1966088 | tf_op jit(solution)/shard_map/ppermute | solution.py:471
  233.3 18.0 %collective-permute-start.27 = (bf16[256,1280]{1,0:T(8,128)(2,1)S(1)}, bf16[256,1280]{1,0:T(8,128)(2,1)}, u32[]{:S(2)}, u32[]{:S(2)}) collective-permute-start(bf16[256,1280]{1,0:T(8,128)(2,1)S(1)} %collective-permute-done.26.refs_3_), channel_id=1, source_target_pairs={{1,0},{2,1},{5,4},{6,5},{9,8},{10,9},{13,12},{14,13},{17,16},{18,1... | collective-permute-start | bytes 1966088 | tf_op jit(solution)/shard_map/ppermute | solution.py:481
  278.2 16.7 %collective-permute-start.29 = (bf16[256,1024]{1,0:T(8,128)(2,1)S(1)}, bf16[256,1024]{1,0:T(8,128)(2,1)S(1)}, u32[]{:S(2)}, u32[]{:S(2)}) collective-permute-start(bf16[256,1024]{1,0:T(8,128)(2,1)S(1)} %bitcast.59), channel_id=1, source_target_pairs={{0,1},{1,2},{2,3},{3,0},{4,5},{5,6},{6,7},{7,4},{8,9},{9,10},{10,1... | collective-permute-start | bytes 1572872 | tf_op jit(solution)/shard_map/ppermute | solution.py:471
  278.6 23.5 %collective-permute-start.31 = (bf16[256,1024]{1,0:T(8,128)(2,1)S(1)}, bf16[256,1024]{1,0:T(8,128)(2,1)S(1)}, u32[]{:S(2)}, u32[]{:S(2)}) collective-permute-start(bf16[256,1024]{1,0:T(8,128)(2,1)S(1)} %bitcast.60), channel_id=1, source_target_pairs={{0,3},{1,0},{2,1},{3,2},{4,7},{5,4},{6,5},{7,6},{8,11},{9,8},{10,9... | collective-permute-start | bytes 1572872 | tf_op jit(solution)/shard_map/ppermute | solution.py:471
  323.4 19.5 %collective-permute-start.33 = (bf16[256,1280]{1,0:T(8,128)(2,1)S(1)}, bf16[256,1280]{1,0:T(8,128)(2,1)S(1)}, u32[]{:S(2)}, u32[]{:S(2)}) collective-permute-start(bf16[256,1280]{1,0:T(8,128)(2,1)S(1)} %shard_map.110.refs_0_), channel_id=1, source_target_pairs={{0,1},{1,2},{2,3},{3,0},{4,5},{5,6},{6,7},{7,4},{8,9},{9,10},{10,1... | collective-permute-start | bytes 1966088 | tf_op jit(solution)/shard_map/ppermute | solution.py:471
  323.6 27.9 %collective-permute-start.35 = (bf16[256,1280]{1,0:T(8,128)(2,1)S(1)}, bf16[256,1280]{1,0:T(8,128)(2,1)S(1)}, u32[]{:S(2)}, u32[]{:S(2)}) collective-permute-start(bf16[256,1280]{1,0:T(8,128)(2,1)S(1)} %shard_map.110.refs_0_), channel_id=1, source_target_pairs={{0,3},{1,0},{2,1},{3,2},{4,7},{5,4},{6,5},{7,6},{8,11},{9,8},{10,9... | collective-permute-start | bytes 1966088 | tf_op jit(solution)/shard_map/ppermute | solution.py:471
  351.6 16.7 %collective-permute-start.36 = (bf16[256,1280]{1,0:T(8,128)(2,1)S(1)}, bf16[256,1280]{1,0:T(8,128)(2,1)S(1)}, u32[]{:S(2)}, u32[]{:S(2)}) collective-permute-start(bf16[256,1280]{1,0:T(8,128)(2,1)S(1)} %collective-permute-done.35.refs_3_), channel_id=1, source_target_pairs={{1,0},{2,1},{5,4},{6,5},{9,8},{10,9},{13,12},{14,13},{17,16},{18,1... | collective-permute-start | bytes 1966088 | tf_op jit(solution)/shard_map/ppermute | solution.py:481
  (33 other events, 371.2 us)
Sparse Core Ops, SparseCore 0:
  76.5 76.3 all-gather.4
  155.7 84.5 all-gather.6
  242.2 63.2 all-gather.8

commit v5 on v3

--- a/solution.py
+++ b/solution.py
@@ -584,6 +584,7 @@
         ahead = [array for _, _, array in body[1:3]]
         across = [array for _, _, array in tail[1:3]]
         body = spread_second(body)
+        turned += [array for _, _, array in body[3:5]]
         tail = spread_second(tail)
         gathers = [[listed([head, body], [[0], [1, 2]]), listed([tail], [[0]])]]
         later_one = shifted(after(outgoing(1, 1), two), 1)

time: 383 us -> 380 us (level)
  starting transfers between devices: 46.2 us -> 50.6 us
    ppermute x15, waiting for transfers between devices: 41.6 us -> 28.1 us  [swapped(): return lax.ppermute(block, 'rep', [(i, i ^ mask) for i in range(replicas)])]
    ppermute x14, waiting for transfers between devices: 109 us -> 120 us  [shifted(): lax.ppermute(block, 'tp', [(i, (i + shift) % parts) for i in range(parts)])]
    ppermute x14, starting transfers between devices: 23.1 us -> 27.7 us  [shifted(): lax.ppermute(block, 'tp', [(i, (i + shift) % parts) for i in range(parts)])]
    unnamed x48 -> x38, local copies, waits for them, and re-layouts: 9.59 us -> 6.83 us
  transfers between devices with their start and end apart: 40 -> 40, of which waited for: 21 -> 22; matrix products, arithmetic and copies ran while one was open for 6% -> 6% of each run, Pallas kernels for 18% -> 18%
where the time goes in v5:
time: 380 us; the launch traced here: 378 us
  waiting for transfers between devices  204 us (54%)
  Pallas kernels  76.5 us (20%)
  starting transfers between devices  50.6 us (13%)
  local copies, waits for them, and re-layouts  24.9 us (7%)
  between operations  13.6 us (4%)
  other arithmetic  8.4 us (2%)
    ppermute x14, waiting for transfers between devices, shifted(): lax.ppermute(block, 'tp', [(i, (i + shift) % parts) for i in range(parts)])  120 us
    ppermute x4, waiting for transfers between devices, all_parts(): leftwards = lax.ppermute(from_right, 'tp', [(1, 0), (2, 1)])  55.6 us
    ppermute x15, waiting for transfers between devices, swapped(): return lax.ppermute(block, 'rep', [(i, i ^ mask) for i in range(replicas)])  28.1 us
    ppermute x14, starting transfers between devices, shifted(): lax.ppermute(block, 'tp', [(i, (i + shift) % parts) for i in range(parts)])  27.7 us
    pallas_call x3, Pallas kernels, project_qkv(): pl.pallas_call(functools.partial(qkv_kernel, count, shifts, pieces, len(w...  27.5 us
    pallas_call x2, Pallas kernels, attend(): pl.pallas_call(functools.partial(attention_kernel, heads), out_shape=jax....  25.5 us
    ppermute x15, starting transfers between devices, swapped(): return lax.ppermute(block, 'rep', [(i, i ^ mask) for i in range(replicas)])  13.9 us
    pallas_call x2, Pallas kernels, project_out(): pl.pallas_call(functools.partial(out_kernel, count, shifts), out_shape=ja...  9.12 us
  transfers between devices with their start and end apart: 40, of which 22 were waited for; matrix products, arithmetic and copies ran while one was open for 6% of the time, Pallas kernels for 18%

profile of v5, /device:TPU:0, one launch (start us, length us, event | category | flops | bytes accessed | tf_op | source)
XLA Modules:
  0.0 378.4 jit_solution(1831307077782747154)
XLA Ops:
  6.5 4.0 %dynamic-slice_bitcast_fusion = (bf16[160,1536]{1,0:T(8,128)(2,1)}, bf16[160,1536]{1,0:T(8,128)(2,1)}, bf16[160,1536]{1,0:T(8,128)(2,1)}, bf16[160,1536]{1,0:T(8...) fusion(bf16[2,160,6144]{2,1,0:T(8,128)(2,1)} %param.11, ...), kind=kLoop, calls=%fused_computation.14 | loop fusion | bytes 7864336 | tf_op jit(solution)/shard_map/squeeze | solution.py:486
  10.5 2.9 collective-permute-start.5
  23.5 10.2 %collective-permute-done.2 = bf16[160,1536]{1,0:T(8,128)(2,1)} collective-permute-done((bf16[160,1536]{1,0:T(8,128)(2,1)}, bf16[160,1536]{1,0:T(8,128)(2,1)}, u32[]{:S(2)}, u32[]{:S(2)}) %collective-permute-start.2) | collective-permute-done | bytes 491552 | tf_op jit(solution)/shard_map/ppermute | solution.py:471
  33.8 9.6 %collective-permute-done.3 = bf16[160,1536]{1,0:T(8,128)(2,1)} collective-permute-done((bf16[160,1536]{1,0:T(8,128)(2,1)}, bf16[160,1536]{1,0:T(8,128)(2,1)}, u32[]{:S(2)}, u32[]{:S(2)}) %collective-permute-start.3) | collective-permute-done | bytes 491552 | tf_op jit(solution)/shard_map/ppermute | solution.py:471
  57.5 13.1 %collective-permute-done.7.refs_11_ = bf16[320,1536]{1,0:T(8,128)(2,1)} collective-permute-done((bf16[320,1536]{1,0:T(8,128)(2,1)}, bf16[320,1536]{1,0:T(8,128)(2,1)}, u32[]{:S(2)}, u32[]{:S(2)}) %collective-permute-start.7) | collective-permute-done | bytes 983072 | tf_op jit(solution)/shard_map/ppermute | solution.py:498
  87.5 7.8 %collective-permute-done.11.refs_4_ = bf16[160,1536]{1,0:T(8,128)(2,1)S(1)} collective-permute-done((bf16[160,1536]{1,0:T(8,128)(2,1)}, bf16[160,1536]{1,0:T(8,128)(2,1)S(1)}, u32[]{:S(2)}, u32[]{:S(2)}) %collective-permute-start.11) | collective-permute-done | bytes 491552 | tf_op jit(solution)/shard_map/ppermute | solution.py:498
  103.3 9.8 %shard_map.102 = (f32[256,1536]{1,0:T(8,128)}, f32[256,1536]{1,0:T(8,128)}) custom-call(s32[13]{0:T(128)S(1)} %stack.40.rows_ref, bf16[512,640]{1,0:T(8,128)(2,1)} %get-tuple-element.61.refs_0_, bf16[512,640]{1,0:T(8,128)(2,1)} %get-tuple-element.60.refs_1_, bf16[512,640]{1,0:T(8,128)(2,1)} %get-tuple-element.59.refs_2_, ...), custom_call_target="tpu_custom_call" | custom-call | flops 3019898880 | bytes 5898240 | tf_op jit(solution)/shard_map/pallas_call | solution.py:187
  113.0 6.6 %collective-permute-done.18 = bf16[160,1536]{1,0:T(8,128)(2,1)S(1)} collective-permute-done((bf16[160,1536]{1,0:T(8,128)(2,1)}, bf16[160,1536]{1,0:T(8,128)(2,1)S(1)}, u32[]{:S(2)}, u32[]{:S(2)}) %collective-permute-start.18) | collective-permute-done | bytes 491552 | tf_op jit(solution)/shard_map/ppermute | solution.py:471
  119.7 7.4 %shard_map.103 = (f32[256,1536]{1,0:T(8,128)}, f32[256,1536]{1,0:T(8,128)}) custom-call(s32[5]{0:T(128)S(1)} %stack.19.rows_ref, bf16[512,640]{1,0:T(8,128)(2,1)} %get-tuple-element.62.refs_0_, f32[4,1,640]{2,1,0:T(1,128)S(1)} %reshape.165.refs_3_.refs_1_, f32[512,1]{1,0:T(8,128)S(1)} %rsqrt.3.refs_4_.refs_2_, ...), custom_call_target="tpu_custom_call" | custom-call | flops 1006632960 | bytes 1966080 | tf_op jit(solution)/shard_map/pallas_call | solution.py:187
  127.2 3.6 collective-permute-start.28
  134.5 12.7 %shard_map.104 = bf16[4,64,1024]{2,1,0:T(8,128)(2,1)S(1)} custom-call(s32[64]{0:T(128)S(1)} %copy-done.7, f32[4,64,1536]{2,1,0:T(8,128)S(1)} %bitcast.65, f32[4,64,1536]{2,1,0:T(8,128)S(1)} %bitcast.66, f32[4,64,128]{2,1,0:T(8,128)S(1)} %get-tuple-element.72.refs_2_.refs_1_, f32[4,64,128]{2,1,0:T(8,128)S(1)} %get-tuple-element.73.refs_3_.refs_2_, ...), custom_call_target="tpu_custom_call" | custom-call | flops 268435456 | bytes 16777216 | tf_op jit(solution)/shard_map/pallas_call | solution.py:413
  147.2 2.5 pad_maximum_fusion.1
  151.2 3.0 collective-permute-start.21
  157.2 10.0 %collective-permute-done.20.refs_1_ = bf16[256,1024]{1,0:T(8,128)(2,1)} collective-permute-done((bf16[256,1024]{1,0:T(8,128)(2,1)S(1)}, bf16[256,1024]{1,0:T(8,128)(2,1)}, u32[]{:S(2)}, u32[]{:S(2)}) %collective-permute-start.20) | collective-permute-done | bytes 524320 | tf_op jit(solution)/shard_map/ppermute | solution.py:471
  167.2 9.2 %collective-permute-done.21.refs_2_ = bf16[256,1024]{1,0:T(8,128)(2,1)} collective-permute-done((bf16[256,1024]{1,0:T(8,128)(2,1)S(1)}, bf16[256,1024]{1,0:T(8,128)(2,1)}, u32[]{:S(2)}, u32[]{:S(2)}) %collective-permute-start.21) | collective-permute-done | bytes 524320 | tf_op jit(solution)/shard_map/ppermute | solution.py:471
  179.6 5.9 %shard_map.105.refs_2_ = f32[256,1280]{1,0:T(8,128)S(1)} custom-call(s32[4]{0:T(128)S(1)} %broadcast_multiply_fusion.column_ref, bf16[256,1024]{1,0:T(8,128)(2,1)S(1)} %bitcast.64, bf16[256,1024]{1,0:T(8,128)(2,1)} %collective-permute-done.20.refs_1_, bf16[256,1024]{1,0:T(8,128)(2,1)} %collective-permute-done.21.refs_2_, ...), custom_call_target="tpu_custom_call" | custom-call | flops 2013265920 | bytes 7864320 | tf_op jit(solution)/shard_map/pallas_call | solution.py:311
  185.5 8.3 %collective-permute-done.23 = bf16[256,1024]{1,0:T(8,128)(2,1)S(1)} collective-permute-done((bf16[256,1024]{1,0:T(8,128)(2,1)}, bf16[256,1024]{1,0:T(8,128)(2,1)S(1)}, u32[]{:S(2)}, u32[]{:S(2)}) %collective-permute-start.23) | collective-permute-done | bytes 524320 | tf_op jit(solution)/shard_map/ppermute | solution.py:481
  193.9 3.2 shard_map.107.refs_0_.refs_5_
  201.0 15.6 %collective-permute-done.24.refs_1_ = bf16[256,1280]{1,0:T(8,128)(2,1)S(1)} collective-permute-done((bf16[256,1280]{1,0:T(8,128)(2,1)S(1)}, bf16[256,1280]{1,0:T(8,128)(2,1)S(1)}, u32[]{:S(2)}, u32[]{:S(2)}) %collective-permute-start.24) | collective-permute-done | bytes 655392 | tf_op jit(solution)/shard_map/ppermute | solution.py:471
  218.2 9.3 %collective-permute-done.26.refs_3_ = bf16[256,1280]{1,0:T(8,128)(2,1)S(1)} collective-permute-done((bf16[256,1280]{1,0:T(8,128)(2,1)S(1)}, bf16[256,1280]{1,0:T(8,128)(2,1)S(1)}, u32[]{:S(2)}, u32[]{:S(2)}) %collective-permute-start.26) | collective-permute-done | bytes 655392 | tf_op jit(solution)/shard_map/ppermute | solution.py:471
  228.9 16.6 %collective-permute-done.27 = bf16[256,1280]{1,0:T(8,128)(2,1)} collective-permute-done((bf16[256,1280]{1,0:T(8,128)(2,1)S(1)}, bf16[256,1280]{1,0:T(8,128)(2,1)}, u32[]{:S(2)}, u32[]{:S(2)}) %collective-permute-start.27) | collective-permute-done | bytes 655392 | tf_op jit(solution)/shard_map/ppermute | solution.py:481
  246.7 10.3 %shard_map.108 = f32[256,1536]{1,0:T(8,128)S(1)} custom-call(s32[32]{0:T(128)S(1)} %copy-done.8, bf16[256,1280]{1,0:T(8,128)(2,1)S(1)} %shard_map.107.refs_0_.refs_5_, bf16[256,1280]{1,0:T(8,128)(2,1)S(1)} %collective-permute-done.24.refs_1_, bf16[256,1280]{1,0:T(8,128)(2,1)S(1)} %broadcast_select_fusion.1.refs_2_, ...), custom_call_target="tpu_custom_call" | custom-call | flops 4026531840 | bytes 15728640 | tf_op jit(solution)/shard_map/pallas_call | solution.py:187
  257.0 12.8 %shard_map.109 = bf16[4,64,1024]{2,1,0:T(8,128)(2,1)S(1)} custom-call(s32[64]{0:T(128)S(1)} %copy-done.7, f32[4,64,1536]{2,1,0:T(8,128)S(1)} %bitcast.58, f32[4,64,128]{2,1,0:T(8,128)S(1)} %get-tuple-element.72.refs_2_.refs_1_, f32[4,64,128]{2,1,0:T(8,128)S(1)} %get-tuple-element.73.refs_3_.refs_2_, f32[1,128]{1,0:T(1,128)S(1)} %get-tuple-element.75.refs_3_, ...), custom_call_target="tpu_custom_call" | custom-call | flops 268435456 | bytes 16777216 | tf_op jit(solution)/shard_map/pallas_call | solution.py:413
  271.1 2.6 collective-permute-start.31
  273.7 12.8 %collective-permute-done.29.refs_1_ = bf16[256,1024]{1,0:T(8,128)(2,1)S(1)} collective-permute-done((bf16[256,1024]{1,0:T(8,128)(2,1)S(1)}, bf16[256,1024]{1,0:T(8,128)(2,1)S(1)}, u32[]{:S(2)}, u32[]{:S(2)}) %collective-permute-start.29) | collective-permute-done | bytes 524320 | tf_op jit(solution)/shard_map/ppermute | solution.py:471
  287.2 9.0 %collective-permute-done.31.refs_3_ = bf16[256,1024]{1,0:T(8,128)(2,1)S(1)} collective-permute-done((bf16[256,1024]{1,0:T(8,128)(2,1)S(1)}, bf16[256,1024]{1,0:T(8,128)(2,1)S(1)}, u32[]{:S(2)}, u32[]{:S(2)}) %collective-permute-start.31) | collective-permute-done | bytes 524320 | tf_op jit(solution)/shard_map/ppermute | solution.py:471
  297.5 14.0 %collective-permute-done.32 = bf16[256,1024]{1,0:T(8,128)(2,1)S(1)} collective-permute-done((bf16[256,1024]{1,0:T(8,128)(2,1)S(1)}, bf16[256,1024]{1,0:T(8,128)(2,1)S(1)}, u32[]{:S(2)}, u32[]{:S(2)}) %collective-permute-start.32) | collective-permute-done | bytes 524320 | tf_op jit(solution)/shard_map/ppermute | solution.py:481
  311.6 6.2 %shard_map.110.refs_0_ = bf16[256,1280]{1,0:T(8,128)(2,1)S(1)} custom-call(s32[4]{0:T(128)S(1)} %broadcast_multiply_fusion.column_ref, bf16[256,1024]{1,0:T(8,128)(2,1)S(1)} %bitcast.61, bf16[256,1024]{1,0:T(8,128)(2,1)S(1)} %collective-permute-done.29.refs_1_, bf16[256,1024]{1,0:T(8,128)(2,1)S(1)} %broadcast_select_fusion.2.refs_2_, ...), custom_call_target="tpu_custom_call" | custom-call | flops 2684354560 | bytes 10485760 | tf_op jit(solution)/shard_map/pallas_call | solution.py:245
  321.8 15.6 %collective-permute-done.33.refs_1_ = bf16[256,1280]{1,0:T(8,128)(2,1)S(1)} collective-permute-done((bf16[256,1280]{1,0:T(8,128)(2,1)S(1)}, bf16[256,1280]{1,0:T(8,128)(2,1)S(1)}, u32[]{:S(2)}, u32[]{:S(2)}) %collective-permute-start.33) | collective-permute-done | bytes 655392 | tf_op jit(solution)/shard_map/ppermute | solution.py:471
  338.0 12.0 %collective-permute-done.35.refs_3_ = bf16[256,1280]{1,0:T(8,128)(2,1)S(1)} collective-permute-done((bf16[256,1280]{1,0:T(8,128)(2,1)S(1)}, bf16[256,1280]{1,0:T(8,128)(2,1)S(1)}, u32[]{:S(2)}, u32[]{:S(2)}) %collective-permute-start.35) | collective-permute-done | bytes 655392 | tf_op jit(solution)/shard_map/ppermute | solution.py:471
  351.4 16.7 %collective-permute-done.36 = bf16[256,1280]{1,0:T(8,128)(2,1)S(1)} collective-permute-done((bf16[256,1280]{1,0:T(8,128)(2,1)S(1)}, bf16[256,1280]{1,0:T(8,128)(2,1)S(1)}, u32[]{:S(2)}, u32[]{:S(2)}) %collective-permute-start.36) | collective-permute-done | bytes 655392 | tf_op jit(solution)/shard_map/ppermute | solution.py:481
  368.1 3.8 shard_map.111
  (144 shorter events, 77.7 us)
Async XLA Ops:
  6.5 169.8 %all-gather.5.cloned.1.call-start = ((), (), s32[]{:S(2)}) async-start(), calls=%async_computation | async-start | bytes 11796480 | tf_op jit(solution)/shard_map/all_gather | solution.py:599
  10.5 35.1 %collective-permute-start.5 = (bf16[160,1536]{1,0:T(8,128)(2,1)S(1)}, bf16[160,1536]{1,0:T(8,128)(2,1)}, u32[]{:S(2)}, u32[]{:S(2)}) collective-permute-start(bf16[160,1536]{1,0:T(8,128)(2,1)S(1)} %get-tuple-element.52.refs_5_), channel_id=1, source_target_pairs={{0,8},{4,12},{8,0},{12,4},{16,24},{20,28},{24,16},{28,20},{1,9},{5... | collective-permute-start | bytes 1474568 | tf_op jit(solution)/shard_map/ppermute | solution.py:498
  13.4 32.1 %collective-permute-start.6 = (bf16[160,1536]{1,0:T(8,128)(2,1)S(1)}, bf16[160,1536]{1,0:T(8,128)(2,1)}, u32[]{:S(2)}, u32[]{:S(2)}) collective-permute-start(bf16[160,1536]{1,0:T(8,128)(2,1)S(1)} %get-tuple-element.52.refs_5_), channel_id=1, source_target_pairs={{0,16},{4,20},{8,24},{12,28},{16,0},{20,4},{24,8},{28,12},{1,17},{... | collective-permute-start | bytes 1474568 | tf_op jit(solution)/shard_map/ppermute | solution.py:498
  17.6 29.6 %collective-permute-start = (bf16[256,2560]{1,0:T(8,128)(2,1)}, bf16[256,2560]{1,0:T(8,128)(2,1)}, u32[]{:S(2)}, u32[]{:S(2)}) collective-permute-start(bf16[256,2560]{1,0:T(8,128)(2,1)} %get-tuple-element.28), channel_id=1, source_target_pairs={{0,4},{4,0},{8,12},{12,8},{16,20},{20,16},{24,28},{28,24},{1,5},{5... | collective-permute-start | bytes 3932168 | tf_op jit(solution)/shard_map/ppermute | solution.py:498
  17.6 16.2 %collective-permute-start.2 = (bf16[160,1536]{1,0:T(8,128)(2,1)}, bf16[160,1536]{1,0:T(8,128)(2,1)}, u32[]{:S(2)}, u32[]{:S(2)}) collective-permute-start(bf16[160,1536]{1,0:T(8,128)(2,1)} %get-tuple-element.54), channel_id=1, source_target_pairs={{0,1},{1,2},{2,3},{3,0},{4,5},{5,6},{6,7},{7,4},{8,9},{9,10},{10,1... | collective-permute-start | bytes 1474568 | tf_op jit(solution)/shard_map/ppermute | solution.py:471
  19.2 24.2 %collective-permute-start.3 = (bf16[160,1536]{1,0:T(8,128)(2,1)}, bf16[160,1536]{1,0:T(8,128)(2,1)}, u32[]{:S(2)}, u32[]{:S(2)}) collective-permute-start(bf16[160,1536]{1,0:T(8,128)(2,1)} %get-tuple-element.53), channel_id=1, source_target_pairs={{0,3},{1,0},{2,1},{3,2},{4,7},{5,4},{6,5},{7,6},{8,11},{9,8},{10,9... | collective-permute-start | bytes 1474568 | tf_op jit(solution)/shard_map/ppermute | solution.py:471
  33.8 19.7 %collective-permute-start.1 = (f32[2,128]{1,0:T(2,128)S(1)}, f32[2,128]{1,0:T(2,128)S(1)}, u32[]{:S(2)}, u32[]{:S(2)}) collective-permute-start(f32[2,128]{1,0:T(2,128)S(1)} %bitcast.68), channel_id=1, source_target_pairs={{0,4},{4,0},{8,12},{12,8},{16,20},{20,16},{24,28},{28,24},{1,5},{5... | collective-permute-start | bytes 3080 | tf_op jit(solution)/shard_map/ppermute | solution.py:498
  45.6 25.0 %collective-permute-start.7 = (bf16[320,1536]{1,0:T(8,128)(2,1)}, bf16[320,1536]{1,0:T(8,128)(2,1)}, u32[]{:S(2)}, u32[]{:S(2)}) collective-permute-start(bf16[320,1536]{1,0:T(8,128)(2,1)} %pad_maximum_fusion.2.refs_10_), channel_id=1, source_target_pairs={{0,8},{4,12},{8,0},{12,4},{16,24},{20,28},{24,16},{28,20},{1,9},{5... | collective-permute-start | bytes 2949128 | tf_op jit(solution)/shard_map/ppermute | solution.py:498
  46.1 26.1 %collective-permute-start.8 = (bf16[320,1536]{1,0:T(8,128)(2,1)}, bf16[320,1536]{1,0:T(8,128)(2,1)}, u32[]{:S(2)}, u32[]{:S(2)}) collective-permute-start(bf16[320,1536]{1,0:T(8,128)(2,1)} %pad_maximum_fusion.2.refs_10_), channel_id=1, source_target_pairs={{0,16},{4,20},{8,24},{12,28},{16,0},{20,4},{24,8},{28,12},{1,17},{... | collective-permute-start | bytes 2949128 | tf_op jit(solution)/shard_map/ppermute | solution.py:498
  47.2 29.8 %collective-permute-start.4 = (bf16[160,1536]{1,0:T(8,128)(2,1)}, bf16[160,1536]{1,0:T(8,128)(2,1)}, u32[]{:S(2)}, u32[]{:S(2)}) collective-permute-start(bf16[160,1536]{1,0:T(8,128)(2,1)} %get-tuple-element.30), channel_id=1, source_target_pairs={{0,2},{1,3},{2,0},{3,1},{4,6},{5,7},{6,4},{7,5},{8,10},{9,11},{10,... | collective-permute-start | bytes 1474568 | tf_op jit(solution)/shard_map/ppermute | solution.py:471
  50.3 26.0 %collective-permute-start.9 = (bf16[80,1536]{1,0:T(8,128)(2,1)}, bf16[80,1536]{1,0:T(8,128)(2,1)S(1)}, u32[]{:S(2)}, u32[]{:S(2)}) collective-permute-start(bf16[80,1536]{1,0:T(8,128)(2,1)} %slice.82), channel_id=1, source_target_pairs={{0,16},{4,20},{8,24},{12,28},{16,0},{20,4},{24,8},{28,12},{1,17},{... | collective-permute-start | bytes 737288 | tf_op jit(solution)/shard_map/ppermute | solution.py:498
  53.5 23.5 %collective-permute-start.10 = (bf16[80,1536]{1,0:T(8,128)(2,1)}, bf16[80,1536]{1,0:T(8,128)(2,1)}, u32[]{:S(2)}, u32[]{:S(2)}) collective-permute-start(bf16[80,1536]{1,0:T(8,128)(2,1)} %slice.83), channel_id=1, source_target_pairs={{0,8},{4,12},{8,0},{12,4},{16,24},{20,28},{24,16},{28,20},{1,9},{5... | collective-permute-start | bytes 737288 | tf_op jit(solution)/shard_map/ppermute | solution.py:498
  77.0 18.3 %collective-permute-start.11 = (bf16[160,1536]{1,0:T(8,128)(2,1)}, bf16[160,1536]{1,0:T(8,128)(2,1)S(1)}, u32[]{:S(2)}, u32[]{:S(2)}) collective-permute-start(bf16[160,1536]{1,0:T(8,128)(2,1)} %collective-permute-done.4.refs_3_), channel_id=1, source_target_pairs={{0,8},{4,12},{8,0},{12,4},{16,24},{20,28},{24,16},{28,20},{1,9},{5... | collective-permute-start | bytes 1474568 | tf_op jit(solution)/shard_map/ppermute | solution.py:498
  78.5 17.2 %collective-permute-start.12 = (bf16[160,1536]{1,0:T(8,128)(2,1)}, bf16[160,1536]{1,0:T(8,128)(2,1)}, u32[]{:S(2)}, u32[]{:S(2)}) collective-permute-start(bf16[160,1536]{1,0:T(8,128)(2,1)} %collective-permute-done.4.refs_3_), channel_id=1, source_target_pairs={{0,16},{4,20},{8,24},{12,28},{16,0},{20,4},{24,8},{28,12},{1,17},{... | collective-permute-start | bytes 1474568 | tf_op jit(solution)/shard_map/ppermute | solution.py:498
  79.0 16.7 %collective-permute-start.17 = (bf16[160,1536]{1,0:T(8,128)(2,1)}, bf16[160,1536]{1,0:T(8,128)(2,1)}, u32[]{:S(2)}, u32[]{:S(2)}) collective-permute-start(bf16[160,1536]{1,0:T(8,128)(2,1)} %get-tuple-element.35), channel_id=1, source_target_pairs={{0,1},{1,2},{2,3},{3,0},{4,5},{5,6},{6,7},{7,4},{8,9},{9,10},{10,1... | collective-permute-start | bytes 1474568 | tf_op jit(solution)/shard_map/ppermute | solution.py:471
  95.7 151.0 %all-gather.7.cloned.1.call-start = ((), (), s32[]{:S(2)}) async-start(), calls=%async_computation.1 | async-start | bytes 17694720 | tf_op jit(solution)/shard_map/all_gather | solution.py:547
  95.7 23.9 %collective-permute-start.18 = (bf16[160,1536]{1,0:T(8,128)(2,1)}, bf16[160,1536]{1,0:T(8,128)(2,1)S(1)}, u32[]{:S(2)}, u32[]{:S(2)}) collective-permute-start(bf16[160,1536]{1,0:T(8,128)(2,1)} %get-tuple-element.36), channel_id=1, source_target_pairs={{0,2},{1,3},{2,0},{3,1},{4,6},{5,7},{6,4},{7,5},{8,10},{9,11},{10,... | collective-permute-start | bytes 1474568 | tf_op jit(solution)/shard_map/ppermute | solution.py:471
  98.1 21.5 %collective-permute-start.13 = (bf16[80,1536]{1,0:T(8,128)(2,1)S(1)}, bf16[80,1536]{1,0:T(8,128)(2,1)S(1)}, u32[]{:S(2)}, u32[]{:S(2)}) collective-permute-start(bf16[80,1536]{1,0:T(8,128)(2,1)S(1)} %slice.84), channel_id=1, source_target_pairs={{0,16},{4,20},{8,24},{12,28},{16,0},{20,4},{24,8},{28,12},{1,17},{... | collective-permute-start | bytes 737288 | tf_op jit(solution)/shard_map/ppermute | solution.py:498
  100.0 19.7 %collective-permute-start.14 = (bf16[80,1536]{1,0:T(8,128)(2,1)S(1)}, bf16[80,1536]{1,0:T(8,128)(2,1)S(1)}, u32[]{:S(2)}, u32[]{:S(2)}) collective-permute-start(bf16[80,1536]{1,0:T(8,128)(2,1)S(1)} %slice.85), channel_id=1, source_target_pairs={{0,8},{4,12},{8,0},{12,4},{16,24},{20,28},{24,16},{28,20},{1,9},{5... | collective-permute-start | bytes 737288 | tf_op jit(solution)/shard_map/ppermute | solution.py:498
  127.2 19.9 %collective-permute-start.28 = (bf16[160,1536]{1,0:T(8,128)(2,1)S(1)}, bf16[160,1536]{1,0:T(8,128)(2,1)S(1)}, u32[]{:S(2)}, u32[]{:S(2)}) collective-permute-start(bf16[160,1536]{1,0:T(8,128)(2,1)S(1)} %copy-done.13), channel_id=1, source_target_pairs={{0,3},{1,0},{2,1},{3,2},{4,7},{5,4},{6,5},{7,6},{8,11},{9,8},{10,9... | collective-permute-start | bytes 1474568 | tf_op jit(solution)/shard_map/ppermute | solution.py:471
  149.6 162.0 %all-gather.9.cloned.1.call-start = ((), (), s32[]{:S(2)}) async-start(), calls=%async_computation.2 | async-start | bytes 11796480 | tf_op jit(solution)/shard_map/all_gather | solution.py:599
  150.4 16.8 %collective-permute-start.20 = (bf16[256,1024]{1,0:T(8,128)(2,1)S(1)}, bf16[256,1024]{1,0:T(8,128)(2,1)}, u32[]{:S(2)}, u32[]{:S(2)}) collective-permute-start(bf16[256,1024]{1,0:T(8,128)(2,1)S(1)} %bitcast.62), channel_id=1, source_target_pairs={{0,1},{1,2},{2,3},{3,0},{4,5},{5,6},{6,7},{7,4},{8,9},{9,10},{10,1... | collective-permute-start | bytes 1572872 | tf_op jit(solution)/shard_map/ppermute | solution.py:471
  151.2 25.1 %collective-permute-start.21 = (bf16[256,1024]{1,0:T(8,128)(2,1)S(1)}, bf16[256,1024]{1,0:T(8,128)(2,1)}, u32[]{:S(2)}, u32[]{:S(2)}) collective-permute-start(bf16[256,1024]{1,0:T(8,128)(2,1)S(1)} %bitcast.63), channel_id=1, source_target_pairs={{0,3},{1,0},{2,1},{3,2},{4,7},{5,4},{6,5},{7,6},{8,11},{9,8},{10,9... | collective-permute-start | bytes 1572872 | tf_op jit(solution)/shard_map/ppermute | solution.py:471
  177.0 16.8 %collective-permute-start.23 = (bf16[256,1024]{1,0:T(8,128)(2,1)}, bf16[256,1024]{1,0:T(8,128)(2,1)S(1)}, u32[]{:S(2)}, u32[]{:S(2)}) collective-permute-start(bf16[256,1024]{1,0:T(8,128)(2,1)} %collective-permute-done.21.refs_2_), channel_id=1, source_target_pairs={{1,0},{2,1},{5,4},{6,5},{9,8},{10,9},{13,12},{14,13},{17,16},{18,1... | collective-permute-start | bytes 1572872 | tf_op jit(solution)/shard_map/ppermute | solution.py:481
  197.1 19.5 %collective-permute-start.24 = (bf16[256,1280]{1,0:T(8,128)(2,1)S(1)}, bf16[256,1280]{1,0:T(8,128)(2,1)S(1)}, u32[]{:S(2)}, u32[]{:S(2)}) collective-permute-start(bf16[256,1280]{1,0:T(8,128)(2,1)S(1)} %shard_map.107.refs_0_.refs_5_), channel_id=1, source_target_pairs={{0,1},{1,2},{2,3},{3,0},{4,5},{5,6},{6,7},{7,4},{8,9},{9,10},{10,1... | collective-permute-start | bytes 1966088 | tf_op jit(solution)/shard_map/ppermute | solution.py:471
  198.9 28.6 %collective-permute-start.26 = (bf16[256,1280]{1,0:T(8,128)(2,1)S(1)}, bf16[256,1280]{1,0:T(8,128)(2,1)S(1)}, u32[]{:S(2)}, u32[]{:S(2)}) collective-permute-start(bf16[256,1280]{1,0:T(8,128)(2,1)S(1)} %shard_map.107.refs_0_.refs_5_), channel_id=1, source_target_pairs={{0,3},{1,0},{2,1},{3,2},{4,7},{5,4},{6,5},{7,6},{8,11},{9,8},{10,9... | collective-permute-start | bytes 1966088 | tf_op jit(solution)/shard_map/ppermute | solution.py:471
  227.5 18.0 %collective-permute-start.27 = (bf16[256,1280]{1,0:T(8,128)(2,1)S(1)}, bf16[256,1280]{1,0:T(8,128)(2,1)}, u32[]{:S(2)}, u32[]{:S(2)}) collective-permute-start(bf16[256,1280]{1,0:T(8,128)(2,1)S(1)} %collective-permute-done.26.refs_3_), channel_id=1, source_target_pairs={{1,0},{2,1},{5,4},{6,5},{9,8},{10,9},{13,12},{14,13},{17,16},{18,1... | collective-permute-start | bytes 1966088 | tf_op jit(solution)/shard_map/ppermute | solution.py:481
  269.8 16.7 %collective-permute-start.29 = (bf16[256,1024]{1,0:T(8,128)(2,1)S(1)}, bf16[256,1024]{1,0:T(8,128)(2,1)S(1)}, u32[]{:S(2)}, u32[]{:S(2)}) collective-permute-start(bf16[256,1024]{1,0:T(8,128)(2,1)S(1)} %bitcast.59), channel_id=1, source_target_pairs={{0,1},{1,2},{2,3},{3,0},{4,5},{5,6},{6,7},{7,4},{8,9},{9,10},{10,1... | collective-permute-start | bytes 1572872 | tf_op jit(solution)/shard_map/ppermute | solution.py:471
  271.1 25.1 %collective-permute-start.31 = (bf16[256,1024]{1,0:T(8,128)(2,1)S(1)}, bf16[256,1024]{1,0:T(8,128)(2,1)S(1)}, u32[]{:S(2)}, u32[]{:S(2)}) collective-permute-start(bf16[256,1024]{1,0:T(8,128)(2,1)S(1)} %bitcast.60), channel_id=1, source_target_pairs={{0,3},{1,0},{2,1},{3,2},{4,7},{5,4},{6,5},{7,6},{8,11},{9,8},{10,9... | collective-permute-start | bytes 1572872 | tf_op jit(solution)/shard_map/ppermute | solution.py:471
  317.9 19.5 %collective-permute-start.33 = (bf16[256,1280]{1,0:T(8,128)(2,1)S(1)}, bf16[256,1280]{1,0:T(8,128)(2,1)S(1)}, u32[]{:S(2)}, u32[]{:S(2)}) collective-permute-start(bf16[256,1280]{1,0:T(8,128)(2,1)S(1)} %shard_map.110.refs_0_), channel_id=1, source_target_pairs={{0,1},{1,2},{2,3},{3,0},{4,5},{5,6},{6,7},{7,4},{8,9},{9,10},{10,1... | collective-permute-start | bytes 1966088 | tf_op jit(solution)/shard_map/ppermute | solution.py:471
  319.7 30.4 %collective-permute-start.35 = (bf16[256,1280]{1,0:T(8,128)(2,1)S(1)}, bf16[256,1280]{1,0:T(8,128)(2,1)S(1)}, u32[]{:S(2)}, u32[]{:S(2)}) collective-permute-start(bf16[256,1280]{1,0:T(8,128)(2,1)S(1)} %shard_map.110.refs_0_), channel_id=1, source_target_pairs={{0,3},{1,0},{2,1},{3,2},{4,7},{5,4},{6,5},{7,6},{8,11},{9,8},{10,9... | collective-permute-start | bytes 1966088 | tf_op jit(solution)/shard_map/ppermute | solution.py:471
  350.1 18.0 %collective-permute-start.36 = (bf16[256,1280]{1,0:T(8,128)(2,1)S(1)}, bf16[256,1280]{1,0:T(8,128)(2,1)S(1)}, u32[]{:S(2)}, u32[]{:S(2)}) collective-permute-start(bf16[256,1280]{1,0:T(8,128)(2,1)S(1)} %collective-permute-done.35.refs_3_), channel_id=1, source_target_pairs={{1,0},{2,1},{5,4},{6,5},{9,8},{10,9},{13,12},{14,13},{17,16},{18,1... | collective-permute-start | bytes 1966088 | tf_op jit(solution)/shard_map/ppermute | solution.py:481
  (27 other events, 280.3 us)
Sparse Core Ops, SparseCore 0:
  95.8 63.2 all-gather.4
  161.0 85.4 all-gather.6
  248.3 63.2 all-gather.8
